TPU v7x, 32 devices: a whole 2x2x4 slice. The times are simulated.
32 devices in a mesh: gx: 8 (over z, y), gy: 4 (over x, core).
Axes of the slice: x: 2, y: 2, z: 4, core: 2. Of those that a mesh axis runs over, the one named last changes fastest.
Arguments:
- offsets: float32 [3, 16, 8, 1024], P(None, 'gx', 'gy'), as said below
- charges: float32 [16, 8, 1024], P('gx', 'gy'), may hold values from -0.08 to 0.08
Outputs:
- potential: float32 [16, 8, 1024], P('gx', 'gy')
Inputs may be any that keep to these rules, and one draw needn't show every extreme that they name: `offsets`: particle p of a leaf lies in sub-cell (p // 4^2, (p // 4) % 4, p % 4) of the leaf's grid of 4^3 equal sub-cells, inside the middle half of that sub-cell along each dimension.
All inputs are finite; a program needn't handle non-finite values. Where the computation divides by a largest or mean magnitude, that divisor is 1e-20 or more.
Results may differ from a plain program's by a relative error of at most 0.0003.
Values sent between devices are 32-bit elements; how exact they have to be, the bound alone decides.
No kernel may reach another device: no remote copies, remote signals or barrier semaphores. Data moves between devices by JAX's collectives and lax.ppermute only.
A program may use at most 192 MiB of HBM per device.

v0:
```python
import jax
import jax.numpy as jnp
from jax import lax
from jax.sharding import PartitionSpec as P

CX = 2
CY = 2
LZ = 16
PPL = 64


highest = lax.Precision.HIGHEST


def padded_2(block, sides, width):
    for axis, dim in sides:
        count = lax.axis_size(axis)
        forward = [(i, i + 1) for i in range(count - 1)]
        backward = [(target, source) for source, target in forward]
        low = lax.ppermute(
            lax.slice_in_dim(block, block.shape[dim] - width, None, axis=dim), axis, forward
        )
        high = lax.ppermute(lax.slice_in_dim(block, 0, width, axis=dim), axis, backward)
        block = jnp.concatenate([low, block, high], axis=dim)
    return block


def cheb_points():
    return jnp.cos((2.0 * jnp.arange(4, dtype=jnp.float32) + 1.0) * jnp.pi / 8.0)


def interpolate(coords):
    points = cheb_points()
    second = 2.0 * points * points - 1.0
    third = 4.0 * points * points * points - 3.0 * points
    value = coords[..., None]
    return 0.25 + 0.5 * (
        value * points
        + (2.0 * value * value - 1.0) * second
        + (4.0 * value * value * value - 3.0 * value) * third
    )


def node_grid():
    points = cheb_points()
    counter = jnp.arange(64, dtype=jnp.int32)
    return jnp.stack([points[counter // 16], points[counter // 4 % 4], points[counter % 4]], -1)


def child_grid():
    counter = jnp.arange(8, dtype=jnp.int32)
    return jnp.stack([counter // 4, counter // 2 % 2, counter % 2], -1).astype(jnp.float32)


def upward_matrix():
    points = cheb_points()
    halves = jnp.array([0.0, 1.0], dtype=jnp.float32)
    shifted = (points[None, :] + 2.0 * halves[:, None] - 1.0) / 2.0
    factor = interpolate(shifted)
    return jnp.einsum("xia,yjb,zkc->xyzijkabc", factor, factor, factor, precision=highest).reshape(
        512, 64
    )


def translation(offset):
    node_points = node_grid()
    child_corner = child_grid()
    box_offsets = 2.0 * offset[None, None, :] + child_corner[:, None, :] - child_corner[None, :, :]
    spread = (node_points[None, :, :] - node_points[:, None, :]) / 2.0
    separation = spread[None, :, None, :, :] - box_offsets[:, None, :, None, :]
    adjacent = (jnp.max(jnp.abs(box_offsets), -1) <= 1.0).astype(jnp.float32)[:, None, :, None]
    distance = jnp.sqrt(jnp.sum(separation * separation, -1))
    return ((1.0 - adjacent) / (distance + adjacent)).reshape(512, 512)


def offset_of(counter):
    return jnp.stack([counter // 9, counter // 3 % 3, counter % 3]) - 1


def translation_tables():

    def one_table(counter):
        return translation(offset_of(counter).astype(jnp.float32))

    return lax.map(one_table, jnp.arange(27, dtype=jnp.int32))


def to_parent(moments):
    size_x, size_y, size_z, _ = moments.shape
    moments = moments.reshape(size_x // 2, 2, size_y // 2, 2, size_z // 2, 2, 64)
    return moments.transpose(0, 2, 4, 1, 3, 5, 6).reshape(
        size_x // 2, size_y // 2, size_z // 2, 512
    )


def from_parent(moments):
    size_x, size_y, size_z, _ = moments.shape
    moments = moments.reshape(size_x, size_y, size_z, 2, 2, 2, 64)
    return moments.transpose(0, 3, 1, 4, 2, 5, 6).reshape(2 * size_x, 2 * size_y, 2 * size_z, 64)


def matmul(left, right):
    return jnp.dot(left, right, precision=highest, preferred_element_type=jnp.float32)


def coarsen(moments, upward):
    parents = to_parent(moments)
    return matmul(parents.reshape(-1, 512), upward).reshape(parents.shape[:3] + (64,))


def refine(local, upward):
    spread_out = matmul(local.reshape(-1, 64), upward.T).reshape(local.shape[:3] + (512,))
    return from_parent(spread_out)


def pad_one(moments):
    return jnp.pad(moments, ((1, 1), (1, 1), (1, 1), (0, 0)))


def far_translate(padded, scaling, tables):
    size_x, size_y, size_z = (padded.shape[0] - 2, padded.shape[1] - 2, padded.shape[2] - 2)

    def step_fn(running, inputs):
        counter, table = inputs
        offset = offset_of(counter)
        window_piece = lax.dynamic_slice(
            padded,
            (offset[0] + 1, offset[1] + 1, offset[2] + 1, jnp.int32(0)),
            (size_x, size_y, size_z, 512),
        )
        return (running + matmul(window_piece.reshape(-1, 512), table), None)

    running, _ = lax.scan(
        step_fn,
        jnp.zeros((size_x * size_y * size_z, 512), jnp.float32),
        (jnp.arange(27, dtype=jnp.int32), tables),
    )
    return (scaling * running).reshape(size_x, size_y, size_z, 512)


def dense_translate(targets, sources, weights):
    node_points = node_grid()
    spread = (node_points[:, None, :] - node_points[None, :, :]) / 2.0
    box_offsets = sources[None, :, :] - targets[:, None, :]
    separation = spread[None, :, None, :, :] - box_offsets[:, None, :, None, :]
    adjacent = (jnp.max(jnp.abs(box_offsets), -1) <= 1.0).astype(jnp.float32)[:, None, :, None]
    distance = jnp.sqrt(jnp.sum(separation * separation, -1))
    kernel = ((1.0 - adjacent) / (distance + adjacent)).reshape(
        targets.shape[0] * 64, sources.shape[0] * 64
    )
    return (0.125 * matmul(kernel, weights.reshape(-1))).reshape(targets.shape[0], 64)


def particle_basis(offsets):
    coords = 2.0 * offsets - 1.0
    along_x = interpolate(coords[0])
    along_y = interpolate(coords[1])
    along_z = interpolate(coords[2])
    product = (
        along_x[..., :, None, None] * along_y[..., None, :, None] * along_z[..., None, None, :]
    )
    return product.reshape(along_x.shape[:-1] + (64,))


def gather_moments(charges, interp_basis):
    return jnp.einsum(
        "...p,...pm->...m",
        charges,
        interp_basis,
        precision=highest,
        preferred_element_type=jnp.float32,
    )


def evaluate_local(interp_basis, local):
    return jnp.einsum(
        "...pm,...m->...p",
        interp_basis,
        local,
        precision=highest,
        preferred_element_type=jnp.float32,
    )


def near_field(targets, sources, weights):
    size_x, size_y, depth, count = (
        targets.shape[1],
        targets.shape[2],
        targets.shape[3],
        targets.shape[4],
    )
    self_mask = jnp.concatenate(
        [
            jnp.zeros((count, count), jnp.float32),
            jnp.eye(count, dtype=jnp.float32),
            jnp.zeros((count, count), jnp.float32),
        ],
        1,
    )
    running = jnp.zeros((size_x, size_y, depth, count), jnp.float32)
    for step_x in range(3):
        for step_y in range(3):
            window = sources[:, step_x : step_x + size_x, step_y : step_y + size_y]
            stacked = jnp.concatenate(
                [
                    window[..., 0:depth, :],
                    window[..., 1 : depth + 1, :],
                    window[..., 2 : depth + 2, :],
                ],
                -1,
            )
            charge_win = weights[step_x : step_x + size_x, step_y : step_y + size_y]
            charge_win = jnp.concatenate(
                [
                    charge_win[..., 0:depth, :],
                    charge_win[..., 1 : depth + 1, :],
                    charge_win[..., 2 : depth + 2, :],
                ],
                -1,
            )
            squared = jnp.zeros((size_x, size_y, depth, count, 3 * count), jnp.float32)
            for comp in range(3):
                differ = targets[comp][..., :, None] - stacked[comp][..., None, :]
                squared = squared + differ * differ
            if step_x == 1 and step_y == 1:
                inverse = lax.rsqrt(squared + self_mask) * (1.0 - self_mask)
            else:
                inverse = lax.rsqrt(squared)
            running = running + jnp.sum(inverse * charge_win[..., None, :], -1)
    return running


def body(offsets, charges):
    index_x = lax.axis_index("gx")
    index_y = lax.axis_index("gy")
    count_x = lax.axis_size("gx")
    count_y = lax.axis_size("gy")
    upward = upward_matrix()
    tables = translation_tables()
    stacked = jnp.concatenate([offsets, charges[None]], 0)
    own_basis = particle_basis(offsets.reshape(3, CX, CY, LZ, PPL))
    own_charges = charges.reshape(CX, CY, LZ, PPL)
    leaf_moments = gather_moments(own_charges, own_basis)
    rim_flat = padded_2(leaf_moments.reshape(CX, CY, LZ * 64), (("gx", 0), ("gy", 1)), 2)
    rim_moments = rim_flat.reshape(CX + 4, CY + 4, LZ, 64)
    near_block = padded_2(stacked, (("gx", 1), ("gy", 2)), 1).reshape(4, CX + 2, CY + 2, LZ, PPL)
    rim_padded = jnp.pad(rim_moments, ((0, 0), (0, 0), (2, 2), (0, 0)))
    leaf_far = from_parent(far_translate(to_parent(rim_padded), 1.0, tables))
    first_moments = coarsen(leaf_moments, upward)
    first_piece = first_moments.reshape(1, CY // 2, LZ // 2 * 64)
    gathered = lax.all_gather(first_piece, ("gx", "gy"), axis=0, tiled=True)
    first_whole = gathered.reshape(count_x, count_y * (CY // 2), LZ // 2, 64)
    second_whole = coarsen(first_whole, upward)
    first_block = lax.dynamic_slice(
        pad_one(to_parent(first_whole)),
        (index_x // 2, index_y // 2, 0, 0),
        (3, 3, LZ // 4 + 2, 512),
    )
    third_whole = coarsen(second_whole, upward)
    first_far = from_parent(far_translate(first_block, 0.5, tables))
    first_far = lax.dynamic_slice(first_far, (index_x % 2, index_y % 2, 0, 0), (1, 1, LZ // 2, 64))
    second_block = lax.dynamic_slice(
        pad_one(to_parent(second_whole)),
        (index_x // 4, index_y // 4, 0, 0),
        (3, 3, LZ // 8 + 2, 512),
    )
    second_far = from_parent(far_translate(second_block, 0.25, tables))
    second_far = lax.dynamic_slice(
        second_far, (index_x // 2 % 2, index_y // 2 % 2, 0, 0), (1, 1, LZ // 4, 64)
    )
    boxes_x, boxes_y, boxes_z = (count_x * CX // 8, count_y * CY // 8, LZ // 8)
    counter = jnp.arange(boxes_x * boxes_y * boxes_z, dtype=jnp.int32)
    sources = jnp.stack(
        [counter // (boxes_y * boxes_z), counter // boxes_z % boxes_y, counter % boxes_z], -1
    ).astype(jnp.float32)
    targets = jnp.stack(
        [
            jnp.full((boxes_z,), index_x // 4, jnp.int32),
            jnp.full((boxes_z,), index_y // 4, jnp.int32),
            jnp.arange(boxes_z, dtype=jnp.int32),
        ],
        -1,
    ).astype(jnp.float32)
    top_far = dense_translate(targets, sources, third_whole.reshape(-1, 64))
    second_local = refine(top_far.reshape(1, 1, boxes_z, 64), upward)
    second_local = (
        lax.dynamic_slice(
            second_local, (index_x // 2 % 2, index_y // 2 % 2, 0, 0), (1, 1, LZ // 4, 64)
        )
        + second_far
    )
    first_local = refine(second_local, upward)
    first_local = (
        lax.dynamic_slice(first_local, (index_x % 2, index_y % 2, 0, 0), (1, 1, LZ // 2, 64))
        + first_far
    )
    leaf_local = refine(first_local, upward) + leaf_far
    far_potential = evaluate_local(own_basis, leaf_local)
    padded = jnp.pad(near_block, ((0, 0), (0, 0), (0, 0), (1, 1), (0, 0)))
    grid_x = (index_x * CX - 1 + jnp.arange(CX + 2, dtype=jnp.int32)).astype(jnp.float32)
    grid_y = (index_y * CY - 1 + jnp.arange(CY + 2, dtype=jnp.int32)).astype(jnp.float32)
    grid_z = jnp.arange(-1, LZ + 1, dtype=jnp.int32).astype(jnp.float32)
    positions = jnp.stack(
        [
            padded[0] + grid_x[:, None, None, None],
            padded[1] + grid_y[None, :, None, None],
            padded[2] + grid_z[None, None, :, None],
        ]
    )
    near_potential = near_field(positions[:, 1:-1, 1:-1, 1:-1], positions, padded[3])
    return (far_potential + near_potential).reshape(CX, CY, LZ * PPL)


def solution(mesh):
    in_specs = (P(None, "gx", "gy", None), P("gx", "gy", None))
    out_specs = P("gx", "gy", None)
    return jax.shard_map(body, mesh=mesh, in_specs=in_specs, out_specs=out_specs, check_vma=False)
```

profile of v0, /device:TPU:0, one launch (start us, length us, event | category | flops | bytes accessed | tf_op | source)
XLA Modules:
  0.0 1354.5 jit_solution(2480983473795699243)
XLA Ops:
  9.9 6.1 collective-permute-start
  16.7 4.8 collective-permute-start.4
  32.2 6.0 dot_general.84
  38.2 6.0 reshape.1437
  44.6 41.3 %all_gather.3 = f32[32,1,512]{2,1,0:T(1,128)S(1)} all-gather(f32[1,1,512]{2,1,0:T(1,128)S(1)} %reshape_reshape.29), channel_id=1, replica_groups=mesh['gx'=8,'gy'=4] {'gx','gy'}, dimensions={0}, use_global_device_ids=true | all-gather | bytes 67584 | tf_op jit(solution)/shard_map/all_gather | solution.py:251
  91.7 385.4 %while.55 = (s32[]{:T(128)}, f32[27,512,512]{2,1,0:T(8,128)}, s32[27]{0:T(128)}, s32[]{:T(128)}, s32[1]{0:T(128)}, /*index=5*/s32[]{:T(128)}, s32[]{:T(128)}, s3...) while((s32[]{:T(128)}, f32[27,512,512]{2,1,0:T(8,128)}, s32[27]{0:T(128)}, s32[]{:T(128)}, s32[1]{0:T(128)}, ...), condition=%wide.region_5.6_spmd, body=%wide.region_2.5_spmd.sunk | while | flops 2651413 | bytes 7449731 | solution.py:85
  97.0 2.6 compare_select_fusion.33
  99.5 2.6 compare_select_fusion.32
  111.2 2.6 compare_select_fusion.33
  113.8 2.6 compare_select_fusion.32
  125.5 2.6 compare_select_fusion.33
  128.1 2.6 compare_select_fusion.32
  142.3 2.6 compare_select_fusion.32
  156.6 2.6 compare_select_fusion.32
  168.3 2.6 compare_select_fusion.33
  170.8 2.6 compare_select_fusion.32
  185.1 2.6 compare_select_fusion.32
  199.4 2.6 compare_select_fusion.32
  213.7 2.6 compare_select_fusion.32
  228.1 2.6 compare_select_fusion.32
  242.3 2.6 compare_select_fusion.32
  254.0 2.6 compare_select_fusion.33
  256.6 2.6 compare_select_fusion.32
  270.9 2.6 compare_select_fusion.32
  285.2 2.6 compare_select_fusion.32
  296.8 2.6 compare_select_fusion.33
  299.4 2.6 compare_select_fusion.32
  313.7 2.6 compare_select_fusion.32
  327.9 2.6 compare_select_fusion.32
  342.2 2.6 compare_select_fusion.32
  356.5 2.6 compare_select_fusion.32
  370.7 2.6 compare_select_fusion.32
  385.0 2.6 compare_select_fusion.32
  399.3 2.6 compare_select_fusion.32
  413.5 2.6 compare_select_fusion.32
  427.8 2.6 compare_select_fusion.32
  442.1 2.6 compare_select_fusion.32
  456.5 2.6 compare_select_fusion.32
  470.7 2.6 compare_select_fusion.32
  477.1 279.2 %while.57 = (s32[]{:T(128)}, f32[4,512]{1,0:T(4,128)S(1)}, s32[27]{0:T(128)S(1)}, f32[3,3,6,512]{3,2,1,0:T(8,128)S(1)}, f32[27,512,512]{2,1,0:T(8,128)}, /*index...) while((s32[]{:T(128)}, f32[4,512]{1,0:T(4,128)S(1)}, ...), condition=%wide.region_9.10_spmd.clone, body=%wide.region_8.9_spmd.clone.sunk | while | flops 12587056 | bytes 1073759 | solution.py:133
  756.4 276.0 %while.56 = (s32[]{:T(128)}, f32[2,512]{1,0:T(2,128)S(1)}, s32[27]{0:T(128)S(1)}, f32[3,3,4,512]{3,2,0,1:T(4,128)S(1)}, f32[27,512,512]{2,1,0:T(8,128)}, /*index...) while((s32[]{:T(128)}, f32[2,512]{1,0:T(2,128)S(1)}, ...), condition=%wide.region_7.8_spmd.clone, body=%wide.region_6.7_spmd.clone.sunk | while | flops 6293552 | bytes 1061471 | solution.py:133
  1039.4 3.0 collective-permute-start.2
  1044.0 4.1 collective-permute-start.6
  1050.6 274.5 %while.58 = (s32[]{:T(128)}, f32[8,512]{1,0:T(8,128)S(1)}, s32[27]{0:T(128)S(1)}, f32[3,3,10,512]{3,2,1,0:T(8,128)S(1)}, f32[27,512,512]{2,1,0:T(8,128)}, /*inde...) while((s32[]{:T(128)}, f32[8,512]{1,0:T(8,128)S(1)}, ...), condition=%wide.region_11.12_spmd.clone, body=%wide.region_10.11_spmd.clone.sunk | while | flops 25174064 | bytes 1098335 | solution.py:133
  1326.6 3.3 fusion.65
  1333.5 4.6 multiply_reduce_fusion.2
  1338.1 7.4 multiply_reduce_fusion.9
  1345.5 8.3 multiply_reduce_fusion.8
  (1017 shorter events, 512.3 us)
Async XLA Ops:
  2.3 13.7 %copy-start.2 = (f32[3,2,2,1024]{3,2,1,0:T(2,128)S(1)}, f32[3,2,2,1024]{3,2,1,0:T(2,128)}, u32[]{:S(2)}) copy-start(f32[3,2,2,1024]{3,2,1,0:T(2,128)} %param.11) | copy-start | bytes 147460
  2.3 13.7 %copy-start.3 = (f32[2,2,1024]{2,1,0:T(2,128)S(1)}, f32[2,2,1024]{2,1,0:T(2,128)}, u32[]{:S(2)}) copy-start(f32[2,2,1024]{2,1,0:T(2,128)} %param.12) | copy-start | bytes 49156
  6.0 32.2 %copy-start = (f32[2,2,16,64,64]{4,3,2,1,0:T(8,128)}, f32[2,2,16,64,64]{4,3,2,1,0:T(8,128)S(1)}, u32[]{:S(2)}) copy-start(f32[2,2,16,64,64]{4,3,2,1,0:T(8,128)S(1)} %copy.95) | copy-start | bytes 3145732
  8.6 1028.7 %collective-permute-start.1 = (f32[2,2,1024]{2,1,0:T(2,128)}, f32[2,2,1024]{2,1,0:T(2,128)}, u32[]{:S(2)}, u32[]{:S(2)}) collective-permute-start(f32[2,2,1024]{2,1,0:T(2,128)} %reshape.1255), channel_id=1, source_target_pairs={{4,0},{8,4},{12,8},{16,12},{20,16},{24,20},{28,24},{5,1},{9,5},{13... | collective-permute-start | bytes 49160 | tf_op jit(solution)/shard_map/ppermute | solution.py:23
  9.9 1026.0 %collective-permute-start = (f32[2,2,1024]{2,1,0:T(2,128)}, f32[2,2,1024]{2,1,0:T(2,128)}, u32[]{:S(2)}, u32[]{:S(2)}) collective-permute-start(f32[2,2,1024]{2,1,0:T(2,128)} %reshape.1255), channel_id=1, source_target_pairs={{0,4},{4,8},{8,12},{12,16},{16,20},{20,24},{24,28},{1,5},{5,9},{9,... | collective-permute-start | bytes 49160 | tf_op jit(solution)/shard_map/ppermute | solution.py:20
  16.7 1025.7 %collective-permute-start.4 = (f32[4,1,2,1024]{3,2,1,0:T(2,128)}, f32[4,1,2,1024]{3,2,1,0:T(2,128)}, u32[]{:S(2)}, u32[]{:S(2)}) collective-permute-start(f32[4,1,2,1024]{3,2,1,0:T(2,128)} %get-tuple-element.663), channel_id=1, source_target_pairs={{0,4},{4,8},{8,12},{12,16},{16,20},{20,24},{24,28},{1,5},{5,9},{9,... | collective-permute-start | bytes 98312 | tf_op jit(solution)/shard_map/ppermute | solution.py:20
  21.5 1020.9 %collective-permute-start.5 = (f32[4,1,2,1024]{3,2,1,0:T(2,128)}, f32[4,1,2,1024]{3,2,1,0:T(2,128)}, u32[]{:S(2)}, u32[]{:S(2)}) collective-permute-start(f32[4,1,2,1024]{3,2,1,0:T(2,128)} %get-tuple-element.664), channel_id=1, source_target_pairs={{4,0},{8,4},{12,8},{16,12},{20,16},{24,20},{28,24},{5,1},{9,5},{13... | collective-permute-start | bytes 98312 | tf_op jit(solution)/shard_map/ppermute | solution.py:23
  477.1 279.2 %copy-start.7 = (f32[2,1,2,512]{3,2,0,1:T(2,128)S(1)}, f32[2,1,2,512]{3,2,0,1:T(2,128)}, u32[]{:S(2)}) copy-start(f32[2,1,2,512]{3,2,0,1:T(2,128)} %reshape.1248) | copy-start | bytes 24580
  756.3 276.1 %copy-start.4 = (f32[64,64]{1,0:T(8,128)S(1)}, f32[64,64]{1,0:T(8,128)}, u32[]{:S(2)}) copy-start(f32[64,64]{1,0:T(8,128)} %fusion.34) | copy-start | bytes 49156
  1038.1 11.5 collective-permute-start.3
  1039.4 10.3 collective-permute-start.2
  1044.0 286.0 %collective-permute-start.6 = (f32[4,4,1,1024]{3,2,1,0:T(1,128)}, f32[4,4,1,1024]{3,2,1,0:T(1,128)}, u32[]{:S(2)}, u32[]{:S(2)}) collective-permute-start(f32[4,4,1,1024]{3,2,1,0:T(1,128)} %get-tuple-element.659), channel_id=1, source_target_pairs={{0,1},{1,2},{2,3},{4,5},{5,6},{6,7},{8,9},{9,10},{10,11},{12,13},{... | collective-permute-start | bytes 196616 | tf_op jit(solution)/shard_map/ppermute | solution.py:20
  1048.1 281.9 %collective-permute-start.7 = (f32[4,4,1,1024]{3,2,1,0:T(1,128)}, f32[4,4,1,1024]{3,2,1,0:T(1,128)}, u32[]{:S(2)}, u32[]{:S(2)}) collective-permute-start(f32[4,4,1,1024]{3,2,1,0:T(1,128)} %get-tuple-element.660), channel_id=1, source_target_pairs={{1,0},{2,1},{3,2},{5,4},{6,5},{7,6},{9,8},{10,9},{11,10},{13,12},{... | collective-permute-start | bytes 196616 | tf_op jit(solution)/shard_map/ppermute | solution.py:23
  1050.1 276.5 %copy-start.1 = (f32[2,2,16,64,64]{4,3,2,1,0:T(8,128)S(1)}, f32[2,2,16,64,64]{4,3,2,1,0:T(8,128)}, u32[]{:S(2)}) copy-start(f32[2,2,16,64,64]{4,3,2,1,0:T(8,128)} %copy-done) | copy-start | bytes 3145732
  1050.6 280.8 %copy-start.8 = (f32[4]{0:T(128)S(1)}, f32[4]{0:T(128)}, u32[]{:S(2)}) copy-start(f32[4]{0:T(128)} %add_convert_fusion.5) | copy-start | bytes 52
  1332.5 5.7 copy-start.5
  1332.5 5.7 copy-start.6
where the time goes:
time: 1370 us; the launch traced here: 1350 us
  loops' own time  661 us (48%)
  other arithmetic  246 us (18%)
  local copies, waits for them, and re-layouts  223 us (16%)
  matrix products  159 us (12%)
  blocking collectives  41.3 us (3%)
  starting transfers between devices  23.4 us (2%)
    another operation x3, loops' own time, far_translate(): lax.scan(step_fn, jnp.zeros((size_x * size_y * size_z, 512), jnp.float32)...  572 us
    dot_general x88, matrix products, matmul(): jnp.dot(left, right, precision=highest, preferred_element_type=jnp.float32)  154 us
    another operation x1, loops' own time, translation_tables(): return lax.map(one_table, jnp.arange(27, dtype=jnp.int32))  88.9 us
    dynamic_slice x108, local copies, waits for them, and re-layouts, translation_tables(): return lax.map(one_table, jnp.arange(27, dtype=jnp.int32))  81.1 us
    gather x28, other arithmetic, node_grid(): points[counter % 4]  72.3 us
    gather x28, other arithmetic, node_grid(): points[counter // 16]  72.1 us
    slice x81, local copies, waits for them, and re-layouts, step_fn(): offset[2] + 1  52.2 us
    all_gather x1, blocking collectives, body(): gathered = lax.all_gather(first_piece, ('gx', 'gy'), axis=0, tiled=True)  41.3 us
  transfers between devices with their start and end apart: 8, of which 0 were waited for; matrix products, arithmetic and copies ran while one was open for 44% of the time, Pallas kernels for 0%

commit v1 on v0

v1 whole, which is shorter than its diff:
```python
import itertools

import jax
import jax.numpy as jnp
import ml_dtypes
import numpy as np
from jax import lax
from jax.experimental import pallas as pl
from jax.experimental.pallas import tpu as pltpu
from jax.sharding import PartitionSpec as P

F32 = jnp.float32
BF16 = jnp.bfloat16
MIB = 1 << 20

CX = 2
CY = 2
LZ = 16
ROWS = 8
FEATURES = 32
VMEM = pl.BlockSpec(memory_space=pltpu.VMEM)
HBM = pl.BlockSpec(memory_space=pl.ANY)


def nodes_1d():
    return np.cos((2.0 * np.arange(4) + 1.0) * np.pi / 8.0)


def cheb_terms(value):
    return value, 2.0 * value * value - 1.0, 4.0 * value**3 - 3.0 * value


def node_weights():
    return [[0.5 * term for term in cheb_terms(point)] for point in nodes_1d()]


def node_grid():
    points = nodes_1d()
    counter = np.arange(64)
    return np.stack([points[counter // 16], points[counter // 4 % 4], points[counter % 4]], -1)


def split_two(table):
    high = table.astype(np.float32).astype(ml_dtypes.bfloat16)
    low = (table - high.astype(np.float64)).astype(np.float32).astype(ml_dtypes.bfloat16)
    return high, low


def upward_tensor():
    points = nodes_1d()
    shifted = (points[None, :] + 2.0 * np.arange(2)[:, None] - 1.0) / 2.0
    factor = 0.25 + 0.0 * shifted[..., None]
    for of_value, of_node in zip(cheb_terms(shifted), cheb_terms(points)):
        factor = factor + 0.5 * of_value[..., None] * of_node
    full = np.einsum("xia,yjb,zkc->xyzijkabc", factor, factor, factor)
    return full.reshape(2, 2, 2, 64, 64)


def inverse_distance(offset):
    grid = node_grid()
    spread = (grid[None, :, :] - grid[:, None, :]) / 2.0 - np.asarray(offset, np.float64)
    return 1.0 / np.sqrt(np.sum(spread * spread, -1))


def adjacent(offset):
    return max(abs(int(step)) for step in offset) <= 1


def canonical_tiles():
    return [
        (cx, cy, cz)
        for cx in range(2)
        for cy in range(2)
        for cz in range(4)
        if not (cx == 0 and cy == 0 and cz <= 1)
    ]


def translation_tiles():
    tiles = []
    for cx, cy, cz in canonical_tiles():
        tile = np.zeros((4, 64, 4, 64))
        for source in range(4):
            for target in range(4):
                offset = (
                    2 * cx + source // 2 - target // 2,
                    2 * cy + source % 2 - target % 2,
                    cz,
                )
                if not adjacent(offset):
                    tile[source, :, target, :] = inverse_distance(offset)
        tiles.append(tile.reshape(256, 256))
    return np.stack(split_two(np.stack(tiles)), 1)


def reflection_matrix(flip_x, flip_y, flip_z):
    index = np.arange(256)
    hx, hy, a, b, c = index // 128, index // 64 % 2, index // 16 % 4, index // 4 % 4, index % 4
    if flip_x:
        hx, a = 1 - hx, 3 - a
    if flip_y:
        hy, b = 1 - hy, 3 - b
    if flip_z:
        c = 3 - c
    matrix = np.zeros((256, 256), np.float32)
    matrix[hx * 128 + hy * 64 + a * 16 + b * 4 + c, index] = 1.0
    return matrix


def reflection_tables():
    pairs = [
        np.concatenate([reflection_matrix(fx, fy, 0), reflection_matrix(fx, fy, 1)], 1)
        for fx in range(2)
        for fy in range(2)
    ]
    return np.stack(pairs).astype(ml_dtypes.bfloat16)


def up_tables():
    upward = upward_tensor()
    table = upward.transpose(0, 1, 3, 2, 4).reshape(256, 128)
    return np.stack(split_two(table))


def down_table():
    upward = upward_tensor()
    table = upward.transpose(4, 2, 0, 1, 3).reshape(64, 512)
    high, low = split_two(table)
    return np.concatenate([high, high, low, np.zeros_like(low)], 0)


def top_tables(boxes_x, boxes_y):
    offsets = range(-(boxes_x - 1), boxes_x), range(-(boxes_y - 1), boxes_y)
    table = np.zeros((len(offsets[0]), len(offsets[1]), 2, 64, 2, 64))
    for (ix, dx), (iy, dy) in itertools.product(enumerate(offsets[0]), enumerate(offsets[1])):
        for source, target in itertools.product(range(2), range(2)):
            offset = (dx, dy, source - target)
            if not adjacent(offset):
                table[ix, iy, source, :, target, :] = 0.125 * inverse_distance(offset)
    return np.stack(split_two(table.reshape(len(offsets[0]), len(offsets[1]), 128, 128)), 2)


def leaf_segments():
    table = np.zeros((LZ, LZ * 64), np.float32)
    for leaf in range(LZ):
        table[leaf, leaf * 64 : leaf * 64 + 64] = 1.0
    return table.astype(ml_dtypes.bfloat16)


def halves(value):
    high = value.astype(BF16)
    return high, (value - high.astype(F32)).astype(BF16)


def dot(left, right):
    return jnp.dot(left, right, preferred_element_type=F32)


def dot_three(value, high_table, low_table):
    rows = value.shape[0]
    high, low = halves(value)
    both = dot(jnp.concatenate([high, low], 0), high_table)
    return both[:rows] + both[rows:] + dot(high, low_table)


def lanes(shape):
    return lax.broadcasted_iota(jnp.int32, shape, len(shape) - 1)


def sublanes(shape):
    return lax.broadcasted_iota(jnp.int32, shape, len(shape) - 2)


def lane_flip(value):
    return pltpu.roll(value, 64, 1)


def weight_rows(pattern):
    weights = node_weights()
    index = sublanes((8, 128))
    rows = []
    for term in range(3):
        row = jnp.full((8, 128), weights[pattern(0)][term], F32)
        for sub in range(1, 8):
            row = jnp.where(index == sub, weights[pattern(sub)][term], row)
        rows.append(row)
    return rows


def basis_rows():
    return (
        weight_rows(lambda sub: sub // 4),
        weight_rows(lambda sub: 2 + sub // 4),
        weight_rows(lambda sub: sub % 4),
    )


def basis_tile(row_x, row_y, row_z, scale, tables):
    y_low, y_high, z_all = tables
    wide = [jnp.broadcast_to(2.0 * row - 1.0, (8, 128)) for row in (row_x, row_y, row_z)]
    terms = [cheb_terms(value) for value in wide]

    def mix(weights, term):
        return 0.25 + (weights[0] * term[0] + weights[1] * term[1] + weights[2] * term[2])

    along_z = mix(z_all, terms[2])
    pair = mix(y_low, terms[1]) * along_z, mix(y_high, terms[1]) * along_z
    tiles = []
    for weights in node_weights():
        along_x = mix(weights, terms[0])
        if scale is not None:
            along_x = along_x * scale
        tiles += [along_x * pair[0], along_x * pair[1]]
    return tiles


def three_pieces(value):
    first = value.astype(BF16).astype(F32)
    rest = value - first
    second = rest.astype(BF16).astype(F32)
    return first, second, rest - second


def source_features(coords):
    rows = []
    total = None
    for coord in coords:
        one, two, three = three_pieces(coord)
        rows += [one, two, one, two, three, one]
        total = coord * coord if total is None else total + coord * coord
    unit = jnp.ones_like(coords[0])
    return rows + [unit] * 3 + list(three_pieces(total)) + [jnp.zeros_like(unit)] * 8


def target_features(coords):
    rows = []
    total = None
    for coord in coords:
        one, two, three = three_pieces(-2.0 * coord)
        rows += [one, one, two, two, one, three]
        total = coord * coord if total is None else total + coord * coord
    unit = jnp.ones_like(coords[0])
    return rows + list(three_pieces(total)) + [unit] * 3 + [jnp.zeros_like(unit)] * 8


def store_features(rows, wide_ref, group):
    for row, value in enumerate(rows):
        wide_ref[group, pl.ds(row, ROWS, stride=FEATURES), :] = value


class Near:
    def __init__(self, raw, wide_ref, source_ref, charge_ref, target_ref):
        self.raw = raw
        self.wide_ref = wide_ref
        self.source_ref = source_ref
        self.charge_ref = charge_ref
        self.target_ref = target_ref
        self.groups = 0
        self.charges = 0
        self.upper = lanes((ROWS, 128)) >= 64
        self.row = sublanes((ROWS, 128))

    def place(self, x, y):
        return self.raw(0, x, y) + (x - 2.0), self.raw(1, x, y) + (y - 2.0)

    def targets(self):
        for ab in range(4):
            x, y = ab // 2 + 1, ab % 2 + 1
            coords = self.place(x, y)
            along_z = self.raw(2, x, y) + jnp.where(self.upper, 0.0, -1.0)
            store_features(target_features(coords + (along_z,)), self.wide_ref, ab)
        for ab in range(4):
            for j in range(ROWS):
                block = self.wide_ref[ab, FEATURES * j : FEATURES * (j + 1), :]
                self.target_ref[ab, j] = block.T.astype(BF16)

    def add_group(self, coords):
        store_features(source_features(coords), self.wide_ref, self.groups)
        self.groups += 1
        return self.groups - 1

    def add_charge(self, charge):
        self.charge_ref[self.charges] = charge
        self.charges += 1
        return self.charges - 1

    def main(self, x, y):
        along_z = self.raw(2, x, y) + jnp.where(self.upper, 0.0, -1.0)
        group = self.add_group(self.place(x, y) + (along_z,))
        return group, self.add_charge(self.raw(3, x, y))

    def outer(self, first, second, side, keep=None):
        place = [self.place(*first), self.place(*second)]

        def merge(one, two):
            if side == 0:
                value = jnp.where(self.upper, two, lane_flip(one))
                return pltpu.roll(value, 1, 0)
            value = jnp.where(self.upper, lane_flip(two), one)
            return pltpu.roll(value, ROWS - 1, 0)

        along_z = merge(self.raw(2, *first), self.raw(2, *second)) + (-2.0 if side == 0 else 1.0)
        coords = (merge(place[0][0], place[1][0]), merge(place[0][1], place[1][1]), along_z)
        charge = merge(self.raw(3, *first), self.raw(3, *second))
        charge = jnp.where(self.row == (0 if side == 0 else ROWS - 1), 0.0, charge)
        group = self.add_group(coords)
        if keep is None:
            return group, self.add_charge(charge)
        low = self.add_charge(jnp.where(self.upper, 0.0, charge))
        high = self.add_charge(jnp.where(self.upper, charge, 0.0))
        return (group, low), (group, high)

    def convert(self):
        for group in range(self.groups):
            for j in range(ROWS):
                block = self.wide_ref[group, FEATURES * j : FEATURES * (j + 1), :]
                self.source_ref[group, j] = block.astype(BF16)

    def run(self, plan, emit):
        eye = sublanes((128, 128)) == lanes((128, 128))

        def pairs(targets, tiles, j, own, total):
            if not tiles:
                return total
            block = jnp.concatenate([self.source_ref[group, j] for group, _ in tiles], 1)
            squared = dot(targets, block)
            for position, (group, charge) in enumerate(tiles):
                inverse = lax.rsqrt(squared[:, 128 * position : 128 * position + 128])
                if group == own:
                    inverse = jnp.where(eye, 0.0, inverse)
                total = total + inverse * self.charge_ref[charge, pl.ds(j, 1), :]
            return total

        def step(j, carry):
            for ab in range(4):
                mains, below, above, own = plan[ab]
                targets = self.target_ref[ab, j]
                total = pairs(targets, mains, j, own, jnp.zeros((128, 128), F32))
                lower = pairs(targets[:64], below, j, None, total[:64])
                higher = pairs(targets[64:], above, j, None, total[64:])
                total = jnp.concatenate([lower, higher], 0)
                emit(ab, j, jnp.sum(total.T, 0, keepdims=True))
            return carry

        lax.fori_loop(0, ROWS, step, 0)


def plan_own(near):
    mains = {(x, y): near.main(x, y) for x in (1, 2) for y in (1, 2)}
    outer = [[near.outer((x, 1), (x, 2), side) for x in (1, 2)] for side in range(2)]
    plan = []
    for ab in range(4):
        own = mains[(ab // 2 + 1, ab % 2 + 1)][0]
        plan.append((list(mains.values()), outer[0], outer[1], own))
    return plan


def plan_beside_y(near):
    plan = []
    sides = []
    for y in (0, 3):
        mains = [near.main(x, y) for x in (1, 2)]
        outer = [[near.outer((1, y), (2, y), side)] for side in range(2)]
        sides.append((mains, outer[0], outer[1], None))
    for ab in range(4):
        plan.append(sides[ab % 2])
    return plan


def plan_beside_x(near):
    plan = []
    for x in (0, 3):
        mains = [near.main(x, y) for y in range(4)]
        middle = [near.outer((x, 1), (x, 2), side) for side in range(2)]
        ends = [near.outer((x, 0), (x, 3), side, keep=True) for side in range(2)]
        for b in range(2):
            plan.append(
                (mains[b : b + 3], [middle[0], ends[0][b]], [middle[1], ends[1][b]], None)
            )
    return plan


def join_plans(plans):
    joined = []
    for ab in range(4):
        parts = [plan[ab] for plan in plans]
        own = next((part[3] for part in parts if part[3] is not None), None)
        joined.append(tuple(sum((part[k] for part in parts), []) for k in range(3)) + (own,))
    return joined


def near_scratch(groups, charges):
    return [
        pltpu.VMEM((groups, ROWS * FEATURES, 128), F32),
        pltpu.VMEM((groups, ROWS, FEATURES, 128), BF16),
        pltpu.VMEM((charges, ROWS, 128), F32),
        pltpu.VMEM((4, ROWS, 128, FEATURES), BF16),
    ]


ONE_ROWS = 8
LEAF_ROWS = 32
EDGE_ROWS = 64


def moments_kernel(offsets, charges, segments, up, own_part, to_low, to_high, basis, sums):
    index_y = lax.axis_index("gy")
    tables = basis_rows()
    for x in range(CX):
        for y in range(CY):
            for j in range(ROWS):
                span = slice(128 * j, 128 * j + 128)
                rows = [offsets[c, x, y : y + 1, span] for c in range(3)]
                charge = charges[x, y : y + 1, span]
                for c, row in enumerate(rows + [charge]):
                    own_part[c, x, y, j : j + 1, :] = row
                    edge = ONE_ROWS + LEAF_ROWS + (c * CX + x) * ROWS + j
                    target = to_low if y == 0 else to_high
                    target[edge : edge + 1, :] = row
                tiles = basis_tile(*rows, charge, tables)
                for k in range(4):
                    pair = jnp.concatenate(tiles[2 * k : 2 * k + 2], 0)
                    high, low = halves(pair)
                    first = (x * CY + y) * 64 + 16 * k
                    basis[0, first : first + 16, span] = high
                    basis[1, first : first + 16, span] = low
    contract = (((1,), (1,)), ((), ()))
    leaf = lax.dot_general(segments[...], basis[0], contract, preferred_element_type=F32)
    leaf = leaf + lax.dot_general(segments[...], basis[1], contract, preferred_element_type=F32)
    sums[...] = dot_three(leaf, up[0], up[1])
    first = sums[pl.ds(0, 8, stride=2), :] + lane_flip(sums[pl.ds(1, 8, stride=2), :])
    first = jnp.where(lanes((8, 128)) < 64, first, 0.0)
    first = jnp.where(lax.rem(index_y, 2) == 1, lane_flip(first), first)
    for target in (to_low, to_high):
        target[0:8, :] = first
        target[8:24, :] = leaf[:, :128]
        target[24:40, :] = leaf[:, 128:]


def moments_call(offsets, charges, segments, up):
    payload = jax.ShapeDtypeStruct((ONE_ROWS + LEAF_ROWS + EDGE_ROWS, 128), F32)
    return pl.pallas_call(
        moments_kernel,
        out_shape=(jax.ShapeDtypeStruct((4, CX, CY, ROWS, 128), F32), payload, payload),
        in_specs=[VMEM] * 4,
        out_specs=(VMEM,) * 3,
        scratch_shapes=[pltpu.VMEM((2, 256, 1024), BF16), pltpu.VMEM((16, 128), F32)],
        compiler_params=pltpu.CompilerParams(vmem_limit_bytes=16 * MIB),
        cost_estimate=pl.CostEstimate(flops=10_000_000, bytes_accessed=300_000, transcendentals=0),
        name="moments",
    )(offsets, charges, segments, up)


PART_ROWS = 4 * 4 * ROWS


def row_kernel(count_y, own_part, to_low, from_low, from_high, *rest):
    others, (out_low, out_high) = rest[:-2], rest[-2:]
    index_y = lax.axis_index("gy")
    ones = count_y // 2 * 8
    has_low = index_y > 0
    has_high = index_y < count_y - 1

    out_low[0:ones, :] = jnp.zeros((ones, 128), F32)
    received = {0: to_low, 1: from_low, count_y - 1: from_high}
    for shift, ref in zip(range(2, count_y - 1), others):
        received[shift] = ref
    for shift, ref in received.items():
        source = lax.rem(index_y - shift + count_y, count_y)
        place = pl.ds(pl.multiple_of(source // 2 * 8, 8), 8)
        out_low[place, :] = out_low[place, :] + ref[0:8, :]
    for piece, (ref, keep) in enumerate(((from_low, has_low), (to_low, None), (from_high, has_high))):
        block = ref[ONE_ROWS : ONE_ROWS + LEAF_ROWS, :]
        if keep is not None:
            block = jnp.where(keep, block, 0.0)
        out_low[ones + LEAF_ROWS * piece : ones + LEAF_ROWS * (piece + 1), :] = block
    shared = ones + 3 * LEAF_ROWS
    out_high[0:shared, :] = out_low[0:shared, :]
    for x, out in enumerate((out_low, out_high)):
        for c in range(4):
            edge = ONE_ROWS + LEAF_ROWS + (c * CX + x) * ROWS
            columns = [
                from_low[edge : edge + ROWS, :],
                own_part[c, x, 0],
                own_part[c, x, 1],
                from_high[edge : edge + ROWS, :],
            ]
            if c == 3:
                columns[0] = jnp.where(has_low, columns[0], 0.0)
                columns[3] = jnp.where(has_high, columns[3], 0.0)
            for y, column in enumerate(columns):
                row = shared + (c * 4 + y) * ROWS
                out[row : row + ROWS, :] = column


def row_call(count_y, own_part, to_low, from_low, from_high, others):
    rows = count_y // 2 * 8 + 3 * LEAF_ROWS + PART_ROWS
    payload = jax.ShapeDtypeStruct((rows, 128), F32)
    operands = (own_part, to_low, from_low, from_high, *others)
    return pl.pallas_call(
        lambda *refs: row_kernel(count_y, *refs),
        out_shape=(payload, payload),
        in_specs=[VMEM] * len(operands),
        out_specs=(VMEM,) * 2,
        compiler_params=pltpu.CompilerParams(vmem_limit_bytes=16 * MIB),
        cost_estimate=pl.CostEstimate(flops=100_000, bytes_accessed=500_000, transcendentals=0),
        name="row",
    )(*operands)


def finish_kernel(count_x, count_y, refs):
    (own_low, own_high, from_low, from_high), refs = refs[:4], refs[4:]
    others, refs = refs[: count_x - 3], refs[count_x - 3 :]
    segments, up, down, flips, top, tiles_hbm, refs = *refs[:6], refs[6:]
    out, refs = refs[0], refs[1:]
    wide_ref, source_ref, charge_ref, target_ref, refs = *refs[:4], refs[4:]
    near_rows, far_rows, tiles, level_one, level_two, boxes, flipped, sums, local, semaphore = refs

    index_x, index_y = lax.axis_index("gx"), lax.axis_index("gy")
    pairs_y = count_y // 2
    ones = pairs_y * 8
    shared = ones + 3 * LEAF_ROWS
    has_low = index_x > 0
    has_high = index_x < count_x - 1
    fetch = pltpu.make_async_copy(tiles_hbm, tiles, semaphore)
    fetch.start()

    columns = (from_low, own_low, own_high, from_high)

    def raw(c, x, y):
        row = shared + (c * 4 + y) * ROWS
        value = columns[x][row : row + ROWS, :]
        if c == 3 and x in (0, 3):
            value = jnp.where(has_low if x == 0 else has_high, value, 0.0)
        return value

    near = Near(raw, wide_ref, source_ref, charge_ref, target_ref)
    near.targets()
    plan = join_plans([plan_own(near), plan_beside_y(near), plan_beside_x(near)])
    near.convert()

    def emit(ab, j, row):
        near_rows[ab, pl.ds(j, 1), :] = row

    near.run(plan, emit)

    level_one[...] = jnp.zeros_like(level_one)
    level_two[...] = jnp.zeros_like(level_two)
    received = {0: own_low, 1: from_low, count_x - 1: from_high}
    for shift, ref in zip(range(2, count_x - 1), others):
        received[shift] = ref
    for shift, ref in received.items():
        source = lax.rem(index_x - shift + count_x, count_x)
        for pair in range(pairs_y):
            level_one[source + 2, pair + 1] = ref[8 * pair : 8 * pair + 8, :]
    half_x = count_x // 2
    children = jnp.concatenate(
        [
            jnp.concatenate([level_one[2 * x + 2, y + 1], level_one[2 * x + 3, y + 1]], 1)
            for x in range(half_x)
            for y in range(pairs_y)
        ],
        0,
    )
    below = half_x * pairs_y * 8
    low_lanes = lanes((4, 128)) < 64
    sums[0:below, :] = dot_three(children, up[0], up[1])
    for x in range(half_x):
        for y in range(pairs_y):
            row = (x * pairs_y + y) * 8
            even = sums[pl.ds(row, 4, stride=2), :]
            odd = sums[pl.ds(row + 1, 4, stride=2), :]
            level_two[x + 2, y + 2, 0:4] = jnp.where(low_lanes, even + lane_flip(odd), 0.0)

    def second_group(group_x, group_y):
        return jnp.concatenate(
            [
                level_two[2 * group_x + h + 2, 2 * group_y + 2]
                + lane_flip(level_two[2 * group_x + h + 2, 2 * group_y + 3])
                for h in range(2)
            ],
            1,
        )

    quarter_x, quarter_y = index_x // 4, index_y // 4
    tops = [(x, y) for x in range(count_x // 4) for y in range(count_y // 4)]
    stacked = jnp.concatenate([second_group(x, y) for x, y in tops], 0)
    if stacked.shape[0] % 16 != 0:
        stacked = jnp.concatenate([stacked, jnp.zeros((8, 256), F32)], 0)
    sums[0 : stacked.shape[0], :] = dot_three(stacked, up[0], up[1])
    top_far = jnp.zeros((16, 128), F32)
    for position, (x, y) in enumerate(tops):
        even = sums[pl.ds(8 * position, 2, stride=2), :]
        odd = sums[pl.ds(8 * position + 1, 2, stride=2), :]
        third = jnp.where(lanes((2, 128)) < 64, even + lane_flip(odd), 0.0)
        third = third[0:1] + lane_flip(third)[1:2]
        table = top.at[x - quarter_x + count_x // 4 - 1, y - quarter_y + count_y // 4 - 1]
        top_far = top_far + dot_three(jnp.broadcast_to(third, (16, 128)), table[0], table[1])

    boxes[...] = jnp.zeros_like(boxes)
    leaf_refs = {-1: from_low, 0: own_low, 1: from_high}
    for gx in (-1, 0, 1):
        for gy in (-1, 0, 1):
            start = ones + LEAF_ROWS * (gy + 1)
            for h in range(2):
                block = leaf_refs[gx][start + 16 * h : start + 16 * h + 16, :]
                if gx != 0:
                    block = jnp.where(has_low if gx < 0 else has_high, block, 0.0)
                span = slice(128 * h, 128 * h + 128)
                boxes[8:24, span] = block
                boxes[32:40, span] = level_one[
                    2 * (index_x // 2 + gx) + h + 2, index_y // 2 + gy + 1
                ]
            boxes[48:56, :] = second_group(quarter_x + gx, quarter_y + gy)
            high, low = halves(boxes[...])
            table = flips[2 * (gx < 0) + (gy < 0)]
            mixed = dot(jnp.concatenate([high, low], 0), table)
            group = 3 * (gx + 1) + gy + 1
            for z in range(2):
                flipped[group, z, 0] = mixed[:64, 256 * z : 256 * z + 256]
                flipped[group, z, 1] = mixed[64:, 256 * z : 256 * z + 256]

    fetch.wait()
    odd_row = lax.rem(sublanes((32, 256)), 2) == 1
    totals = {}
    for position, (cx, cy, cz) in enumerate(canonical_tiles()):
        entries = [
            (gx, gy, dz)
            for gx in sorted({cx, -cx})
            for gy in sorted({cy, -cy})
            for dz in sorted({cz, -cz})
        ]
        pieces = [[], []]
        for gx, gy, dz in entries:
            group = 3 * (gx + 1) + gy + 1
            for part in range(2):
                view = flipped.at[group, int(dz < 0), part]
                block = jnp.concatenate(
                    [view[8 + dz : 24 + dz, :], view[32 + dz : 40 + dz, :], view[48 + dz : 56 + dz, :]],
                    0,
                )
                if abs(dz) == 3:
                    block = jnp.where(odd_row if dz < 0 else ~odd_row, block, 0.0)
                pieces[part].append(block.astype(BF16))
        rows = 32 * len(entries)
        both = dot(jnp.concatenate(pieces[0] + pieces[1], 0), tiles[position, 0])
        result = both[:rows] + both[rows:] + dot(jnp.concatenate(pieces[0], 0), tiles[position, 1])
        for order, (gx, gy, dz) in enumerate(entries):
            key = (int(gx < 0), int(gy < 0), int(dz < 0))
            piece = result[32 * order : 32 * order + 32]
            totals[key] = totals[key] + piece if key in totals else piece
    far = None
    for (fx, fy, fz), total in totals.items():
        if (fx, fy, fz) != (0, 0, 0):
            high, low = halves(total)
            table = flips[2 * fx + fy, :, 256 * fz : 256 * fz + 256]
            both = dot(jnp.concatenate([high, low], 0), table)
            total = both[:32] + both[32:]
        far = total if far is None else far + total

    def select(block, hx, hy):
        tile = jnp.where(hx == 1, block[:, 128:256], block[:, 0:128])
        return jnp.where(hy == 1, lane_flip(tile), tile)

    def refine(parent):
        keep = lanes((16, 128)) < 64
        parent = jnp.where(keep, parent, 0.0)
        high = parent.astype(BF16).astype(F32)
        low = parent - high
        left = jnp.concatenate([high + lane_flip(low), high], 1).astype(BF16)
        spread = dot(left, down[...])
        for half in range(2):
            for h in range(2):
                span = slice(256 * half + 128 * h, 256 * half + 128 * h + 128)
                local[h, pl.ds(half, 16, stride=2), :] = spread[:, span]
        return jnp.concatenate([local[0], local[1]], 1)

    top_local = jnp.where(
        sublanes((16, 128)) == 0, top_far, jnp.where(sublanes((16, 128)) == 1, lane_flip(top_far), 0.0)
    )
    children_far = refine(top_local)
    half_index_x, half_index_y = index_x // 2, index_y // 2
    second = select(children_far[0:8], lax.rem(half_index_x, 2), lax.rem(half_index_y, 2))
    second = second + 0.25 * select(far[24:32], lax.rem(half_index_x, 2), lax.rem(half_index_y, 2))
    zeros = jnp.zeros((8, 128), F32)
    children_far = refine(jnp.concatenate([second, zeros], 0))
    first = select(children_far[0:8], lax.rem(index_x, 2), lax.rem(index_y, 2))
    first = first + 0.5 * select(far[16:24], lax.rem(index_x, 2), lax.rem(index_y, 2))
    leaf = refine(jnp.concatenate([first, zeros], 0))[0:16] + far[0:16]

    one, two = halves(leaf)
    turned = jnp.concatenate([one.astype(F32), two.astype(F32)], 0).T.astype(BF16)
    table = jnp.concatenate([segments[...], segments[...]], 0)
    tables = basis_rows()
    for x in range(CX):
        for y in range(CY):
            column = x * CY + y
            spread = dot(turned[64 * column : 64 * column + 64], table)
            for j in range(ROWS):
                span = slice(128 * j, 128 * j + 128)
                rows = [raw(c, x + 1, y + 1)[j : j + 1] for c in range(3)]
                basis = basis_tile(*rows, None, tables)
                total = None
                for k in range(8):
                    term = basis[k] * spread[8 * k : 8 * k + 8, span]
                    total = term if total is None else total + term
                value = jnp.sum(total, 0, keepdims=True) + near_rows[column, j : j + 1, :]
                out[x, y : y + 1, span] = value


def finish_call(count_x, count_y, payloads, others, constants):
    segments, up, down, flips, top, tiles = constants
    operands = (*payloads, *others, segments, up, down, flips, top, tiles)
    half_x, half_y = count_x // 2, count_y // 2
    scratch = near_scratch(32, 36) + [
        pltpu.VMEM((4, ROWS, 128), F32),
        pltpu.VMEM((4, ROWS, 128), F32),
        pltpu.VMEM(tiles.shape, BF16),
        pltpu.VMEM((count_x + 4, half_y + 2, 8, 128), F32),
        pltpu.VMEM((half_x + 4, half_y + 4, 8, 128), F32),
        pltpu.VMEM((64, 256), F32),
        pltpu.VMEM((9, 2, 2, 64, 256), F32),
        pltpu.VMEM((max(16, half_x * half_y * 8), 128), F32),
        pltpu.VMEM((2, 32, 128), F32),
        pltpu.SemaphoreType.DMA,
    ]
    return pl.pallas_call(
        lambda *refs: finish_kernel(count_x, count_y, refs),
        out_shape=jax.ShapeDtypeStruct((CX, CY, LZ * 64), F32),
        in_specs=[VMEM] * (len(operands) - 1) + [HBM],
        out_specs=VMEM,
        scratch_shapes=scratch,
        compiler_params=pltpu.CompilerParams(vmem_limit_bytes=56 * MIB),
        name="finish",
    )(*operands)


def shift_ring(value, axis, shift):
    count = lax.axis_size(axis)
    return lax.ppermute(value, axis, [(i, (i + shift) % count) for i in range(count)])


def solution(mesh):
    count_x, count_y = mesh.shape["gx"], mesh.shape["gy"]
    segments, up, down, flips = leaf_segments(), up_tables(), down_table(), reflection_tables()
    top, tiles = top_tables(count_x // 4, count_y // 4), translation_tiles()

    def body(offsets, charges):
        constants = [jnp.asarray(table) for table in (segments, up, down, flips, top, tiles)]
        own_part, to_low, to_high = moments_call(offsets, charges, constants[0], constants[1])
        from_low = shift_ring(to_high, "gy", 1)
        from_high = shift_ring(to_low, "gy", count_y - 1)
        own_one = to_low[:ONE_ROWS]
        others = [shift_ring(own_one, "gy", shift) for shift in range(2, count_y - 1)]
        row_low, row_high = row_call(count_y, own_part, to_low, from_low, from_high, others)
        next_low = shift_ring(row_high, "gx", 1)
        next_high = shift_ring(row_low, "gx", count_x - 1)
        row_one = row_low[: count_y // 2 * 8]
        others = [shift_ring(row_one, "gx", shift) for shift in range(2, count_x - 1)]
        payloads = (row_low, row_high, next_low, next_high)
        return finish_call(count_x, count_y, payloads, others, constants)

    in_specs = (P(None, "gx", "gy", None), P("gx", "gy", None))
    out_specs = P("gx", "gy", None)
    return jax.shard_map(body, mesh=mesh, in_specs=in_specs, out_specs=out_specs, check_vma=False)
```

time: 1370 us -> 43.7 us (0.03); the launches traced: 1350 us -> 43.4 us
  loops' own time: 661 us -> 0 us
  other arithmetic: 246 us -> 0 us
  local copies, waits for them, and re-layouts: 223 us -> 3.97 us
  matrix products: 159 us -> 0 us
  blocking collectives: 41.3 us -> 0 us
  Pallas kernels: 0 us -> 15.9 us
    another operation x4 -> x0, loops' own time: 661 us -> none  [the longest x3 572 us: far_translate(): lax.scan(step_fn, jnp.zeros((size_x * size_y * size_z, 512), jnp.float32)...]
    dot_general x90 -> x0, matrix products: 159 us -> none  [the longest x88 154 us: matmul(): jnp.dot(left, right, precision=highest, preferred_element_type=jnp.float32)]
    gather x56 -> x0, other arithmetic: 144 us -> none  [the longest x28 72.3 us: node_grid(): points[counter % 4]]
    dynamic_slice x110 -> x0, local copies, waits for them, and re-layouts: 81.1 us -> none  [the longest x108 81.1 us: translation_tables(): return lax.map(one_table, jnp.arange(27, dtype=jnp.int32))]
    slice x87 -> x2, local copies, waits for them, and re-layouts: 53.3 us -> 0.01 us  [the longest x1 0.01 us: body(): own_one = to_low[:ONE_ROWS]]
    reduce_sum x31 -> x0, other arithmetic: 51.2 us -> none  [the longest x27 30.7 us: translation(): distance = jnp.sqrt(jnp.sum(separation * separation, -1))]
    all_gather x1 -> x0, blocking collectives: 41.3 us -> none  [body(): gathered = lax.all_gather(first_piece, ('gx', 'gy'), axis=0, tiled=True)]
    dynamic_update_slice x27 -> x0, local copies, waits for them, and re-layouts: 29 us -> none  [translation_tables(): return lax.map(one_table, jnp.arange(27, dtype=jnp.int32))]
  transfers between devices with their start and end apart: 8 -> 10, of which waited for: 0 -> 4; matrix products, arithmetic and copies ran while one was open for 44% -> 0% of each run, Pallas kernels for 0% -> 0%
where the time goes in v1:
time: 43.7 us; the launch traced here: 43.4 us
  Pallas kernels  15.9 us (36%)
  starting transfers between devices  14.6 us (33%)
  waiting for transfers between devices  8.86 us (20%)
  local copies, waits for them, and re-layouts  3.97 us (9%)
    pallas_call x1, Pallas kernels, finish_call(): pl.pallas_call(lambda *refs: finish_kernel(count_x, count_y, refs), out_s...  14.8 us
    ppermute x10, starting transfers between devices, shift_ring(): lax.ppermute(value, axis, [(i, (i + shift) % count) for i in range(count)])  14.6 us
    ppermute x10, waiting for transfers between devices, shift_ring(): lax.ppermute(value, axis, [(i, (i + shift) % count) for i in range(count)])  8.86 us
    unnamed x26, local copies, waits for them, and re-layouts  3.21 us
    pallas_call x1, Pallas kernels, moments_call(): pl.pallas_call(moments_kernel, out_shape=(jax.ShapeDtypeStruct((4, CX, CY...  1.08 us
  transfers between devices with their start and end apart: 10, of which 4 were waited for; matrix products, arithmetic and copies ran while one was open for 0% of the time, Pallas kernels for 0%

profile of v1, /device:TPU:0, one launch (start us, length us, event | category | flops | bytes accessed | tf_op | source)
XLA Modules:
  0.0 43.4 jit_solution(11987479554156432705)
XLA Ops:
  0.0 0.0 copy-start
  0.0 0.9 %copy-done = bf16[2,256,128]{2,1,0:T(8,128)(2,1)S(1)} copy-done((bf16[2,256,128]{2,1,0:T(8,128)(2,1)S(1)}, bf16[2,256,128]{2,1,0:T(8,128)(2,1)}, u32[]{:S(2)}) %copy-start) | copy-done | bytes 131096
  0.9 0.0 copy-start.2
  0.9 0.8 %copy-done.2 = bf16[16,1024]{1,0:T(8,128)(2,1)S(1)} copy-done((bf16[16,1024]{1,0:T(8,128)(2,1)S(1)}, bf16[16,1024]{1,0:T(8,128)(2,1)}, u32[]{:S(2)}) %copy-start.2) | copy-done | bytes 32792
  1.7 0.0 copy-start.4
  1.7 0.8 %copy-done.4 = f32[3,2,2,1024]{3,2,1,0:T(2,128)S(1)} copy-done((f32[3,2,2,1024]{3,2,1,0:T(2,128)S(1)}, f32[3,2,2,1024]{3,2,1,0:T(2,128)}, u32[]{:S(2)}) %copy-start.4) | copy-done | bytes 49176
  2.5 0.0 copy-start.5
  2.5 0.7 %copy-done.5 = f32[2,2,1024]{2,1,0:T(2,128)S(1)} copy-done((f32[2,2,1024]{2,1,0:T(2,128)S(1)}, f32[2,2,1024]{2,1,0:T(2,128)}, u32[]{:S(2)}) %copy-start.5) | copy-done | bytes 16408
  3.2 1.1 %moments.1 = (f32[4,2,2,8,128]{4,3,2,1,0:T(8,128)S(1)}, f32[104,128]{1,0:T(8,128)S(1)}, f32[104,128]{1,0:T(8,128)S(1)}) custom-call(f32[3,2,2,1024]{3,2,1,0:T(2,128)S(1)} %copy-done.4, f32[2,2,1024]{2,1,0:T(2,128)S(1)} %copy-done.5, bf16[16,1024]{1,0:T(8,128)(2,1)S(1)} %copy-done.2, bf16[2,256,128]{2,1,0:T(8,128)(2,1)S(1)} %copy-done), custom_call_target="tpu_custom_call" | custom-call | flops 10000000 | bytes 300000 | tf_op jit(solution)/shard_map/moments/pallas_call | solution.py:442
  4.3 0.5 %collective-permute-start = (f32[104,128]{1,0:T(8,128)S(1)}, f32[104,128]{1,0:T(8,128)S(1)}, u32[]{:S(2)}, u32[]{:S(2)}) collective-permute-start(f32[104,128]{1,0:T(8,128)S(1)} %get-tuple-element.12), channel_id=1, source_target_pairs={{0,1},{1,2},{2,3},{3,0},{4,5},{5,6},{6,7},{7,4},{8,9},{9,10},{10,1... | collective-permute-start | bytes 159752 | tf_op jit(solution)/shard_map/ppermute | solution.py:740
  4.7 1.9 %collective-permute-start.1 = (f32[104,128]{1,0:T(8,128)S(1)}, f32[104,128]{1,0:T(8,128)S(1)}, u32[]{:S(2)}, u32[]{:S(2)}) collective-permute-start(f32[104,128]{1,0:T(8,128)S(1)} %get-tuple-element.11.refs_1_), channel_id=1, source_target_pairs={{0,3},{1,0},{2,1},{3,2},{4,7},{5,4},{6,5},{7,6},{8,11},{9,8},{10,9... | collective-permute-start | bytes 159752 | tf_op jit(solution)/shard_map/ppermute | solution.py:740
  6.7 2.3 %collective-permute-start.2 = (f32[8,128]{1,0:T(8,128)S(1)}, f32[8,128]{1,0:T(8,128)S(1)}, u32[]{:S(2)}, u32[]{:S(2)}) collective-permute-start(f32[8,128]{1,0:T(8,128)S(1)} %slice.6), channel_id=1, source_target_pairs={{0,2},{1,3},{2,0},{3,1},{4,6},{5,7},{6,4},{7,5},{8,10},{9,11},{10,... | collective-permute-start | bytes 12296 | tf_op jit(solution)/shard_map/ppermute | solution.py:740
  9.0 2.1 %collective-permute-done.2.refs_4_ = f32[8,128]{1,0:T(8,128)S(1)} collective-permute-done((f32[8,128]{1,0:T(8,128)S(1)}, f32[8,128]{1,0:T(8,128)S(1)}, u32[]{:S(2)}, u32[]{:S(2)}) %collective-permute-start.2) | collective-permute-done | bytes 4128 | tf_op jit(solution)/shard_map/ppermute | solution.py:740
  11.1 0.0 collective-permute-done.refs_2_
  11.1 0.0 collective-permute-done.1.refs_3_
  11.2 0.0 copy-start.1
  11.2 0.0 copy-start.3
  11.2 1.6 %collective-permute-start.3 = (f32[240,128]{1,0:T(8,128)S(1)}, f32[240,128]{1,0:T(8,128)S(1)}, u32[]{:S(2)}, u32[]{:S(2)}) collective-permute-start(f32[240,128]{1,0:T(8,128)S(1)} %get-tuple-element.14.refs_1_), channel_id=1, source_target_pairs={{0,4},{4,8},{8,12},{12,16},{16,20},{20,24},{24,28},{28,0},{1,5},{5... | collective-permute-start | bytes 368648 | tf_op jit(solution)/shard_map/ppermute | solution.py:740
  12.8 3.2 %collective-permute-start.4 = (f32[240,128]{1,0:T(8,128)S(1)}, f32[240,128]{1,0:T(8,128)S(1)}, u32[]{:S(2)}, u32[]{:S(2)}) collective-permute-start(f32[240,128]{1,0:T(8,128)S(1)} %get-tuple-element.13.refs_0_), channel_id=1, source_target_pairs={{0,28},{4,0},{8,4},{12,8},{16,12},{20,16},{24,20},{28,24},{1,29},{... | collective-permute-start | bytes 368648 | tf_op jit(solution)/shard_map/ppermute | solution.py:740
  16.0 1.8 %collective-permute-start.9 = (f32[16,128]{1,0:T(8,128)S(1)}, f32[16,128]{1,0:T(8,128)S(1)}, u32[]{:S(2)}, u32[]{:S(2)}) collective-permute-start(f32[16,128]{1,0:T(8,128)S(1)} %slice.7), channel_id=1, source_target_pairs={{0,24},{4,28},{8,0},{12,4},{16,8},{20,12},{24,16},{28,20},{1,25},{... | collective-permute-start | bytes 24584 | tf_op jit(solution)/shard_map/ppermute | solution.py:740
  17.8 0.0 collective-permute-start.8
  17.8 3.0 %collective-permute-start.7 = (f32[16,128]{1,0:T(8,128)S(1)}, f32[16,128]{1,0:T(8,128)S(1)}, u32[]{:S(2)}, u32[]{:S(2)}) collective-permute-start(f32[16,128]{1,0:T(8,128)S(1)} %slice.7), channel_id=1, source_target_pairs={{0,16},{4,20},{8,24},{12,28},{16,0},{20,4},{24,8},{28,12},{1,17},{... | collective-permute-start | bytes 24584 | tf_op jit(solution)/shard_map/ppermute | solution.py:740
  20.8 0.0 collective-permute-done.9.refs_8_
  20.8 0.0 copy-start.8
  20.8 0.0 collective-permute-start.6
  20.8 1.6 %collective-permute-done.8.refs_7_ = f32[16,128]{1,0:T(8,128)S(1)} collective-permute-done((f32[16,128]{1,0:T(8,128)S(1)}, f32[16,128]{1,0:T(8,128)S(1)}, u32[]{:S(2)}, u32[]{:S(2)}) %collective-permute-start.8) | collective-permute-done | bytes 8224 | tf_op jit(solution)/shard_map/ppermute | solution.py:740
  22.3 0.0 copy-start.9
  22.3 0.3 collective-permute-start.5
  22.6 0.0 collective-permute-done.7.refs_6_
  22.6 0.0 copy-start.10
  22.6 3.6 %collective-permute-done.6.refs_5_ = f32[16,128]{1,0:T(8,128)S(1)} collective-permute-done((f32[16,128]{1,0:T(8,128)S(1)}, f32[16,128]{1,0:T(8,128)S(1)}, u32[]{:S(2)}, u32[]{:S(2)}) %collective-permute-start.6) | collective-permute-done | bytes 8224 | tf_op jit(solution)/shard_map/ppermute | solution.py:740
  26.2 0.0 copy-start.11
  26.2 1.6 %collective-permute-done.5.refs_4_ = f32[16,128]{1,0:T(8,128)S(1)} collective-permute-done((f32[16,128]{1,0:T(8,128)S(1)}, f32[16,128]{1,0:T(8,128)S(1)}, u32[]{:S(2)}, u32[]{:S(2)}) %collective-permute-start.5) | collective-permute-done | bytes 8224 | tf_op jit(solution)/shard_map/ppermute | solution.py:740
  27.8 0.0 copy-start.12
  27.8 0.0 collective-permute-done.3.refs_2_
  27.8 0.0 collective-permute-done.4.refs_3_
  27.8 0.0 copy-start.7
  27.8 0.8 %jit_solution_.3.refs_13_ = bf16[3,1,2,128,128]{4,3,2,1,0:T(8,128)(2,1)} broadcast(bf16[]{:T(256)} %constant.16.clone), dimensions={} | broadcast | bytes 196610 | tf_op jit(solution)
  28.6 0.0 copy-done.1
  28.6 0.0 copy-done.3
  28.6 0.0 copy-done.8
  28.6 0.0 copy-done.9
  28.6 0.0 copy-done.10
  28.6 0.0 copy-done.11
  28.6 0.0 copy-done.12
  28.6 0.0 copy-done.6
  28.6 0.0 copy-done.7
  28.6 14.8 %finish.1 = f32[2,2,1024]{2,1,0:T(2,128)} custom-call(f32[240,128]{1,0:T(8,128)} %copy-done.1, f32[240,128]{1,0:T(8,128)} %copy-done.3, f32[240,128]{1,0:T(8,128)} %copy-done.6, f32[240,128]{1,0:T(8,128)} %copy-done.7, f32[16,128]{1,0:T(8,128)} %copy-done.12, f32[16,128]{1,0:T(8,128)} %copy-done.11, f32[16,128]{1,0:T(8,128)} %copy-done.10, ...), custom_call_target="tpu_custom_call" | custom-call | tf_op jit(solution)/shard_map/finish/pallas_call | solution.py:727
  (4 shorter events, 0.1 us)
Async XLA Ops:
  0.0 0.9 %copy-start = (bf16[2,256,128]{2,1,0:T(8,128)(2,1)S(1)}, bf16[2,256,128]{2,1,0:T(8,128)(2,1)}, u32[]{:S(2)}) copy-start(bf16[2,256,128]{2,1,0:T(8,128)(2,1)} %constant.13.clone.up.refs_10_) | copy-start | bytes 393220
  0.9 0.8 %copy-start.2 = (bf16[16,1024]{1,0:T(8,128)(2,1)S(1)}, bf16[16,1024]{1,0:T(8,128)(2,1)}, u32[]{:S(2)}) copy-start(bf16[16,1024]{1,0:T(8,128)(2,1)} %constant.12.clone.segments.refs_9_) | copy-start | bytes 98308
  1.7 0.8 %copy-start.4 = (f32[3,2,2,1024]{3,2,1,0:T(2,128)S(1)}, f32[3,2,2,1024]{3,2,1,0:T(2,128)}, u32[]{:S(2)}) copy-start(f32[3,2,2,1024]{3,2,1,0:T(2,128)} %offsets.1) | copy-start | bytes 147460
  2.5 0.7 %copy-start.5 = (f32[2,2,1024]{2,1,0:T(2,128)S(1)}, f32[2,2,1024]{2,1,0:T(2,128)}, u32[]{:S(2)}) copy-start(f32[2,2,1024]{2,1,0:T(2,128)} %charges.1) | copy-start | bytes 49156
  4.3 6.9 %collective-permute-start = (f32[104,128]{1,0:T(8,128)S(1)}, f32[104,128]{1,0:T(8,128)S(1)}, u32[]{:S(2)}, u32[]{:S(2)}) collective-permute-start(f32[104,128]{1,0:T(8,128)S(1)} %get-tuple-element.12), channel_id=1, source_target_pairs={{0,1},{1,2},{2,3},{3,0},{4,5},{5,6},{6,7},{7,4},{8,9},{9,10},{10,1... | collective-permute-start | bytes 159752 | tf_op jit(solution)/shard_map/ppermute | solution.py:740
  4.7 6.4 %collective-permute-start.1 = (f32[104,128]{1,0:T(8,128)S(1)}, f32[104,128]{1,0:T(8,128)S(1)}, u32[]{:S(2)}, u32[]{:S(2)}) collective-permute-start(f32[104,128]{1,0:T(8,128)S(1)} %get-tuple-element.11.refs_1_), channel_id=1, source_target_pairs={{0,3},{1,0},{2,1},{3,2},{4,7},{5,4},{6,5},{7,6},{8,11},{9,8},{10,9... | collective-permute-start | bytes 159752 | tf_op jit(solution)/shard_map/ppermute | solution.py:740
  6.7 4.5 %collective-permute-start.2 = (f32[8,128]{1,0:T(8,128)S(1)}, f32[8,128]{1,0:T(8,128)S(1)}, u32[]{:S(2)}, u32[]{:S(2)}) collective-permute-start(f32[8,128]{1,0:T(8,128)S(1)} %slice.6), channel_id=1, source_target_pairs={{0,2},{1,3},{2,0},{3,1},{4,6},{5,7},{6,4},{7,5},{8,10},{9,11},{10,... | collective-permute-start | bytes 12296 | tf_op jit(solution)/shard_map/ppermute | solution.py:740
  11.2 17.4 %copy-start.1 = (f32[240,128]{1,0:T(8,128)}, f32[240,128]{1,0:T(8,128)S(1)}, u32[]{:S(2)}) copy-start(f32[240,128]{1,0:T(8,128)S(1)} %get-tuple-element.13.refs_0_) | copy-start | bytes 368644
  11.2 17.4 %copy-start.3 = (f32[240,128]{1,0:T(8,128)}, f32[240,128]{1,0:T(8,128)S(1)}, u32[]{:S(2)}) copy-start(f32[240,128]{1,0:T(8,128)S(1)} %get-tuple-element.14.refs_1_) | copy-start | bytes 368644
  11.2 16.6 %collective-permute-start.3 = (f32[240,128]{1,0:T(8,128)S(1)}, f32[240,128]{1,0:T(8,128)S(1)}, u32[]{:S(2)}, u32[]{:S(2)}) collective-permute-start(f32[240,128]{1,0:T(8,128)S(1)} %get-tuple-element.14.refs_1_), channel_id=1, source_target_pairs={{0,4},{4,8},{8,12},{12,16},{16,20},{20,24},{24,28},{28,0},{1,5},{5... | collective-permute-start | bytes 368648 | tf_op jit(solution)/shard_map/ppermute | solution.py:740
  12.8 15.0 %collective-permute-start.4 = (f32[240,128]{1,0:T(8,128)S(1)}, f32[240,128]{1,0:T(8,128)S(1)}, u32[]{:S(2)}, u32[]{:S(2)}) collective-permute-start(f32[240,128]{1,0:T(8,128)S(1)} %get-tuple-element.13.refs_0_), channel_id=1, source_target_pairs={{0,28},{4,0},{8,4},{12,8},{16,12},{20,16},{24,20},{28,24},{1,29},{... | collective-permute-start | bytes 368648 | tf_op jit(solution)/shard_map/ppermute | solution.py:740
  16.0 4.8 %collective-permute-start.9 = (f32[16,128]{1,0:T(8,128)S(1)}, f32[16,128]{1,0:T(8,128)S(1)}, u32[]{:S(2)}, u32[]{:S(2)}) collective-permute-start(f32[16,128]{1,0:T(8,128)S(1)} %slice.7), channel_id=1, source_target_pairs={{0,24},{4,28},{8,0},{12,4},{16,8},{20,12},{24,16},{28,20},{1,25},{... | collective-permute-start | bytes 24584 | tf_op jit(solution)/shard_map/ppermute | solution.py:740
  17.8 4.5 %collective-permute-start.8 = (f32[16,128]{1,0:T(8,128)S(1)}, f32[16,128]{1,0:T(8,128)S(1)}, u32[]{:S(2)}, u32[]{:S(2)}) collective-permute-start(f32[16,128]{1,0:T(8,128)S(1)} %slice.7), channel_id=1, source_target_pairs={{0,20},{4,24},{8,28},{12,0},{16,4},{20,8},{24,12},{28,16},{1,21},{... | collective-permute-start | bytes 24584 | tf_op jit(solution)/shard_map/ppermute | solution.py:740
  17.8 4.8 %collective-permute-start.7 = (f32[16,128]{1,0:T(8,128)S(1)}, f32[16,128]{1,0:T(8,128)S(1)}, u32[]{:S(2)}, u32[]{:S(2)}) collective-permute-start(f32[16,128]{1,0:T(8,128)S(1)} %slice.7), channel_id=1, source_target_pairs={{0,16},{4,20},{8,24},{12,28},{16,0},{20,4},{24,8},{28,12},{1,17},{... | collective-permute-start | bytes 24584 | tf_op jit(solution)/shard_map/ppermute | solution.py:740
  20.8 7.8 %copy-start.8 = (f32[16,128]{1,0:T(8,128)}, f32[16,128]{1,0:T(8,128)S(1)}, u32[]{:S(2)}) copy-start(f32[16,128]{1,0:T(8,128)S(1)} %collective-permute-done.9.refs_8_) | copy-start | bytes 24580
  20.8 5.4 %collective-permute-start.6 = (f32[16,128]{1,0:T(8,128)S(1)}, f32[16,128]{1,0:T(8,128)S(1)}, u32[]{:S(2)}, u32[]{:S(2)}) collective-permute-start(f32[16,128]{1,0:T(8,128)S(1)} %slice.7), channel_id=1, source_target_pairs={{0,12},{4,16},{8,20},{12,24},{16,28},{20,0},{24,4},{28,8},{1,13},{... | collective-permute-start | bytes 24584 | tf_op jit(solution)/shard_map/ppermute | solution.py:740
  22.3 6.2 %copy-start.9 = (f32[16,128]{1,0:T(8,128)}, f32[16,128]{1,0:T(8,128)S(1)}, u32[]{:S(2)}) copy-start(f32[16,128]{1,0:T(8,128)S(1)} %collective-permute-done.8.refs_7_) | copy-start | bytes 24580
  22.3 5.4 %collective-permute-start.5 = (f32[16,128]{1,0:T(8,128)S(1)}, f32[16,128]{1,0:T(8,128)S(1)}, u32[]{:S(2)}, u32[]{:S(2)}) collective-permute-start(f32[16,128]{1,0:T(8,128)S(1)} %slice.7), channel_id=1, source_target_pairs={{0,8},{4,12},{8,16},{12,20},{16,24},{20,28},{24,0},{28,4},{1,9},{5... | collective-permute-start | bytes 24584 | tf_op jit(solution)/shard_map/ppermute | solution.py:740
  22.6 5.9 %copy-start.10 = (f32[16,128]{1,0:T(8,128)}, f32[16,128]{1,0:T(8,128)S(1)}, u32[]{:S(2)}) copy-start(f32[16,128]{1,0:T(8,128)S(1)} %collective-permute-done.7.refs_6_) | copy-start | bytes 24580
  26.2 2.4 %copy-start.11 = (f32[16,128]{1,0:T(8,128)}, f32[16,128]{1,0:T(8,128)S(1)}, u32[]{:S(2)}) copy-start(f32[16,128]{1,0:T(8,128)S(1)} %collective-permute-done.6.refs_5_) | copy-start | bytes 24580
  27.8 0.8 %copy-start.12 = (f32[16,128]{1,0:T(8,128)}, f32[16,128]{1,0:T(8,128)S(1)}, u32[]{:S(2)}) copy-start(f32[16,128]{1,0:T(8,128)S(1)} %collective-permute-done.5.refs_4_) | copy-start | bytes 24580
  27.8 0.8 %copy-start.6 = (f32[240,128]{1,0:T(8,128)}, f32[240,128]{1,0:T(8,128)S(1)}, u32[]{:S(2)}) copy-start(f32[240,128]{1,0:T(8,128)S(1)} %collective-permute-done.3.refs_2_) | copy-start | bytes 368644
  27.8 0.8 %copy-start.7 = (f32[240,128]{1,0:T(8,128)}, f32[240,128]{1,0:T(8,128)S(1)}, u32[]{:S(2)}) copy-start(f32[240,128]{1,0:T(8,128)S(1)} %collective-permute-done.4.refs_3_) | copy-start | bytes 368644

commit v2 on v1

--- a/solution.py
+++ b/solution.py
@@ -19,7 +19,7 @@
 ROWS = 8
 FEATURES = 32
 VMEM = pl.BlockSpec(memory_space=pltpu.VMEM)
-HBM = pl.BlockSpec(memory_space=pl.ANY)
+HBM = pl.BlockSpec(memory_space=pltpu.HBM)
 
 
 def nodes_1d():
@@ -140,11 +140,10 @@
     return np.stack(split_two(table.reshape(len(offsets[0]), len(offsets[1]), 128, 128)), 2)
 
 
-def leaf_segments():
-    table = np.zeros((LZ, LZ * 64), np.float32)
-    for leaf in range(LZ):
-        table[leaf, leaf * 64 : leaf * 64 + 64] = 1.0
-    return table.astype(ml_dtypes.bfloat16)
+def small_tables(boxes_x, boxes_y):
+    down = down_table().reshape(256, 4, 128).transpose(1, 0, 2)
+    parts = [up_tables(), down, top_tables(boxes_x, boxes_y)]
+    return np.concatenate([part.reshape(-1, 128) for part in parts], 0)
 
 
 def halves(value):
@@ -169,6 +168,11 @@
 
 def sublanes(shape):
     return lax.broadcasted_iota(jnp.int32, shape, len(shape) - 2)
+
+
+def leaf_segments(leaves):
+    shape = (leaves, LZ * 64)
+    return jnp.where(lanes(shape) // 64 == lax.rem(sublanes(shape), LZ), 1.0, 0.0).astype(BF16)
 
 
 def lane_flip(value):
@@ -249,10 +253,9 @@
 
 
 class Near:
-    def __init__(self, raw, wide_ref, source_ref, charge_ref, target_ref):
+    def __init__(self, raw, wide_ref, charge_ref, target_ref):
         self.raw = raw
         self.wide_ref = wide_ref
-        self.source_ref = source_ref
         self.charge_ref = charge_ref
         self.target_ref = target_ref
         self.groups = 0
@@ -310,20 +313,15 @@
         high = self.add_charge(jnp.where(self.upper, charge, 0.0))
         return (group, low), (group, high)
 
-    def convert(self):
-        for group in range(self.groups):
-            for j in range(ROWS):
-                block = self.wide_ref[group, FEATURES * j : FEATURES * (j + 1), :]
-                self.source_ref[group, j] = block.astype(BF16)
-
     def run(self, plan, emit):
         eye = sublanes((128, 128)) == lanes((128, 128))
 
         def pairs(targets, tiles, j, own, total):
             if not tiles:
                 return total
-            block = jnp.concatenate([self.source_ref[group, j] for group, _ in tiles], 1)
-            squared = dot(targets, block)
+            span = pl.ds(pl.multiple_of(j * FEATURES, FEATURES), FEATURES)
+            block = jnp.concatenate([self.wide_ref[group, span, :] for group, _ in tiles], 1)
+            squared = dot(targets, block.astype(BF16))
             for position, (group, charge) in enumerate(tiles):
                 inverse = lax.rsqrt(squared[:, 128 * position : 128 * position + 128])
                 if group == own:
@@ -392,7 +390,6 @@
 def near_scratch(groups, charges):
     return [
         pltpu.VMEM((groups, ROWS * FEATURES, 128), F32),
-        pltpu.VMEM((groups, ROWS, FEATURES, 128), BF16),
         pltpu.VMEM((charges, ROWS, 128), F32),
         pltpu.VMEM((4, ROWS, 128, FEATURES), BF16),
     ]
@@ -403,9 +400,21 @@
 EDGE_ROWS = 64
 
 
-def moments_kernel(offsets, charges, segments, up, own_part, to_low, to_high, basis, sums):
+def moments_kernel(
+    offsets_hbm, charges_hbm, small_hbm, own_part, to_low, to_high, offsets, charges, up, basis, sums, semaphores
+):
     index_y = lax.axis_index("gy")
+    copies = [
+        pltpu.make_async_copy(offsets_hbm, offsets, semaphores.at[0]),
+        pltpu.make_async_copy(charges_hbm, charges, semaphores.at[1]),
+        pltpu.make_async_copy(small_hbm.at[0:512], up, semaphores.at[2]),
+    ]
+    for copy in copies:
+        copy.start()
     tables = basis_rows()
+    segments = leaf_segments(LZ)
+    copies[0].wait()
+    copies[1].wait()
     for x in range(CX):
         for y in range(CY):
             for j in range(ROWS):
@@ -425,9 +434,10 @@
                     basis[0, first : first + 16, span] = high
                     basis[1, first : first + 16, span] = low
     contract = (((1,), (1,)), ((), ()))
-    leaf = lax.dot_general(segments[...], basis[0], contract, preferred_element_type=F32)
-    leaf = leaf + lax.dot_general(segments[...], basis[1], contract, preferred_element_type=F32)
-    sums[...] = dot_three(leaf, up[0], up[1])
+    leaf = lax.dot_general(segments, basis[0], contract, preferred_element_type=F32)
+    leaf = leaf + lax.dot_general(segments, basis[1], contract, preferred_element_type=F32)
+    copies[2].wait()
+    sums[...] = dot_three(leaf, up[0:256], up[256:512])
     first = sums[pl.ds(0, 8, stride=2), :] + lane_flip(sums[pl.ds(1, 8, stride=2), :])
     first = jnp.where(lanes((8, 128)) < 64, first, 0.0)
     first = jnp.where(lax.rem(index_y, 2) == 1, lane_flip(first), first)
@@ -437,18 +447,25 @@
         target[24:40, :] = leaf[:, 128:]
 
 
-def moments_call(offsets, charges, segments, up):
+def moments_call(offsets, charges, small):
     payload = jax.ShapeDtypeStruct((ONE_ROWS + LEAF_ROWS + EDGE_ROWS, 128), F32)
     return pl.pallas_call(
         moments_kernel,
         out_shape=(jax.ShapeDtypeStruct((4, CX, CY, ROWS, 128), F32), payload, payload),
-        in_specs=[VMEM] * 4,
+        in_specs=[HBM] * 3,
         out_specs=(VMEM,) * 3,
-        scratch_shapes=[pltpu.VMEM((2, 256, 1024), BF16), pltpu.VMEM((16, 128), F32)],
-        compiler_params=pltpu.CompilerParams(vmem_limit_bytes=16 * MIB),
+        scratch_shapes=[
+            pltpu.VMEM(offsets.shape, F32),
+            pltpu.VMEM(charges.shape, F32),
+            pltpu.VMEM((512, 128), BF16),
+            pltpu.VMEM((2, 256, 1024), BF16),
+            pltpu.VMEM((16, 128), F32),
+            pltpu.SemaphoreType.DMA((3,)),
+        ],
+        compiler_params=pltpu.CompilerParams(vmem_limit_bytes=8 * MIB),
         cost_estimate=pl.CostEstimate(flops=10_000_000, bytes_accessed=300_000, transcendentals=0),
         name="moments",
-    )(offsets, charges, segments, up)
+    )(offsets, charges, small)
 
 
 PART_ROWS = 4 * 4 * ROWS
@@ -502,7 +519,7 @@
         out_shape=(payload, payload),
         in_specs=[VMEM] * len(operands),
         out_specs=(VMEM,) * 2,
-        compiler_params=pltpu.CompilerParams(vmem_limit_bytes=16 * MIB),
+        compiler_params=pltpu.CompilerParams(vmem_limit_bytes=8 * MIB),
         cost_estimate=pl.CostEstimate(flops=100_000, bytes_accessed=500_000, transcendentals=0),
         name="row",
     )(*operands)
@@ -511,10 +528,10 @@
 def finish_kernel(count_x, count_y, refs):
     (own_low, own_high, from_low, from_high), refs = refs[:4], refs[4:]
     others, refs = refs[: count_x - 3], refs[count_x - 3 :]
-    segments, up, down, flips, top, tiles_hbm, refs = *refs[:6], refs[6:]
+    constants, refs = refs[:3], refs[3:]
     out, refs = refs[0], refs[1:]
-    wide_ref, source_ref, charge_ref, target_ref, refs = *refs[:4], refs[4:]
-    near_rows, far_rows, tiles, level_one, level_two, boxes, flipped, sums, local, semaphore = refs
+    wide_ref, charge_ref, target_ref, refs = *refs[:3], refs[3:]
+    near_rows, small, flips, tiles, level_one, level_two, boxes, flipped, sums, local, semaphores = refs
 
     index_x, index_y = lax.axis_index("gx"), lax.axis_index("gy")
     pairs_y = count_y // 2
@@ -522,8 +539,12 @@
     shared = ones + 3 * LEAF_ROWS
     has_low = index_x > 0
     has_high = index_x < count_x - 1
-    fetch = pltpu.make_async_copy(tiles_hbm, tiles, semaphore)
-    fetch.start()
+    fetches = [
+        pltpu.make_async_copy(constant, place, semaphores.at[k])
+        for k, (constant, place) in enumerate(zip(constants, (small, flips, tiles)))
+    ]
+    for fetch in fetches:
+        fetch.start()
 
     columns = (from_low, own_low, own_high, from_high)
 
@@ -534,16 +555,16 @@
             value = jnp.where(has_low if x == 0 else has_high, value, 0.0)
         return value
 
-    near = Near(raw, wide_ref, source_ref, charge_ref, target_ref)
+    near = Near(raw, wide_ref, charge_ref, target_ref)
     near.targets()
     plan = join_plans([plan_own(near), plan_beside_y(near), plan_beside_x(near)])
-    near.convert()
 
     def emit(ab, j, row):
         near_rows[ab, pl.ds(j, 1), :] = row
 
     near.run(plan, emit)
 
+    fetches[0].wait()
     level_one[...] = jnp.zeros_like(level_one)
     level_two[...] = jnp.zeros_like(level_two)
     received = {0: own_low, 1: from_low, count_x - 1: from_high}
@@ -564,7 +585,7 @@
     )
     below = half_x * pairs_y * 8
     low_lanes = lanes((4, 128)) < 64
-    sums[0:below, :] = dot_three(children, up[0], up[1])
+    sums[0:below, :] = dot_three(children, small[0:256], small[256:512])
     for x in range(half_x):
         for y in range(pairs_y):
             row = (x * pairs_y + y) * 8
@@ -587,16 +608,19 @@
     stacked = jnp.concatenate([second_group(x, y) for x, y in tops], 0)
     if stacked.shape[0] % 16 != 0:
         stacked = jnp.concatenate([stacked, jnp.zeros((8, 256), F32)], 0)
-    sums[0 : stacked.shape[0], :] = dot_three(stacked, up[0], up[1])
+    sums[0 : stacked.shape[0], :] = dot_three(stacked, small[0:256], small[256:512])
     top_far = jnp.zeros((16, 128), F32)
     for position, (x, y) in enumerate(tops):
         even = sums[pl.ds(8 * position, 2, stride=2), :]
         odd = sums[pl.ds(8 * position + 1, 2, stride=2), :]
         third = jnp.where(lanes((2, 128)) < 64, even + lane_flip(odd), 0.0)
         third = third[0:1] + lane_flip(third)[1:2]
-        table = top.at[x - quarter_x + count_x // 4 - 1, y - quarter_y + count_y // 4 - 1]
+        step_x, step_y = x - quarter_x + count_x // 4 - 1, y - quarter_y + count_y // 4 - 1
+        row = 1536 + 256 * (step_x * (count_y // 4 * 2 - 1) + step_y)
+        table = [small[pl.ds(pl.multiple_of(row + 128 * k, 128), 128), :] for k in range(2)]
         top_far = top_far + dot_three(jnp.broadcast_to(third, (16, 128)), table[0], table[1])
 
+    fetches[1].wait()
     boxes[...] = jnp.zeros_like(boxes)
     leaf_refs = {-1: from_low, 0: own_low, 1: from_high}
     for gx in (-1, 0, 1):
@@ -620,7 +644,7 @@
                 flipped[group, z, 0] = mixed[:64, 256 * z : 256 * z + 256]
                 flipped[group, z, 1] = mixed[64:, 256 * z : 256 * z + 256]
 
-    fetch.wait()
+    fetches[2].wait()
     odd_row = lax.rem(sublanes((32, 256)), 2) == 1
     totals = {}
     for position, (cx, cy, cz) in enumerate(canonical_tiles()):
@@ -668,7 +692,8 @@
         high = parent.astype(BF16).astype(F32)
         low = parent - high
         left = jnp.concatenate([high + lane_flip(low), high], 1).astype(BF16)
-        spread = dot(left, down[...])
+        down = jnp.concatenate([small[512 + 256 * k : 768 + 256 * k, :] for k in range(4)], 1)
+        spread = dot(left, down)
         for half in range(2):
             for h in range(2):
                 span = slice(256 * half + 128 * h, 256 * half + 128 * h + 128)
@@ -690,7 +715,7 @@
 
     one, two = halves(leaf)
     turned = jnp.concatenate([one.astype(F32), two.astype(F32)], 0).T.astype(BF16)
-    table = jnp.concatenate([segments[...], segments[...]], 0)
+    table = leaf_segments(2 * LZ)
     tables = basis_rows()
     for x in range(CX):
         for y in range(CY):
@@ -709,30 +734,32 @@
 
 
 def finish_call(count_x, count_y, payloads, others, constants):
-    segments, up, down, flips, top, tiles = constants
-    operands = (*payloads, *others, segments, up, down, flips, top, tiles)
+    operands = (*payloads, *others, *constants)
     half_x, half_y = count_x // 2, count_y // 2
     scratch = near_scratch(32, 36) + [
         pltpu.VMEM((4, ROWS, 128), F32),
-        pltpu.VMEM((4, ROWS, 128), F32),
-        pltpu.VMEM(tiles.shape, BF16),
+        *[pltpu.VMEM(constant.shape, BF16) for constant in constants],
         pltpu.VMEM((count_x + 4, half_y + 2, 8, 128), F32),
         pltpu.VMEM((half_x + 4, half_y + 4, 8, 128), F32),
         pltpu.VMEM((64, 256), F32),
         pltpu.VMEM((9, 2, 2, 64, 256), F32),
         pltpu.VMEM((max(16, half_x * half_y * 8), 128), F32),
         pltpu.VMEM((2, 32, 128), F32),
-        pltpu.SemaphoreType.DMA,
+        pltpu.SemaphoreType.DMA((3,)),
     ]
     return pl.pallas_call(
         lambda *refs: finish_kernel(count_x, count_y, refs),
         out_shape=jax.ShapeDtypeStruct((CX, CY, LZ * 64), F32),
-        in_specs=[VMEM] * (len(operands) - 1) + [HBM],
+        in_specs=[VMEM] * (len(operands) - 3) + [HBM] * 3,
         out_specs=VMEM,
         scratch_shapes=scratch,
-        compiler_params=pltpu.CompilerParams(vmem_limit_bytes=56 * MIB),
+        compiler_params=pltpu.CompilerParams(vmem_limit_bytes=24 * MIB),
         name="finish",
     )(*operands)
+
+
+def in_hbm(value):
+    return pltpu.with_memory_space_constraint(value, pltpu.HBM)
 
 
 def shift_ring(value, axis, shift):
@@ -742,12 +769,12 @@
 
 def solution(mesh):
     count_x, count_y = mesh.shape["gx"], mesh.shape["gy"]
-    segments, up, down, flips = leaf_segments(), up_tables(), down_table(), reflection_tables()
-    top, tiles = top_tables(count_x // 4, count_y // 4), translation_tiles()
+    tables = small_tables(count_x // 4, count_y // 4), reflection_tables(), translation_tiles()
 
     def body(offsets, charges):
-        constants = [jnp.asarray(table) for table in (segments, up, down, flips, top, tiles)]
-        own_part, to_low, to_high = moments_call(offsets, charges, constants[0], constants[1])
+        constants = [in_hbm(jnp.asarray(table)) for table in tables]
+        offsets, charges = in_hbm(offsets), in_hbm(charges)
+        own_part, to_low, to_high = moments_call(offsets, charges, constants[0])
         from_low = shift_ring(to_high, "gy", 1)
         from_high = shift_ring(to_low, "gy", count_y - 1)
         own_one = to_low[:ONE_ROWS]

time: 43.7 us -> 39 us (0.89)
  local copies, waits for them, and re-layouts: 3.97 us -> 0.01 us
  Pallas kernels: 15.9 us -> 15.3 us
    unnamed x26 -> x0, local copies, waits for them, and re-layouts: 3.21 us -> none
    pallas_call x1, Pallas kernels: 14.8 us -> 13.3 us  [finish_call(): pl.pallas_call(lambda *refs: finish_kernel(count_x, count_y, refs), out_s...]
    pallas_call x1, Pallas kernels: 1.08 us -> 1.93 us  [moments_call(): pl.pallas_call(moments_kernel, out_shape=(jax.ShapeDtypeStruct((4, CX, CY...]
    another operation x1 -> x0, local copies, waits for them, and re-layouts: 0.76 us -> none
where the time goes in v2:
time: 39 us; the launch traced here: 38.8 us
  Pallas kernels  15.3 us (39%)
  starting transfers between devices  14.6 us (37%)
  waiting for transfers between devices  8.88 us (23%)
    ppermute x10, starting transfers between devices, shift_ring(): lax.ppermute(value, axis, [(i, (i + shift) % count) for i in range(count)])  14.6 us
    pallas_call x1, Pallas kernels, finish_call(): pl.pallas_call(lambda *refs: finish_kernel(count_x, count_y, refs), out_s...  13.3 us
    ppermute x10, waiting for transfers between devices, shift_ring(): lax.ppermute(value, axis, [(i, (i + shift) % count) for i in range(count)])  8.88 us
    pallas_call x1, Pallas kernels, moments_call(): pl.pallas_call(moments_kernel, out_shape=(jax.ShapeDtypeStruct((4, CX, CY...  1.93 us
  transfers between devices with their start and end apart: 10, of which 4 were waited for; matrix products, arithmetic and copies ran while one was open for 0% of the time, Pallas kernels for 0%

profile of v2, /device:TPU:0, one launch (start us, length us, event | category | flops | bytes accessed | tf_op | source)
XLA Modules:
  0.0 38.8 jit_solution(17120200074312003484)
XLA Ops:
  0.0 1.9 %moments.1 = (f32[4,2,2,8,128]{4,3,2,1,0:T(8,128)S(1)}, f32[104,128]{1,0:T(8,128)S(1)}, f32[104,128]{1,0:T(8,128)S(1)}) custom-call(f32[3,2,2,1024]{3,2,1,0:T(2,128)} %offsets_hbm.1, f32[2,2,1024]{2,1,0:T(2,128)} %charges_hbm.1, bf16[2304,128]{1,0:T(8,128)(2,1)} %constant.6.clone.small_hbm.refs_9_), custom_call_target="tpu_custom_call" | custom-call | flops 10000000 | bytes 300000 | tf_op jit(solution)/shard_map/moments/pallas_call | solution.py:452
  1.9 0.5 %collective-permute-start = (f32[104,128]{1,0:T(8,128)S(1)}, f32[104,128]{1,0:T(8,128)S(1)}, u32[]{:S(2)}, u32[]{:S(2)}) collective-permute-start(f32[104,128]{1,0:T(8,128)S(1)} %get-tuple-element.12), channel_id=1, source_target_pairs={{0,1},{1,2},{2,3},{3,0},{4,5},{5,6},{6,7},{7,4},{8,9},{9,10},{10,1... | collective-permute-start | bytes 159752 | tf_op jit(solution)/shard_map/ppermute | solution.py:767
  2.4 2.0 %collective-permute-start.1 = (f32[104,128]{1,0:T(8,128)S(1)}, f32[104,128]{1,0:T(8,128)S(1)}, u32[]{:S(2)}, u32[]{:S(2)}) collective-permute-start(f32[104,128]{1,0:T(8,128)S(1)} %get-tuple-element.11.refs_1_), channel_id=1, source_target_pairs={{0,3},{1,0},{2,1},{3,2},{4,7},{5,4},{6,5},{7,6},{8,11},{9,8},{10,9... | collective-permute-start | bytes 159752 | tf_op jit(solution)/shard_map/ppermute | solution.py:767
  4.4 2.2 %collective-permute-start.2 = (f32[8,128]{1,0:T(8,128)S(1)}, f32[8,128]{1,0:T(8,128)S(1)}, u32[]{:S(2)}, u32[]{:S(2)}) collective-permute-start(f32[8,128]{1,0:T(8,128)S(1)} %slice.6), channel_id=1, source_target_pairs={{0,2},{1,3},{2,0},{3,1},{4,6},{5,7},{6,4},{7,5},{8,10},{9,11},{10,... | collective-permute-start | bytes 12296 | tf_op jit(solution)/shard_map/ppermute | solution.py:767
  6.7 2.1 %collective-permute-done.2.refs_4_ = f32[8,128]{1,0:T(8,128)S(1)} collective-permute-done((f32[8,128]{1,0:T(8,128)S(1)}, f32[8,128]{1,0:T(8,128)S(1)}, u32[]{:S(2)}, u32[]{:S(2)}) %collective-permute-start.2) | collective-permute-done | bytes 4128 | tf_op jit(solution)/shard_map/ppermute | solution.py:767
  8.8 0.0 collective-permute-done.refs_2_
  8.8 0.0 collective-permute-done.1.refs_3_
  8.9 1.6 %collective-permute-start.3 = (f32[240,128]{1,0:T(8,128)S(1)}, f32[240,128]{1,0:T(8,128)S(1)}, u32[]{:S(2)}, u32[]{:S(2)}) collective-permute-start(f32[240,128]{1,0:T(8,128)S(1)} %get-tuple-element.14.refs_1_), channel_id=1, source_target_pairs={{0,4},{4,8},{8,12},{12,16},{16,20},{20,24},{24,28},{28,0},{1,5},{5... | collective-permute-start | bytes 368648 | tf_op jit(solution)/shard_map/ppermute | solution.py:767
  10.5 3.2 %collective-permute-start.4 = (f32[240,128]{1,0:T(8,128)S(1)}, f32[240,128]{1,0:T(8,128)S(1)}, u32[]{:S(2)}, u32[]{:S(2)}) collective-permute-start(f32[240,128]{1,0:T(8,128)S(1)} %get-tuple-element.13.refs_0_), channel_id=1, source_target_pairs={{0,28},{4,0},{8,4},{12,8},{16,12},{20,16},{24,20},{28,24},{1,29},{... | collective-permute-start | bytes 368648 | tf_op jit(solution)/shard_map/ppermute | solution.py:767
  13.7 1.8 %collective-permute-start.9 = (f32[16,128]{1,0:T(8,128)S(1)}, f32[16,128]{1,0:T(8,128)S(1)}, u32[]{:S(2)}, u32[]{:S(2)}) collective-permute-start(f32[16,128]{1,0:T(8,128)S(1)} %slice.7), channel_id=1, source_target_pairs={{0,24},{4,28},{8,0},{12,4},{16,8},{20,12},{24,16},{28,20},{1,25},{... | collective-permute-start | bytes 24584 | tf_op jit(solution)/shard_map/ppermute | solution.py:767
  15.5 0.0 collective-permute-start.8
  15.5 3.0 %collective-permute-start.7 = (f32[16,128]{1,0:T(8,128)S(1)}, f32[16,128]{1,0:T(8,128)S(1)}, u32[]{:S(2)}, u32[]{:S(2)}) collective-permute-start(f32[16,128]{1,0:T(8,128)S(1)} %slice.7), channel_id=1, source_target_pairs={{0,16},{4,20},{8,24},{12,28},{16,0},{20,4},{24,8},{28,12},{1,17},{... | collective-permute-start | bytes 24584 | tf_op jit(solution)/shard_map/ppermute | solution.py:767
  18.4 0.0 collective-permute-done.9.refs_8_
  18.5 0.0 collective-permute-start.6
  18.5 1.6 %collective-permute-done.8.refs_7_ = f32[16,128]{1,0:T(8,128)S(1)} collective-permute-done((f32[16,128]{1,0:T(8,128)S(1)}, f32[16,128]{1,0:T(8,128)S(1)}, u32[]{:S(2)}, u32[]{:S(2)}) %collective-permute-start.8) | collective-permute-done | bytes 8224 | tf_op jit(solution)/shard_map/ppermute | solution.py:767
  20.0 0.3 collective-permute-start.5
  20.3 0.0 collective-permute-done.7.refs_6_
  20.3 3.6 %collective-permute-done.6.refs_5_ = f32[16,128]{1,0:T(8,128)S(1)} collective-permute-done((f32[16,128]{1,0:T(8,128)S(1)}, f32[16,128]{1,0:T(8,128)S(1)}, u32[]{:S(2)}, u32[]{:S(2)}) %collective-permute-start.6) | collective-permute-done | bytes 8224 | tf_op jit(solution)/shard_map/ppermute | solution.py:767
  23.9 1.6 %collective-permute-done.5.refs_4_ = f32[16,128]{1,0:T(8,128)S(1)} collective-permute-done((f32[16,128]{1,0:T(8,128)S(1)}, f32[16,128]{1,0:T(8,128)S(1)}, u32[]{:S(2)}, u32[]{:S(2)}) %collective-permute-start.5) | collective-permute-done | bytes 8224 | tf_op jit(solution)/shard_map/ppermute | solution.py:767
  25.5 0.0 collective-permute-done.3.refs_2_
  25.5 0.0 collective-permute-done.4.refs_3_
  25.5 13.3 %finish.1 = f32[2,2,1024]{2,1,0:T(2,128)} custom-call(f32[240,128]{1,0:T(8,128)S(1)} %get-tuple-element.13.refs_0_, f32[240,128]{1,0:T(8,128)S(1)} %get-tuple-element.14.refs_1_, f32[240,128]{1,0:T(8,128)S(1)} %collective-permute-done.3.refs_2_, f32[240,128]{1,0:T(8,128)S(1)} %collective-permute-done.4.refs_3_, ...), custom_call_target="tpu_custom_call" | custom-call | tf_op jit(solution)/shard_map/finish/pallas_call | solution.py:750
  (3 shorter events, 0.0 us)
Async XLA Ops:
  1.9 6.9 %collective-permute-start = (f32[104,128]{1,0:T(8,128)S(1)}, f32[104,128]{1,0:T(8,128)S(1)}, u32[]{:S(2)}, u32[]{:S(2)}) collective-permute-start(f32[104,128]{1,0:T(8,128)S(1)} %get-tuple-element.12), channel_id=1, source_target_pairs={{0,1},{1,2},{2,3},{3,0},{4,5},{5,6},{6,7},{7,4},{8,9},{9,10},{10,1... | collective-permute-start | bytes 159752 | tf_op jit(solution)/shard_map/ppermute | solution.py:767
  2.4 6.4 %collective-permute-start.1 = (f32[104,128]{1,0:T(8,128)S(1)}, f32[104,128]{1,0:T(8,128)S(1)}, u32[]{:S(2)}, u32[]{:S(2)}) collective-permute-start(f32[104,128]{1,0:T(8,128)S(1)} %get-tuple-element.11.refs_1_), channel_id=1, source_target_pairs={{0,3},{1,0},{2,1},{3,2},{4,7},{5,4},{6,5},{7,6},{8,11},{9,8},{10,9... | collective-permute-start | bytes 159752 | tf_op jit(solution)/shard_map/ppermute | solution.py:767
  4.4 4.4 %collective-permute-start.2 = (f32[8,128]{1,0:T(8,128)S(1)}, f32[8,128]{1,0:T(8,128)S(1)}, u32[]{:S(2)}, u32[]{:S(2)}) collective-permute-start(f32[8,128]{1,0:T(8,128)S(1)} %slice.6), channel_id=1, source_target_pairs={{0,2},{1,3},{2,0},{3,1},{4,6},{5,7},{6,4},{7,5},{8,10},{9,11},{10,... | collective-permute-start | bytes 12296 | tf_op jit(solution)/shard_map/ppermute | solution.py:767
  8.9 16.6 %collective-permute-start.3 = (f32[240,128]{1,0:T(8,128)S(1)}, f32[240,128]{1,0:T(8,128)S(1)}, u32[]{:S(2)}, u32[]{:S(2)}) collective-permute-start(f32[240,128]{1,0:T(8,128)S(1)} %get-tuple-element.14.refs_1_), channel_id=1, source_target_pairs={{0,4},{4,8},{8,12},{12,16},{16,20},{20,24},{24,28},{28,0},{1,5},{5... | collective-permute-start | bytes 368648 | tf_op jit(solution)/shard_map/ppermute | solution.py:767
  10.5 15.0 %collective-permute-start.4 = (f32[240,128]{1,0:T(8,128)S(1)}, f32[240,128]{1,0:T(8,128)S(1)}, u32[]{:S(2)}, u32[]{:S(2)}) collective-permute-start(f32[240,128]{1,0:T(8,128)S(1)} %get-tuple-element.13.refs_0_), channel_id=1, source_target_pairs={{0,28},{4,0},{8,4},{12,8},{16,12},{20,16},{24,20},{28,24},{1,29},{... | collective-permute-start | bytes 368648 | tf_op jit(solution)/shard_map/ppermute | solution.py:767
  13.7 4.8 %collective-permute-start.9 = (f32[16,128]{1,0:T(8,128)S(1)}, f32[16,128]{1,0:T(8,128)S(1)}, u32[]{:S(2)}, u32[]{:S(2)}) collective-permute-start(f32[16,128]{1,0:T(8,128)S(1)} %slice.7), channel_id=1, source_target_pairs={{0,24},{4,28},{8,0},{12,4},{16,8},{20,12},{24,16},{28,20},{1,25},{... | collective-permute-start | bytes 24584 | tf_op jit(solution)/shard_map/ppermute | solution.py:767
  15.5 4.5 %collective-permute-start.8 = (f32[16,128]{1,0:T(8,128)S(1)}, f32[16,128]{1,0:T(8,128)S(1)}, u32[]{:S(2)}, u32[]{:S(2)}) collective-permute-start(f32[16,128]{1,0:T(8,128)S(1)} %slice.7), channel_id=1, source_target_pairs={{0,20},{4,24},{8,28},{12,0},{16,4},{20,8},{24,12},{28,16},{1,21},{... | collective-permute-start | bytes 24584 | tf_op jit(solution)/shard_map/ppermute | solution.py:767
  15.5 4.8 %collective-permute-start.7 = (f32[16,128]{1,0:T(8,128)S(1)}, f32[16,128]{1,0:T(8,128)S(1)}, u32[]{:S(2)}, u32[]{:S(2)}) collective-permute-start(f32[16,128]{1,0:T(8,128)S(1)} %slice.7), channel_id=1, source_target_pairs={{0,16},{4,20},{8,24},{12,28},{16,0},{20,4},{24,8},{28,12},{1,17},{... | collective-permute-start | bytes 24584 | tf_op jit(solution)/shard_map/ppermute | solution.py:767
  18.5 5.4 %collective-permute-start.6 = (f32[16,128]{1,0:T(8,128)S(1)}, f32[16,128]{1,0:T(8,128)S(1)}, u32[]{:S(2)}, u32[]{:S(2)}) collective-permute-start(f32[16,128]{1,0:T(8,128)S(1)} %slice.7), channel_id=1, source_target_pairs={{0,12},{4,16},{8,20},{12,24},{16,28},{20,0},{24,4},{28,8},{1,13},{... | collective-permute-start | bytes 24584 | tf_op jit(solution)/shard_map/ppermute | solution.py:767
  20.0 5.4 %collective-permute-start.5 = (f32[16,128]{1,0:T(8,128)S(1)}, f32[16,128]{1,0:T(8,128)S(1)}, u32[]{:S(2)}, u32[]{:S(2)}) collective-permute-start(f32[16,128]{1,0:T(8,128)S(1)} %slice.7), channel_id=1, source_target_pairs={{0,8},{4,12},{8,16},{12,20},{16,24},{20,28},{24,0},{28,4},{1,9},{5... | collective-permute-start | bytes 24584 | tf_op jit(solution)/shard_map/ppermute | solution.py:767

commit v3 on v2

--- a/solution.py
+++ b/solution.py
@@ -1,3 +1,4 @@
+import functools
 import itertools
 
 import jax
@@ -252,9 +253,12 @@
         wide_ref[group, pl.ds(row, ROWS, stride=FEATURES), :] = value
 
 
+def column(raw, x, y):
+    return raw(0) + (x - 2.0), raw(1) + (y - 2.0), raw(2), raw(3)
+
+
 class Near:
-    def __init__(self, raw, wide_ref, charge_ref, target_ref):
-        self.raw = raw
+    def __init__(self, wide_ref, charge_ref, target_ref):
         self.wide_ref = wide_ref
         self.charge_ref = charge_ref
         self.target_ref = target_ref
@@ -263,15 +267,12 @@
         self.upper = lanes((ROWS, 128)) >= 64
         self.row = sublanes((ROWS, 128))
 
-    def place(self, x, y):
-        return self.raw(0, x, y) + (x - 2.0), self.raw(1, x, y) + (y - 2.0)
-
-    def targets(self):
-        for ab in range(4):
-            x, y = ab // 2 + 1, ab % 2 + 1
-            coords = self.place(x, y)
-            along_z = self.raw(2, x, y) + jnp.where(self.upper, 0.0, -1.0)
-            store_features(target_features(coords + (along_z,)), self.wide_ref, ab)
+    def in_pair(self, along_z):
+        return along_z + jnp.where(self.upper, 0.0, -1.0)
+
+    def targets(self, columns):
+        for ab, (x, y, z, _) in enumerate(columns):
+            store_features(target_features((x, y, self.in_pair(z))), self.wide_ref, ab)
         for ab in range(4):
             for j in range(ROWS):
                 block = self.wide_ref[ab, FEATURES * j : FEATURES * (j + 1), :]
@@ -287,14 +288,11 @@
         self.charges += 1
         return self.charges - 1
 
-    def main(self, x, y):
-        along_z = self.raw(2, x, y) + jnp.where(self.upper, 0.0, -1.0)
-        group = self.add_group(self.place(x, y) + (along_z,))
-        return group, self.add_charge(self.raw(3, x, y))
-
-    def outer(self, first, second, side, keep=None):
-        place = [self.place(*first), self.place(*second)]
-
+    def main(self, source):
+        x, y, z, charge = source
+        return self.add_group((x, y, self.in_pair(z))), self.add_charge(charge)
+
+    def outer(self, first, second, side, keep=False):
         def merge(one, two):
             if side == 0:
                 value = jnp.where(self.upper, two, lane_flip(one))
@@ -302,12 +300,10 @@
             value = jnp.where(self.upper, lane_flip(two), one)
             return pltpu.roll(value, ROWS - 1, 0)
 
-        along_z = merge(self.raw(2, *first), self.raw(2, *second)) + (-2.0 if side == 0 else 1.0)
-        coords = (merge(place[0][0], place[1][0]), merge(place[0][1], place[1][1]), along_z)
-        charge = merge(self.raw(3, *first), self.raw(3, *second))
+        x, y, z, charge = [merge(one, two) for one, two in zip(first, second)]
         charge = jnp.where(self.row == (0 if side == 0 else ROWS - 1), 0.0, charge)
-        group = self.add_group(coords)
-        if keep is None:
+        group = self.add_group((x, y, z + (-2.0 if side == 0 else 1.0)))
+        if not keep:
             return group, self.add_charge(charge)
         low = self.add_charge(jnp.where(self.upper, 0.0, charge))
         high = self.add_charge(jnp.where(self.upper, charge, 0.0))
@@ -317,8 +313,6 @@
         eye = sublanes((128, 128)) == lanes((128, 128))
 
         def pairs(targets, tiles, j, own, total):
-            if not tiles:
-                return total
             span = pl.ds(pl.multiple_of(j * FEATURES, FEATURES), FEATURES)
             block = jnp.concatenate([self.wide_ref[group, span, :] for group, _ in tiles], 1)
             squared = dot(targets, block.astype(BF16))
@@ -330,8 +324,7 @@
             return total
 
         def step(j, carry):
-            for ab in range(4):
-                mains, below, above, own = plan[ab]
+            for ab, mains, below, above, own in plan:
                 targets = self.target_ref[ab, j]
                 total = pairs(targets, mains, j, own, jnp.zeros((128, 128), F32))
                 lower = pairs(targets[:64], below, j, None, total[:64])
@@ -340,68 +333,63 @@
                 emit(ab, j, jnp.sum(total.T, 0, keepdims=True))
             return carry
 
-        lax.fori_loop(0, ROWS, step, 0)
-
-
-def plan_own(near):
-    mains = {(x, y): near.main(x, y) for x in (1, 2) for y in (1, 2)}
-    outer = [[near.outer((x, 1), (x, 2), side) for x in (1, 2)] for side in range(2)]
+        lax.fori_loop(0, ROWS, step, 0, unroll=True)
+
+
+def plan_own(near, columns):
+    mains = [near.main(source) for source in columns]
+    outer = [
+        [near.outer(columns[2 * x], columns[2 * x + 1], side) for x in range(2)]
+        for side in range(2)
+    ]
+    return [(ab, mains, outer[0], outer[1], mains[ab][0]) for ab in range(4)]
+
+
+def plan_beside_y(near, columns):
     plan = []
-    for ab in range(4):
-        own = mains[(ab // 2 + 1, ab % 2 + 1)][0]
-        plan.append((list(mains.values()), outer[0], outer[1], own))
+    for b in range(2):
+        mains = [near.main(source) for source in columns[b]]
+        outer = [[near.outer(*columns[b], side)] for side in range(2)]
+        plan += [(2 * a + b, mains, outer[0], outer[1], None) for a in range(2)]
     return plan
 
 
-def plan_beside_y(near):
-    plan = []
-    sides = []
-    for y in (0, 3):
-        mains = [near.main(x, y) for x in (1, 2)]
-        outer = [[near.outer((1, y), (2, y), side)] for side in range(2)]
-        sides.append((mains, outer[0], outer[1], None))
-    for ab in range(4):
-        plan.append(sides[ab % 2])
-    return plan
-
-
-def plan_beside_x(near):
-    plan = []
-    for x in (0, 3):
-        mains = [near.main(x, y) for y in range(4)]
-        middle = [near.outer((x, 1), (x, 2), side) for side in range(2)]
-        ends = [near.outer((x, 0), (x, 3), side, keep=True) for side in range(2)]
-        for b in range(2):
-            plan.append(
-                (mains[b : b + 3], [middle[0], ends[0][b]], [middle[1], ends[1][b]], None)
-            )
-    return plan
-
-
-def join_plans(plans):
-    joined = []
-    for ab in range(4):
-        parts = [plan[ab] for plan in plans]
-        own = next((part[3] for part in parts if part[3] is not None), None)
-        joined.append(tuple(sum((part[k] for part in parts), []) for k in range(3)) + (own,))
-    return joined
+def plan_beside_x(near, columns, side_x):
+    mains = [near.main(source) for source in columns]
+    middle = [near.outer(columns[1], columns[2], side) for side in range(2)]
+    ends = [near.outer(columns[0], columns[3], side, keep=True) for side in range(2)]
+    return [
+        (2 * side_x + b, mains[b : b + 3], [middle[0], ends[0][b]], [middle[1], ends[1][b]], None)
+        for b in range(2)
+    ]
 
 
 def near_scratch(groups, charges):
     return [
         pltpu.VMEM((groups, ROWS * FEATURES, 128), F32),
         pltpu.VMEM((charges, ROWS, 128), F32),
-        pltpu.VMEM((4, ROWS, 128, FEATURES), BF16),
     ]
+
+
+NEAR_SHAPE = (4, ROWS, 128)
+
+
+def near_cost(pairs):
+    return pl.CostEstimate(flops=40 * pairs, bytes_accessed=600_000, transcendentals=pairs)
 
 
 ONE_ROWS = 8
 LEAF_ROWS = 32
-EDGE_ROWS = 64
+PART_ROWS = 4 * CX * CY * ROWS
+OWN_ROWS = ONE_ROWS + LEAF_ROWS + PART_ROWS
+
+
+def part_row(c, x, y):
+    return ONE_ROWS + LEAF_ROWS + ((c * CX + x) * CY + y) * ROWS
 
 
 def moments_kernel(
-    offsets_hbm, charges_hbm, small_hbm, own_part, to_low, to_high, offsets, charges, up, basis, sums, semaphores
+    offsets_hbm, charges_hbm, small_hbm, block, offsets, charges, up, basis, sums, semaphores
 ):
     index_y = lax.axis_index("gy")
     copies = [
@@ -422,10 +410,8 @@
                 rows = [offsets[c, x, y : y + 1, span] for c in range(3)]
                 charge = charges[x, y : y + 1, span]
                 for c, row in enumerate(rows + [charge]):
-                    own_part[c, x, y, j : j + 1, :] = row
-                    edge = ONE_ROWS + LEAF_ROWS + (c * CX + x) * ROWS + j
-                    target = to_low if y == 0 else to_high
-                    target[edge : edge + 1, :] = row
+                    place = part_row(c, x, y) + j
+                    block[place : place + 1, :] = row
                 tiles = basis_tile(*rows, charge, tables)
                 for k in range(4):
                     pair = jnp.concatenate(tiles[2 * k : 2 * k + 2], 0)
@@ -441,19 +427,17 @@
     first = sums[pl.ds(0, 8, stride=2), :] + lane_flip(sums[pl.ds(1, 8, stride=2), :])
     first = jnp.where(lanes((8, 128)) < 64, first, 0.0)
     first = jnp.where(lax.rem(index_y, 2) == 1, lane_flip(first), first)
-    for target in (to_low, to_high):
-        target[0:8, :] = first
-        target[8:24, :] = leaf[:, :128]
-        target[24:40, :] = leaf[:, 128:]
+    block[0:8, :] = first
+    block[8:24, :] = leaf[:, :128]
+    block[24:40, :] = leaf[:, 128:]
 
 
 def moments_call(offsets, charges, small):
-    payload = jax.ShapeDtypeStruct((ONE_ROWS + LEAF_ROWS + EDGE_ROWS, 128), F32)
     return pl.pallas_call(
         moments_kernel,
-        out_shape=(jax.ShapeDtypeStruct((4, CX, CY, ROWS, 128), F32), payload, payload),
+        out_shape=jax.ShapeDtypeStruct((OWN_ROWS, 128), F32),
         in_specs=[HBM] * 3,
-        out_specs=(VMEM,) * 3,
+        out_specs=VMEM,
         scratch_shapes=[
             pltpu.VMEM(offsets.shape, F32),
             pltpu.VMEM(charges.shape, F32),
@@ -468,75 +452,212 @@
     )(offsets, charges, small)
 
 
-PART_ROWS = 4 * 4 * ROWS
-
-
-def row_kernel(count_y, own_part, to_low, from_low, from_high, *rest):
-    others, (out_low, out_high) = rest[:-2], rest[-2:]
-    index_y = lax.axis_index("gy")
-    ones = count_y // 2 * 8
-    has_low = index_y > 0
-    has_high = index_y < count_y - 1
-
-    out_low[0:ones, :] = jnp.zeros((ones, 128), F32)
-    received = {0: to_low, 1: from_low, count_y - 1: from_high}
-    for shift, ref in zip(range(2, count_y - 1), others):
-        received[shift] = ref
-    for shift, ref in received.items():
-        source = lax.rem(index_y - shift + count_y, count_y)
-        place = pl.ds(pl.multiple_of(source // 2 * 8, 8), 8)
-        out_low[place, :] = out_low[place, :] + ref[0:8, :]
-    for piece, (ref, keep) in enumerate(((from_low, has_low), (to_low, None), (from_high, has_high))):
-        block = ref[ONE_ROWS : ONE_ROWS + LEAF_ROWS, :]
-        if keep is not None:
-            block = jnp.where(keep, block, 0.0)
-        out_low[ones + LEAF_ROWS * piece : ones + LEAF_ROWS * (piece + 1), :] = block
-    shared = ones + 3 * LEAF_ROWS
-    out_high[0:shared, :] = out_low[0:shared, :]
-    for x, out in enumerate((out_low, out_high)):
-        for c in range(4):
-            edge = ONE_ROWS + LEAF_ROWS + (c * CX + x) * ROWS
-            columns = [
-                from_low[edge : edge + ROWS, :],
-                own_part[c, x, 0],
-                own_part[c, x, 1],
-                from_high[edge : edge + ROWS, :],
-            ]
-            if c == 3:
-                columns[0] = jnp.where(has_low, columns[0], 0.0)
-                columns[3] = jnp.where(has_high, columns[3], 0.0)
-            for y, column in enumerate(columns):
-                row = shared + (c * 4 + y) * ROWS
-                out[row : row + ROWS, :] = column
-
-
-def row_call(count_y, own_part, to_low, from_low, from_high, others):
-    rows = count_y // 2 * 8 + 3 * LEAF_ROWS + PART_ROWS
-    payload = jax.ShapeDtypeStruct((rows, 128), F32)
-    operands = (own_part, to_low, from_low, from_high, *others)
+EDGE_ROWS = LEAF_ROWS + 4 * CX * ROWS
+
+
+def bits_below(index, bit):
+    return lax.rem(index, 1 << bit)
+
+
+def bit_of(index, bit):
+    return lax.rem(index // (1 << bit), 2)
+
+
+def in_order(is_first, own, other):
+    return jnp.concatenate([jnp.where(is_first, own, other), jnp.where(is_first, other, own)], 0)
+
+
+def edge_block(block, y):
+    rows = [block[ONE_ROWS : ONE_ROWS + LEAF_ROWS, :]]
+    for c in range(4):
+        for x in range(CX):
+            rows.append(block[part_row(c, x, y) : part_row(c, x, y) + ROWS, :])
+    return jnp.concatenate(rows, 0)
+
+
+def group_kernel(level, last_level, own_ref, other_ref, out):
+    index = lax.axis_index("gy")
+    ones = ONE_ROWS << (level - 1)
+    is_first = bit_of(index, level - 1) == 0
+    if level == 1:
+        out[0:ones, :] = own_ref[0:ones, :] + other_ref[0:ones, :]
+        first = jnp.where(is_first, edge_block(own_ref, 0), edge_block(other_ref, 0))
+        last = jnp.where(is_first, edge_block(other_ref, 1), edge_block(own_ref, 1))
+    else:
+        half = ones // 2
+        out[0:ones, :] = in_order(is_first, own_ref[0:half, :], other_ref[0:half, :])
+        own_far = own_ref[half + EDGE_ROWS : half + 2 * EDGE_ROWS, :]
+        other_far = other_ref[half + EDGE_ROWS : half + 2 * EDGE_ROWS, :]
+        first = jnp.where(is_first, own_far, other_far)
+        last = jnp.where(is_first, other_far, own_far)
+    lower = bit_of(index, level) == 0
+    out[ones : ones + EDGE_ROWS, :] = jnp.where(lower, last, first)
+    if not last_level:
+        out[ones + EDGE_ROWS : ones + 2 * EDGE_ROWS, :] = jnp.where(lower, first, last)
+
+
+def pack_call(kernel, rows, operands, name):
     return pl.pallas_call(
-        lambda *refs: row_kernel(count_y, *refs),
-        out_shape=(payload, payload),
+        kernel,
+        out_shape=jax.ShapeDtypeStruct((rows, 128), F32),
         in_specs=[VMEM] * len(operands),
-        out_specs=(VMEM,) * 2,
+        out_specs=VMEM,
         compiler_params=pltpu.CompilerParams(vmem_limit_bytes=8 * MIB),
-        cost_estimate=pl.CostEstimate(flops=100_000, bytes_accessed=500_000, transcendentals=0),
+        cost_estimate=pl.CostEstimate(flops=100_000, bytes_accessed=300_000, transcendentals=0),
+        name=name,
+    )(*operands)
+
+
+ROW_LEAF = 3 * LEAF_ROWS
+ROW_PART = 4 * 4 * ROWS
+
+
+def row_part(c, y):
+    return ROW_LEAF + (c * 4 + y) * ROWS
+
+
+def row_kernel(levels, block, other, *refs):
+    exchanged, (ones_out, even_out, odd_out) = refs[: 2 * (levels - 1)], refs[-3:]
+    index = lax.axis_index("gy")
+    even = lax.rem(lax.axis_index("gx"), 2) == 0
+    is_first = bit_of(index, 0) == 0
+    low = jnp.where(is_first, 0.0, edge_block(other, 1))
+    high = jnp.where(is_first, edge_block(other, 0), 0.0)
+    ones = ONE_ROWS
+    for level in range(1, levels):
+        own, received = exchanged[2 * level - 2 : 2 * level]
+        ones = ONE_ROWS << (level - 1)
+        facing = received[ones : ones + EDGE_ROWS, :]
+        below = bits_below(index, level)
+        upper = bit_of(index, level) == 1
+        low = jnp.where(upper & (below == 0), facing, low)
+        high = jnp.where(~upper & (below == (1 << level) - 1), facing, high)
+        if level == levels - 1:
+            ones_out[...] = in_order(~upper, own[0:ones, :], received[0:ones, :])
+    leaf = block[ONE_ROWS : ONE_ROWS + LEAF_ROWS, :]
+    for piece, rows in enumerate((low[0:LEAF_ROWS], leaf, high[0:LEAF_ROWS])):
+        for out in (even_out, odd_out):
+            out[LEAF_ROWS * piece : LEAF_ROWS * (piece + 1), :] = rows
+    for c in range(4):
+        columns = []
+        for x in range(CX):
+            row = LEAF_ROWS + (c * CX + x) * ROWS
+            own = [block[part_row(c, x, y) : part_row(c, x, y) + ROWS, :] for y in range(CY)]
+            columns.append([low[row : row + ROWS], *own, high[row : row + ROWS]])
+        for y in range(4):
+            span = slice(row_part(c, y), row_part(c, y) + ROWS)
+            even_out[span, :] = jnp.where(even, columns[1][y], columns[0][y])
+            odd_out[span, :] = jnp.where(even, columns[0][y], columns[1][y])
+
+
+def row_call(levels, operands):
+    ones = jax.ShapeDtypeStruct((ONE_ROWS << (levels - 1), 128), F32)
+    payload = jax.ShapeDtypeStruct((ROW_LEAF + ROW_PART, 128), F32)
+    return pl.pallas_call(
+        lambda *refs: row_kernel(levels, *refs[: 2 * levels], *refs[-3:]),
+        out_shape=(ones, payload, payload),
+        in_specs=[VMEM] * len(operands),
+        out_specs=(VMEM,) * 3,
+        compiler_params=pltpu.CompilerParams(vmem_limit_bytes=8 * MIB),
+        cost_estimate=pl.CostEstimate(flops=100_000, bytes_accessed=600_000, transcendentals=0),
         name="row",
     )(*operands)
 
 
+def merge_call(bit, own, other, after):
+    def kernel(own_ref, other_ref, after_ref, out):
+        is_first = bit_of(lax.axis_index("gx"), bit) == 0
+        out[...] = in_order(is_first, own_ref[...], other_ref[...])
+
+    return pack_call(kernel, 2 * own.shape[0], (own, other, after), "merge")
+
+
+def own_kernel(block, after, out, targets, wide_ref, charge_ref):
+    near = Near(wide_ref, charge_ref, targets)
+
+    def raw(x, y):
+        return lambda c: block[part_row(c, x, y) : part_row(c, x, y) + ROWS, :]
+
+    columns = [column(raw(ab // 2, ab % 2), ab // 2 + 1, ab % 2 + 1) for ab in range(4)]
+    near.targets(columns)
+    plan = plan_own(near, columns)
+
+    def emit(ab, j, row):
+        out[ab, pl.ds(j, 1), :] = row
+
+    near.run(plan, emit)
+
+
+def beside_y_kernel(even_ref, odd_ref, targets, before, out, wide_ref, charge_ref):
+    even = lax.rem(lax.axis_index("gx"), 2) == 0
+    near = Near(wide_ref, charge_ref, targets)
+
+    def raw(x, y):
+        def read(c):
+            span = slice(row_part(c, y), row_part(c, y) + ROWS)
+            return jnp.where(even == (x == 1), even_ref[span, :], odd_ref[span, :])
+
+        return read
+
+    columns = [[column(raw(x, y), x + 1, y) for x in range(2)] for y in (0, 3)]
+    plan = plan_beside_y(near, columns)
+    out[...] = before[...]
+
+    def emit(ab, j, row):
+        out[ab, pl.ds(j, 1), :] = out[ab, pl.ds(j, 1), :] + row
+
+    near.run(plan, emit)
+
+
+def beside_x_kernel(parity, received, targets, before, after, out, wide_ref, charge_ref):
+    index, count = lax.axis_index("gx"), lax.axis_size("gx")
+    even = lax.rem(index, 2) == 0
+    side = jnp.where(even == (parity == 0), 1, 0)
+    alone = (index == 0) | (index == count - 1) if parity == 1 else None
+    near = Near(wide_ref, charge_ref, targets)
+
+    def raw(y):
+        def read(c):
+            value = received[row_part(c, y) : row_part(c, y) + ROWS, :]
+            return jnp.where(alone, 0.0, value) if c == 3 and alone is not None else value
+
+        return read
+
+    columns = [column(raw(y), 3.0 * side.astype(F32), y) for y in range(4)]
+    plan = plan_beside_x(near, columns, side)
+    out[...] = before[...]
+
+    def emit(ab, j, row):
+        out[ab, pl.ds(j, 1), :] = out[ab, pl.ds(j, 1), :] + row
+
+    near.run(plan, emit)
+
+
+def near_call(kernel, operands, groups, charges, pairs, name, with_targets=False):
+    out_shape = jax.ShapeDtypeStruct(NEAR_SHAPE, F32)
+    if with_targets:
+        out_shape = out_shape, jax.ShapeDtypeStruct((4, ROWS, 128, FEATURES), BF16)
+    return pl.pallas_call(
+        kernel,
+        out_shape=out_shape,
+        in_specs=[VMEM] * len(operands),
+        out_specs=(VMEM, VMEM) if with_targets else VMEM,
+        scratch_shapes=near_scratch(groups, charges),
+        compiler_params=pltpu.CompilerParams(vmem_limit_bytes=12 * MIB),
+        cost_estimate=near_cost(pairs),
+        name=name,
+    )(*operands)
+
+
 def finish_kernel(count_x, count_y, refs):
-    (own_low, own_high, from_low, from_high), refs = refs[:4], refs[4:]
-    others, refs = refs[: count_x - 3], refs[count_x - 3 :]
+    (own_block, even_ref, odd_ref, from_even, from_odd, own_ones, other_ones, near_rows), refs = refs[:8], refs[8:]
     constants, refs = refs[:3], refs[3:]
     out, refs = refs[0], refs[1:]
-    wide_ref, charge_ref, target_ref, refs = *refs[:3], refs[3:]
-    near_rows, small, flips, tiles, level_one, level_two, boxes, flipped, sums, local, semaphores = refs
+    small, flips, tiles, level_one, level_two, boxes, flipped, sums, local, semaphores = refs
 
     index_x, index_y = lax.axis_index("gx"), lax.axis_index("gy")
+    is_even = lax.rem(index_x, 2) == 0
     pairs_y = count_y // 2
-    ones = pairs_y * 8
-    shared = ones + 3 * LEAF_ROWS
     has_low = index_x > 0
     has_high = index_x < count_x - 1
     fetches = [
@@ -546,35 +667,17 @@
     for fetch in fetches:
         fetch.start()
 
-    columns = (from_low, own_low, own_high, from_high)
-
-    def raw(c, x, y):
-        row = shared + (c * 4 + y) * ROWS
-        value = columns[x][row : row + ROWS, :]
-        if c == 3 and x in (0, 3):
-            value = jnp.where(has_low if x == 0 else has_high, value, 0.0)
-        return value
-
-    near = Near(raw, wide_ref, charge_ref, target_ref)
-    near.targets()
-    plan = join_plans([plan_own(near), plan_beside_y(near), plan_beside_x(near)])
-
-    def emit(ab, j, row):
-        near_rows[ab, pl.ds(j, 1), :] = row
-
-    near.run(plan, emit)
-
     fetches[0].wait()
     level_one[...] = jnp.zeros_like(level_one)
     level_two[...] = jnp.zeros_like(level_two)
-    received = {0: own_low, 1: from_low, count_x - 1: from_high}
-    for shift, ref in zip(range(2, count_x - 1), others):
-        received[shift] = ref
-    for shift, ref in received.items():
-        source = lax.rem(index_x - shift + count_x, count_x)
+    half_x = count_x // 2
+    lower = index_x < half_x
+    for x in range(half_x):
         for pair in range(pairs_y):
-            level_one[source + 2, pair + 1] = ref[8 * pair : 8 * pair + 8, :]
-    half_x = count_x // 2
+            row = 8 * (x * pairs_y + pair)
+            one, two = own_ones[row : row + 8, :], other_ones[row : row + 8, :]
+            level_one[x + 2, pair + 1] = jnp.where(lower, one, two)
+            level_one[x + half_x + 2, pair + 1] = jnp.where(lower, two, one)
     children = jnp.concatenate(
         [
             jnp.concatenate([level_one[2 * x + 2, y + 1], level_one[2 * x + 3, y + 1]], 1)
@@ -622,16 +725,17 @@
 
     fetches[1].wait()
     boxes[...] = jnp.zeros_like(boxes)
-    leaf_refs = {-1: from_low, 0: own_low, 1: from_high}
     for gx in (-1, 0, 1):
         for gy in (-1, 0, 1):
-            start = ones + LEAF_ROWS * (gy + 1)
             for h in range(2):
-                block = leaf_refs[gx][start + 16 * h : start + 16 * h + 16, :]
-                if gx != 0:
-                    block = jnp.where(has_low if gx < 0 else has_high, block, 0.0)
+                rows = slice(LEAF_ROWS * (gy + 1) + 16 * h, LEAF_ROWS * (gy + 1) + 16 * h + 16)
+                if gx == 0:
+                    moments = even_ref[rows, :]
+                else:
+                    moments = jnp.where(is_even == (gx == 1), from_even[rows, :], from_odd[rows, :])
+                    moments = jnp.where(has_low if gx < 0 else has_high, moments, 0.0)
                 span = slice(128 * h, 128 * h + 128)
-                boxes[8:24, span] = block
+                boxes[8:24, span] = moments
                 boxes[32:40, span] = level_one[
                     2 * (index_x // 2 + gx) + h + 2, index_y // 2 + gy + 1
                 ]
@@ -723,7 +827,8 @@
             spread = dot(turned[64 * column : 64 * column + 64], table)
             for j in range(ROWS):
                 span = slice(128 * j, 128 * j + 128)
-                rows = [raw(c, x + 1, y + 1)[j : j + 1] for c in range(3)]
+                places = [part_row(c, x, y) + j for c in range(3)]
+                rows = [own_block[place : place + 1, :] for place in places]
                 basis = basis_tile(*rows, None, tables)
                 total = None
                 for k in range(8):
@@ -733,11 +838,9 @@
                 out[x, y : y + 1, span] = value
 
 
-def finish_call(count_x, count_y, payloads, others, constants):
-    operands = (*payloads, *others, *constants)
+def finish_call(count_x, count_y, operands, constants):
     half_x, half_y = count_x // 2, count_y // 2
-    scratch = near_scratch(32, 36) + [
-        pltpu.VMEM((4, ROWS, 128), F32),
+    scratch = [
         *[pltpu.VMEM(constant.shape, BF16) for constant in constants],
         pltpu.VMEM((count_x + 4, half_y + 2, 8, 128), F32),
         pltpu.VMEM((half_x + 4, half_y + 4, 8, 128), F32),
@@ -750,42 +853,60 @@
     return pl.pallas_call(
         lambda *refs: finish_kernel(count_x, count_y, refs),
         out_shape=jax.ShapeDtypeStruct((CX, CY, LZ * 64), F32),
-        in_specs=[VMEM] * (len(operands) - 3) + [HBM] * 3,
+        in_specs=[VMEM] * len(operands) + [HBM] * 3,
         out_specs=VMEM,
         scratch_shapes=scratch,
         compiler_params=pltpu.CompilerParams(vmem_limit_bytes=24 * MIB),
         name="finish",
-    )(*operands)
+    )(*operands, *constants)
 
 
 def in_hbm(value):
     return pltpu.with_memory_space_constraint(value, pltpu.HBM)
 
 
-def shift_ring(value, axis, shift):
+def swap_bit(value, axis, bit):
+    return lax.ppermute(value, axis, [(i, i ^ (1 << bit)) for i in range(lax.axis_size(axis))])
+
+
+def swap_odd_even(value, axis):
     count = lax.axis_size(axis)
-    return lax.ppermute(value, axis, [(i, (i + shift) % count) for i in range(count)])
+    partner = [i if i in (0, count - 1) else (i + 1 if i % 2 == 1 else i - 1) for i in range(count)]
+    return lax.ppermute(value, axis, list(enumerate(partner)))
 
 
 def solution(mesh):
     count_x, count_y = mesh.shape["gx"], mesh.shape["gy"]
+    levels_x, levels_y = count_x.bit_length() - 1, count_y.bit_length() - 1
     tables = small_tables(count_x // 4, count_y // 4), reflection_tables(), translation_tiles()
 
     def body(offsets, charges):
         constants = [in_hbm(jnp.asarray(table)) for table in tables]
-        offsets, charges = in_hbm(offsets), in_hbm(charges)
-        own_part, to_low, to_high = moments_call(offsets, charges, constants[0])
-        from_low = shift_ring(to_high, "gy", 1)
-        from_high = shift_ring(to_low, "gy", count_y - 1)
-        own_one = to_low[:ONE_ROWS]
-        others = [shift_ring(own_one, "gy", shift) for shift in range(2, count_y - 1)]
-        row_low, row_high = row_call(count_y, own_part, to_low, from_low, from_high, others)
-        next_low = shift_ring(row_high, "gx", 1)
-        next_high = shift_ring(row_low, "gx", count_x - 1)
-        row_one = row_low[: count_y // 2 * 8]
-        others = [shift_ring(row_one, "gx", shift) for shift in range(2, count_x - 1)]
-        payloads = (row_low, row_high, next_low, next_high)
-        return finish_call(count_x, count_y, payloads, others, constants)
+        block = moments_call(in_hbm(offsets), in_hbm(charges), constants[0])
+        other = swap_bit(block, "gy", 0)
+        pair = block, other
+        exchanged = []
+        for level in range(1, levels_y):
+            last = level == levels_y - 1
+            rows = (ONE_ROWS << (level - 1)) + EDGE_ROWS * (1 if last else 2)
+            sent = pack_call(functools.partial(group_kernel, level, last), rows, pair, "group")
+            pair = sent, swap_bit(sent, "gy", level)
+            exchanged += pair
+        near, targets = near_call(own_kernel, (block, sent), 8, 8, 4_500_000, "near_own", True)
+        ones, even, odd = row_call(levels_y, (block, other, *exchanged, near))
+        other_ones = swap_bit(ones, "gx", 0)
+        from_even = swap_bit(even, "gx", 0)
+        from_odd = swap_odd_even(odd, "gx")
+        near = near_call(beside_y_kernel, (even, odd, targets, near), 8, 8, 2_200_000, "near_y")
+        for bit in range(levels_x - 1):
+            ones = merge_call(bit, ones, other_ones, near)
+            other_ones = swap_bit(ones, "gx", bit + 1)
+            if bit < 2:
+                side = functools.partial(beside_x_kernel, bit)
+                operands = (from_even if bit == 0 else from_odd, targets, near, ones)
+                near = near_call(side, operands, 8, 10, 1_200_000, "near_x")
+        operands = (block, even, odd, from_even, from_odd, ones, other_ones, near)
+        return finish_call(count_x, count_y, operands, constants)
 
     in_specs = (P(None, "gx", "gy", None), P("gx", "gy", None))
     out_specs = P("gx", "gy", None)

time: 39 us -> 33 us (0.85)
  waiting for transfers between devices: 8.88 us -> 1.32 us
  starting transfers between devices: 14.6 us -> 15.6 us
  Pallas kernels: 15.3 us -> 15.9 us
    pallas_call x2 -> x9, Pallas kernels: 1.97 us -> 10.1 us  [the longest x4 8.09 us: near_call(): pl.pallas_call(kernel, out_shape=out_shape, in_specs=[VMEM] * len(operand...]
    ppermute x10 -> x7, waiting for transfers between devices: 8.88 us -> 1.32 us  [the longest x6 1.32 us: swap_bit(): lax.ppermute(value, axis, [(i, i ^ 1 << bit) for i in range(lax.axis_size...]
    pallas_call x1, Pallas kernels: 13.3 us -> 5.79 us  [finish_call(): pl.pallas_call(lambda *refs: finish_kernel(count_x, count_y, refs), out_s...]
    ppermute x10 -> x7, starting transfers between devices: 14.6 us -> 15.6 us  [the longest x6 14.9 us: swap_bit(): lax.ppermute(value, axis, [(i, i ^ 1 << bit) for i in range(lax.axis_size...]
  transfers between devices with their start and end apart: 10 -> 7, of which waited for: 4 -> 3; matrix products, arithmetic and copies ran while one was open for 0% -> 0% of each run, Pallas kernels for 0% -> 25%
where the time goes in v3:
time: 33 us; the launch traced here: 32.9 us
  Pallas kernels  15.9 us (48%)
  starting transfers between devices  15.6 us (47%)
  waiting for transfers between devices  1.32 us (4%)
    ppermute x6, starting transfers between devices, swap_bit(): lax.ppermute(value, axis, [(i, i ^ 1 << bit) for i in range(lax.axis_size...  14.9 us
    pallas_call x4, Pallas kernels, near_call(): pl.pallas_call(kernel, out_shape=out_shape, in_specs=[VMEM] * len(operand...  8.09 us
    pallas_call x1, Pallas kernels, finish_call(): pl.pallas_call(lambda *refs: finish_kernel(count_x, count_y, refs), out_s...  5.79 us
    pallas_call x1, Pallas kernels, moments_call(): pl.pallas_call(moments_kernel, out_shape=jax.ShapeDtypeStruct((OWN_ROWS,...  1.92 us
    ppermute x6, waiting for transfers between devices, swap_bit(): lax.ppermute(value, axis, [(i, i ^ 1 << bit) for i in range(lax.axis_size...  1.32 us
  transfers between devices with their start and end apart: 7, of which 3 were waited for; matrix products, arithmetic and copies ran while one was open for 0% of the time, Pallas kernels for 25%

profile of v3, /device:TPU:0, one launch (start us, length us, event | category | flops | bytes accessed | tf_op | source)
XLA Modules:
  0.0 32.9 jit_solution(1055302488033510687)
XLA Ops:
  0.0 1.9 %moments.1.own_ref.block.refs_0_ = f32[168,128]{1,0:T(8,128)S(1)} custom-call(f32[3,2,2,1024]{3,2,1,0:T(2,128)} %offsets_hbm.1, f32[2,2,1024]{2,1,0:T(2,128)} %charges_hbm.1, bf16[2304,128]{1,0:T(8,128)(2,1)} %constant.6.clone.small_hbm.refs_8_), custom_call_target="tpu_custom_call" | custom-call | flops 10000000 | bytes 300000 | tf_op jit(solution)/shard_map/moments/pallas_call | solution.py:436
  1.9 0.5 %collective-permute-start = (f32[168,128]{1,0:T(8,128)S(1)}, f32[168,128]{1,0:T(8,128)S(1)}, u32[]{:S(2)}, u32[]{:S(2)}) collective-permute-start(f32[168,128]{1,0:T(8,128)S(1)} %moments.1.own_ref.block.refs_0_), channel_id=1, source_target_pairs={{0,1},{1,0},{2,3},{3,2},{4,5},{5,4},{6,7},{7,6},{8,9},{9,8},{10,11... | collective-permute-start | bytes 258056 | tf_op jit(solution)/shard_map/ppermute | solution.py:869
  2.4 0.9 %collective-permute-done.other_ref.refs_1_ = f32[168,128]{1,0:T(8,128)S(1)} collective-permute-done((f32[168,128]{1,0:T(8,128)S(1)}, f32[168,128]{1,0:T(8,128)S(1)}, u32[]{:S(2)}, u32[]{:S(2)}) %collective-permute-start) | collective-permute-done | bytes 86048 | tf_op jit(solution)/shard_map/ppermute | solution.py:869
  3.4 2.9 %collective-permute-start.1 = (f32[104,128]{1,0:T(8,128)S(1)}, f32[104,128]{1,0:T(8,128)S(1)}, u32[]{:S(2)}, u32[]{:S(2)}) collective-permute-start(f32[104,128]{1,0:T(8,128)S(1)} %group.1.after.refs_2_), channel_id=1, source_target_pairs={{0,2},{1,3},{2,0},{3,1},{4,6},{5,7},{6,4},{7,5},{8,10},{9,11},{10,... | collective-permute-start | bytes 159752 | tf_op jit(solution)/shard_map/ppermute | solution.py:869
  6.3 3.1 %near_own.1 = (f32[4,8,128]{2,1,0:T(8,128)S(1)}, bf16[4,8,128,32]{3,2,1,0:T(8,128)(2,1)S(1)}) custom-call(f32[168,128]{1,0:T(8,128)S(1)} %moments.1.own_ref.block.refs_0_, f32[104,128]{1,0:T(8,128)S(1)} %group.1.after.refs_2_), custom_call_target="tpu_custom_call" | custom-call | flops 180000000 | bytes 600000 | tf_op jit(solution)/shard_map/near_own/pallas_call | solution.py:640
  9.5 0.0 collective-permute-done.1.refs_3_
  9.5 1.6 %collective-permute-start.2 = (f32[224,128]{1,0:T(8,128)S(1)}, f32[224,128]{1,0:T(8,128)S(1)}, u32[]{:S(2)}, u32[]{:S(2)}) collective-permute-start(f32[224,128]{1,0:T(8,128)S(1)} %get-tuple-element.11.even_ref.refs_1_), channel_id=1, source_target_pairs={{0,4},{4,0},{8,12},{12,8},{16,20},{20,16},{24,28},{28,24},{1,5},{5... | collective-permute-start | bytes 344072 | tf_op jit(solution)/shard_map/ppermute | solution.py:869
  11.1 0.7 %collective-permute-start.3 = (f32[224,128]{1,0:T(8,128)S(1)}, f32[224,128]{1,0:T(8,128)S(1)}, u32[]{:S(2)}, u32[]{:S(2)}) collective-permute-start(f32[224,128]{1,0:T(8,128)S(1)} %get-tuple-element.12.odd_ref.refs_2_), channel_id=1, source_target_pairs={{0,0},{4,8},{8,4},{12,16},{16,12},{20,24},{24,20},{28,28},{1,1},{5... | collective-permute-start | bytes 344072 | tf_op jit(solution)/shard_map/ppermute | solution.py:875
  11.8 4.3 %collective-permute-start.4 = (f32[16,128]{1,0:T(8,128)S(1)}, f32[16,128]{1,0:T(8,128)S(1)}, u32[]{:S(2)}, u32[]{:S(2)}) collective-permute-start(f32[16,128]{1,0:T(8,128)S(1)} %get-tuple-element.13.own_ref), channel_id=1, source_target_pairs={{0,4},{4,0},{8,12},{12,8},{16,20},{20,16},{24,28},{28,24},{1,5},{5... | collective-permute-start | bytes 24584 | tf_op jit(solution)/shard_map/ppermute | solution.py:869
  16.1 1.7 %near_y.1.after_ref.before = f32[4,8,128]{2,1,0:T(8,128)S(1)} custom-call(f32[224,128]{1,0:T(8,128)S(1)} %get-tuple-element.11.even_ref.refs_1_, f32[224,128]{1,0:T(8,128)S(1)} %get-tuple-element.12.odd_ref.refs_2_, bf16[4,8,128,32]{3,2,1,0:T(8,128)(2,1)S(1)} %get-tuple-element.14.targets, f32[4,8,128]{2,1,0:T(8,128)S(1)} %get-tuple-element.10.refs_4_.before), custom_call_target="tpu_custom_call" | custom-call | flops 88000000 | bytes 600000 | tf_op jit(solution)/shard_map/near_y/pallas_call | solution.py:640
  17.8 0.0 collective-permute-done.4.other_ref
  17.9 2.5 %collective-permute-start.5 = (f32[32,128]{1,0:T(8,128)S(1)}, f32[32,128]{1,0:T(8,128)S(1)}, u32[]{:S(2)}, u32[]{:S(2)}) collective-permute-start(f32[32,128]{1,0:T(8,128)S(1)} %merge.2.after.own_ref), channel_id=1, source_target_pairs={{0,8},{4,12},{8,0},{12,4},{16,24},{20,28},{24,16},{28,20},{1,9},{5... | collective-permute-start | bytes 49160 | tf_op jit(solution)/shard_map/ppermute | solution.py:869
  20.3 0.0 collective-permute-done.2.received.refs_3_
  20.3 1.6 %near_x.2.after_ref.before = f32[4,8,128]{2,1,0:T(8,128)S(1)} custom-call(f32[224,128]{1,0:T(8,128)S(1)} %collective-permute-done.2.received.refs_3_, bf16[4,8,128,32]{3,2,1,0:T(8,128)(2,1)S(1)} %get-tuple-element.14.targets, f32[4,8,128]{2,1,0:T(8,128)S(1)} %near_y.1.after_ref.before, f32[32,128]{1,0:T(8,128)S(1)} %merge.2.after.own_ref), custom_call_target="tpu_custom_call" | custom-call | flops 48000000 | bytes 600000 | tf_op jit(solution)/shard_map/near_x/pallas_call | solution.py:640
  21.9 0.1 collective-permute-done.5.other_ref
  22.1 3.1 %collective-permute-start.6 = (f32[64,128]{1,0:T(8,128)S(1)}, f32[64,128]{1,0:T(8,128)S(1)}, u32[]{:S(2)}, u32[]{:S(2)}) collective-permute-start(f32[64,128]{1,0:T(8,128)S(1)} %merge.3.after.refs_5_), channel_id=1, source_target_pairs={{0,16},{4,20},{8,24},{12,28},{16,0},{20,4},{24,8},{28,12},{1,17},{... | collective-permute-start | bytes 98312 | tf_op jit(solution)/shard_map/ppermute | solution.py:869
  25.2 0.0 collective-permute-done.3.received.refs_4_
  25.2 1.6 %near_x.3.refs_7_ = f32[4,8,128]{2,1,0:T(8,128)S(1)} custom-call(f32[224,128]{1,0:T(8,128)S(1)} %collective-permute-done.3.received.refs_4_, bf16[4,8,128,32]{3,2,1,0:T(8,128)(2,1)S(1)} %get-tuple-element.14.targets, f32[4,8,128]{2,1,0:T(8,128)S(1)} %near_x.2.after_ref.before, f32[64,128]{1,0:T(8,128)S(1)} %merge.3.after.refs_5_), custom_call_target="tpu_custom_call" | custom-call | flops 48000000 | bytes 600000 | tf_op jit(solution)/shard_map/near_x/pallas_call | solution.py:640
  26.8 0.3 collective-permute-done.6.refs_6_
  27.1 5.8 %finish.1 = f32[2,2,1024]{2,1,0:T(2,128)} custom-call(f32[168,128]{1,0:T(8,128)S(1)} %moments.1.own_ref.block.refs_0_, f32[224,128]{1,0:T(8,128)S(1)} %get-tuple-element.11.even_ref.refs_1_, f32[224,128]{1,0:T(8,128)S(1)} %get-tuple-element.12.odd_ref.refs_2_, f32[224,128]{1,0:T(8,128)S(1)} %collective-permute-done.2.received.refs_3_, ...), custom_call_target="tpu_custom_call" | custom-call | tf_op jit(solution)/shard_map/finish/pallas_call | solution.py:853
  (4 shorter events, 0.1 us)
Async XLA Ops:
  1.9 1.4 %collective-permute-start = (f32[168,128]{1,0:T(8,128)S(1)}, f32[168,128]{1,0:T(8,128)S(1)}, u32[]{:S(2)}, u32[]{:S(2)}) collective-permute-start(f32[168,128]{1,0:T(8,128)S(1)} %moments.1.own_ref.block.refs_0_), channel_id=1, source_target_pairs={{0,1},{1,0},{2,3},{3,2},{4,5},{5,4},{6,7},{7,6},{8,9},{9,8},{10,11... | collective-permute-start | bytes 258056 | tf_op jit(solution)/shard_map/ppermute | solution.py:869
  3.4 6.1 %collective-permute-start.1 = (f32[104,128]{1,0:T(8,128)S(1)}, f32[104,128]{1,0:T(8,128)S(1)}, u32[]{:S(2)}, u32[]{:S(2)}) collective-permute-start(f32[104,128]{1,0:T(8,128)S(1)} %group.1.after.refs_2_), channel_id=1, source_target_pairs={{0,2},{1,3},{2,0},{3,1},{4,6},{5,7},{6,4},{7,5},{8,10},{9,11},{10,... | collective-permute-start | bytes 159752 | tf_op jit(solution)/shard_map/ppermute | solution.py:869
  9.5 10.8 %collective-permute-start.2 = (f32[224,128]{1,0:T(8,128)S(1)}, f32[224,128]{1,0:T(8,128)S(1)}, u32[]{:S(2)}, u32[]{:S(2)}) collective-permute-start(f32[224,128]{1,0:T(8,128)S(1)} %get-tuple-element.11.even_ref.refs_1_), channel_id=1, source_target_pairs={{0,4},{4,0},{8,12},{12,8},{16,20},{20,16},{24,28},{28,24},{1,5},{5... | collective-permute-start | bytes 344072 | tf_op jit(solution)/shard_map/ppermute | solution.py:869
  11.1 14.1 %collective-permute-start.3 = (f32[224,128]{1,0:T(8,128)S(1)}, f32[224,128]{1,0:T(8,128)S(1)}, u32[]{:S(2)}, u32[]{:S(2)}) collective-permute-start(f32[224,128]{1,0:T(8,128)S(1)} %get-tuple-element.12.odd_ref.refs_2_), channel_id=1, source_target_pairs={{0,0},{4,8},{8,4},{12,16},{16,12},{20,24},{24,20},{28,28},{1,1},{5... | collective-permute-start | bytes 344072 | tf_op jit(solution)/shard_map/ppermute | solution.py:875
  11.8 6.1 %collective-permute-start.4 = (f32[16,128]{1,0:T(8,128)S(1)}, f32[16,128]{1,0:T(8,128)S(1)}, u32[]{:S(2)}, u32[]{:S(2)}) collective-permute-start(f32[16,128]{1,0:T(8,128)S(1)} %get-tuple-element.13.own_ref), channel_id=1, source_target_pairs={{0,4},{4,0},{8,12},{12,8},{16,20},{20,16},{24,28},{28,24},{1,5},{5... | collective-permute-start | bytes 24584 | tf_op jit(solution)/shard_map/ppermute | solution.py:869
  17.9 4.2 %collective-permute-start.5 = (f32[32,128]{1,0:T(8,128)S(1)}, f32[32,128]{1,0:T(8,128)S(1)}, u32[]{:S(2)}, u32[]{:S(2)}) collective-permute-start(f32[32,128]{1,0:T(8,128)S(1)} %merge.2.after.own_ref), channel_id=1, source_target_pairs={{0,8},{4,12},{8,0},{12,4},{16,24},{20,28},{24,16},{28,20},{1,9},{5... | collective-permute-start | bytes 49160 | tf_op jit(solution)/shard_map/ppermute | solution.py:869
  22.1 5.0 %collective-permute-start.6 = (f32[64,128]{1,0:T(8,128)S(1)}, f32[64,128]{1,0:T(8,128)S(1)}, u32[]{:S(2)}, u32[]{:S(2)}) collective-permute-start(f32[64,128]{1,0:T(8,128)S(1)} %merge.3.after.refs_5_), channel_id=1, source_target_pairs={{0,16},{4,20},{8,24},{12,28},{16,0},{20,4},{24,8},{28,12},{1,17},{... | collective-permute-start | bytes 98312 | tf_op jit(solution)/shard_map/ppermute | solution.py:869

commit v4 on v3

--- a/solution.py
+++ b/solution.py
@@ -75,6 +75,9 @@
         for cz in range(4)
         if not (cx == 0 and cy == 0 and cz <= 1)
     ]
+
+
+TILES_FIRST = 10
 
 
 def translation_tiles():
@@ -226,31 +229,37 @@
     return first, second, rest - second
 
 
-def source_features(coords):
-    rows = []
-    total = None
-    for coord in coords:
-        one, two, three = three_pieces(coord)
-        rows += [one, two, one, two, three, one]
-        total = coord * coord if total is None else total + coord * coord
-    unit = jnp.ones_like(coords[0])
-    return rows + [unit] * 3 + list(three_pieces(total)) + [jnp.zeros_like(unit)] * 8
-
-
-def target_features(coords):
-    rows = []
-    total = None
-    for coord in coords:
-        one, two, three = three_pieces(-2.0 * coord)
-        rows += [one, one, two, two, one, three]
-        total = coord * coord if total is None else total + coord * coord
-    unit = jnp.ones_like(coords[0])
-    return rows + list(three_pieces(total)) + [unit] * 3 + [jnp.zeros_like(unit)] * 8
-
-
-def store_features(rows, wide_ref, group):
-    for row, value in enumerate(rows):
-        wide_ref[group, pl.ds(row, ROWS, stride=FEATURES), :] = value
+PIECES = 12
+
+
+def feature_pieces(coords, scale):
+    total = coords[0] * coords[0] + coords[1] * coords[1] + coords[2] * coords[2]
+    return [piece for value in [scale * coord for coord in coords] + [total] for piece in three_pieces(value)]
+
+
+def pick(row, pieces, choice):
+    value = jnp.broadcast_to(pieces[choice[0]], (8, 128))
+    for piece in sorted(set(choice) - {choice[0]}):
+        mask = None
+        for place, chosen in enumerate(choice):
+            if chosen == piece:
+                mask = row == place if mask is None else mask | (row == place)
+        value = jnp.where(mask, jnp.broadcast_to(pieces[piece], (8, 128)), value)
+    return value
+
+
+def feature_block(read, choice, length_choice):
+    row = sublanes((8, 128))
+    zero, one = jnp.zeros((1, 128), F32), jnp.ones((1, 128), F32)
+    blocks = [
+        pick(row, [read(3 * c), read(3 * c + 1), read(3 * c + 2), zero], choice) for c in range(3)
+    ]
+    blocks.append(pick(row, [read(9), read(10), read(11), one, zero], length_choice))
+    return jnp.concatenate(blocks, 0)
+
+
+SOURCE_CHOICE = (0, 1, 0, 1, 2, 0, 0, 0), (3, 3, 3, 0, 1, 2, 3, 3)
+TARGET_CHOICE = (0, 0, 1, 1, 0, 2, 3, 3), (0, 1, 2, 3, 3, 3, 4, 4)
 
 
 def column(raw, x, y):
@@ -272,14 +281,14 @@
 
     def targets(self, columns):
         for ab, (x, y, z, _) in enumerate(columns):
-            store_features(target_features((x, y, self.in_pair(z))), self.wide_ref, ab)
-        for ab in range(4):
+            pieces = feature_pieces((x, y, self.in_pair(z)), -2.0)
             for j in range(ROWS):
-                block = self.wide_ref[ab, FEATURES * j : FEATURES * (j + 1), :]
+                block = feature_block(lambda k: pieces[k][j : j + 1], *TARGET_CHOICE)
                 self.target_ref[ab, j] = block.T.astype(BF16)
 
     def add_group(self, coords):
-        store_features(source_features(coords), self.wide_ref, self.groups)
+        for k, piece in enumerate(feature_pieces(coords, 1.0)):
+            self.wide_ref[self.groups, k] = piece
         self.groups += 1
         return self.groups - 1
 
@@ -312,10 +321,15 @@
     def run(self, plan, emit):
         eye = sublanes((128, 128)) == lanes((128, 128))
 
-        def pairs(targets, tiles, j, own, total):
-            span = pl.ds(pl.multiple_of(j * FEATURES, FEATURES), FEATURES)
-            block = jnp.concatenate([self.wide_ref[group, span, :] for group, _ in tiles], 1)
-            squared = dot(targets, block.astype(BF16))
+        def source(group, j, built):
+            if group not in built:
+                read = lambda k: self.wide_ref[group, k, pl.ds(j, 1), :]
+                built[group] = feature_block(read, *SOURCE_CHOICE).astype(BF16)
+            return built[group]
+
+        def pairs(targets, tiles, j, own, total, built):
+            block = jnp.concatenate([source(group, j, built) for group, _ in tiles], 1)
+            squared = dot(targets, block)
             for position, (group, charge) in enumerate(tiles):
                 inverse = lax.rsqrt(squared[:, 128 * position : 128 * position + 128])
                 if group == own:
@@ -324,11 +338,12 @@
             return total
 
         def step(j, carry):
+            built = {}
             for ab, mains, below, above, own in plan:
                 targets = self.target_ref[ab, j]
-                total = pairs(targets, mains, j, own, jnp.zeros((128, 128), F32))
-                lower = pairs(targets[:64], below, j, None, total[:64])
-                higher = pairs(targets[64:], above, j, None, total[64:])
+                total = pairs(targets, mains, j, own, jnp.zeros((128, 128), F32), built)
+                lower = pairs(targets[:64], below, j, None, total[:64], built)
+                higher = pairs(targets[64:], above, j, None, total[64:], built)
                 total = jnp.concatenate([lower, higher], 0)
                 emit(ab, j, jnp.sum(total.T, 0, keepdims=True))
             return carry
@@ -366,7 +381,7 @@
 
 def near_scratch(groups, charges):
     return [
-        pltpu.VMEM((groups, ROWS * FEATURES, 128), F32),
+        pltpu.VMEM((groups, PIECES, ROWS, 128), F32),
         pltpu.VMEM((charges, ROWS, 128), F32),
     ]
 
@@ -475,7 +490,7 @@
     return jnp.concatenate(rows, 0)
 
 
-def group_kernel(level, last_level, own_ref, other_ref, out):
+def group_kernel(level, last_level, own_ref, other_ref, after, out):
     index = lax.axis_index("gy")
     ones = ONE_ROWS << (level - 1)
     is_first = bit_of(index, level - 1) == 0
@@ -510,6 +525,8 @@
 
 ROW_LEAF = 3 * LEAF_ROWS
 ROW_PART = 4 * 4 * ROWS
+ROW_ROWS = ROW_LEAF + ROW_PART
+ROW_BOTH = ROW_ROWS + ROW_PART
 
 
 def row_part(c, y):
@@ -517,7 +534,7 @@
 
 
 def row_kernel(levels, block, other, *refs):
-    exchanged, (ones_out, even_out, odd_out) = refs[: 2 * (levels - 1)], refs[-3:]
+    exchanged, (ones_out, out) = refs[: 2 * (levels - 1)], refs[-2:]
     index = lax.axis_index("gy")
     even = lax.rem(lax.axis_index("gx"), 2) == 0
     is_first = bit_of(index, 0) == 0
@@ -536,8 +553,7 @@
             ones_out[...] = in_order(~upper, own[0:ones, :], received[0:ones, :])
     leaf = block[ONE_ROWS : ONE_ROWS + LEAF_ROWS, :]
     for piece, rows in enumerate((low[0:LEAF_ROWS], leaf, high[0:LEAF_ROWS])):
-        for out in (even_out, odd_out):
-            out[LEAF_ROWS * piece : LEAF_ROWS * (piece + 1), :] = rows
+        out[LEAF_ROWS * piece : LEAF_ROWS * (piece + 1), :] = rows
     for c in range(4):
         columns = []
         for x in range(CX):
@@ -545,19 +561,19 @@
             own = [block[part_row(c, x, y) : part_row(c, x, y) + ROWS, :] for y in range(CY)]
             columns.append([low[row : row + ROWS], *own, high[row : row + ROWS]])
         for y in range(4):
-            span = slice(row_part(c, y), row_part(c, y) + ROWS)
-            even_out[span, :] = jnp.where(even, columns[1][y], columns[0][y])
-            odd_out[span, :] = jnp.where(even, columns[0][y], columns[1][y])
+            facing, far = row_part(c, y), row_part(c, y) + ROW_PART
+            out[facing : facing + ROWS, :] = jnp.where(even, columns[1][y], columns[0][y])
+            out[far : far + ROWS, :] = jnp.where(even, columns[0][y], columns[1][y])
 
 
 def row_call(levels, operands):
-    ones = jax.ShapeDtypeStruct((ONE_ROWS << (levels - 1), 128), F32)
-    payload = jax.ShapeDtypeStruct((ROW_LEAF + ROW_PART, 128), F32)
     return pl.pallas_call(
-        lambda *refs: row_kernel(levels, *refs[: 2 * levels], *refs[-3:]),
-        out_shape=(ones, payload, payload),
+        lambda *refs: row_kernel(levels, *refs[: 2 * levels], *refs[-2:]),
+        out_shape=[
+            jax.ShapeDtypeStruct((rows, 128), F32) for rows in (ONE_ROWS << (levels - 1), ROW_BOTH)
+        ],
         in_specs=[VMEM] * len(operands),
-        out_specs=(VMEM,) * 3,
+        out_specs=[VMEM] * 2,
         compiler_params=pltpu.CompilerParams(vmem_limit_bytes=8 * MIB),
         cost_estimate=pl.CostEstimate(flops=100_000, bytes_accessed=600_000, transcendentals=0),
         name="row",
@@ -572,30 +588,99 @@
     return pack_call(kernel, 2 * own.shape[0], (own, other, after), "merge")
 
 
-def own_kernel(block, after, out, targets, wide_ref, charge_ref):
-    near = Near(wide_ref, charge_ref, targets)
+def hand_on_call(halo, after):
+    def kernel(halo_ref, after_ref, out):
+        out[...] = halo_ref[...]
+
+    return pack_call(kernel, halo.shape[0], (halo, after), "hand_on")
+
+
+def relay_call(received, after):
+    def kernel(received_ref, after_ref, out):
+        out[0:ROW_LEAF, :] = received_ref[0:ROW_LEAF, :]
+        out[ROW_LEAF:ROW_ROWS, :] = received_ref[ROW_ROWS:ROW_BOTH, :]
+
+    return pack_call(kernel, ROW_ROWS, (received, after), "relay")
+
+
+def own_kernel(block, targets, features, charges):
+    near = Near(features, charges, targets)
 
     def raw(x, y):
         return lambda c: block[part_row(c, x, y) : part_row(c, x, y) + ROWS, :]
 
     columns = [column(raw(ab // 2, ab % 2), ab // 2 + 1, ab % 2 + 1) for ab in range(4)]
     near.targets(columns)
-    plan = plan_own(near, columns)
-
-    def emit(ab, j, row):
-        out[ab, pl.ds(j, 1), :] = row
-
-    near.run(plan, emit)
-
-
-def beside_y_kernel(even_ref, odd_ref, targets, before, out, wide_ref, charge_ref):
+    return near, plan_own(near, columns)
+
+
+def own_call(block, after, small, tiles):
+    plans = []
+
+    def prepare(block_ref, small, targets, features, charges, small_out, semaphore):
+        copy = pltpu.make_async_copy(small, small_out, semaphore)
+        copy.start()
+        plans.append(own_kernel(block_ref, targets, features, charges)[1])
+        copy.wait()
+
+    def run(targets, features, charges, after_ref, tiles, out, tiles_out, semaphore):
+        copy = pltpu.make_async_copy(tiles, tiles_out, semaphore)
+        copy.start()
+
+        def emit(ab, j, row):
+            out[ab, pl.ds(j, 1), :] = row
+
+        Near(features, charges, targets).run(plans[0], emit)
+        copy.wait()
+
+    prepared = pl.pallas_call(
+        prepare,
+        out_shape=(
+            jax.ShapeDtypeStruct((4, ROWS, 128, FEATURES), BF16),
+            jax.ShapeDtypeStruct((8, PIECES, ROWS, 128), F32),
+            jax.ShapeDtypeStruct((8, ROWS, 128), F32),
+            jax.ShapeDtypeStruct(small.shape, BF16),
+        ),
+        in_specs=[VMEM, HBM],
+        out_specs=(VMEM,) * 4,
+        scratch_shapes=[pltpu.SemaphoreType.DMA],
+        compiler_params=pltpu.CompilerParams(vmem_limit_bytes=8 * MIB),
+        cost_estimate=near_cost(500_000),
+        name="features",
+    )(block, small)
+    near, tiles_near = pl.pallas_call(
+        run,
+        out_shape=(
+            jax.ShapeDtypeStruct(NEAR_SHAPE, F32),
+            jax.ShapeDtypeStruct(tiles.shape, BF16),
+        ),
+        in_specs=[VMEM] * 4 + [HBM],
+        out_specs=(VMEM,) * 2,
+        scratch_shapes=[pltpu.SemaphoreType.DMA],
+        compiler_params=pltpu.CompilerParams(vmem_limit_bytes=8 * MIB),
+        cost_estimate=near_cost(4_500_000),
+        name="near_own",
+    )(*prepared[:3], after(prepared[2]), tiles)
+    return near, prepared[0], prepared[3], tiles_near
+
+
+def beside_y_kernel(
+    row_ref, targets, before, flips, tiles, out, flips_out, tiles_out, wide_ref, charge_ref, semaphores
+):
+    copies = [
+        pltpu.make_async_copy(flips, flips_out, semaphores.at[0]),
+        pltpu.make_async_copy(tiles, tiles_out, semaphores.at[1]),
+    ]
+    for copy in copies:
+        copy.start()
     even = lax.rem(lax.axis_index("gx"), 2) == 0
     near = Near(wide_ref, charge_ref, targets)
 
     def raw(x, y):
         def read(c):
-            span = slice(row_part(c, y), row_part(c, y) + ROWS)
-            return jnp.where(even == (x == 1), even_ref[span, :], odd_ref[span, :])
+            facing, far = row_part(c, y), row_part(c, y) + ROW_PART
+            own = row_ref[facing : facing + ROWS, :], row_ref[far : far + ROWS, :]
+            return jnp.where(even == (x == 1), *own)
 
         return read
 
@@ -607,25 +692,41 @@
         out[ab, pl.ds(j, 1), :] = out[ab, pl.ds(j, 1), :] + row
 
     near.run(plan, emit)
-
-
-def beside_x_kernel(parity, received, targets, before, after, out, wide_ref, charge_ref):
+    for copy in copies:
+        copy.wait()
+
+
+def beside_y_call(row, targets, before, constants):
+    near_shape = jax.ShapeDtypeStruct(NEAR_SHAPE, F32)
+    tables = [jax.ShapeDtypeStruct(constant.shape, BF16) for constant in constants]
+    return pl.pallas_call(
+        beside_y_kernel,
+        out_shape=(near_shape, *tables),
+        in_specs=[VMEM] * 3 + [HBM] * 2,
+        out_specs=(VMEM,) * 3,
+        scratch_shapes=near_scratch(8, 8) + [pltpu.SemaphoreType.DMA((2,))],
+        compiler_params=pltpu.CompilerParams(vmem_limit_bytes=8 * MIB),
+        cost_estimate=near_cost(2_200_000),
+        name="near_y",
+    )(row, targets, before, *constants)
+
+
+def beside_x(parity, received, targets, out, wide_ref, charge_ref):
     index, count = lax.axis_index("gx"), lax.axis_size("gx")
     even = lax.rem(index, 2) == 0
     side = jnp.where(even == (parity == 0), 1, 0)
-    alone = (index == 0) | (index == count - 1) if parity == 1 else None
+    alone = (index == 0) | (index == count - 1)
     near = Near(wide_ref, charge_ref, targets)
 
     def raw(y):
-        def read(c):
+        def coordinate(c):
             value = received[row_part(c, y) : row_part(c, y) + ROWS, :]
-            return jnp.where(alone, 0.0, value) if c == 3 and alone is not None else value
-
-        return read
+            return jnp.where(alone, 0.0, value) if c == 3 and parity == 1 else value
+
+        return coordinate
 
     columns = [column(raw(y), 3.0 * side.astype(F32), y) for y in range(4)]
     plan = plan_beside_x(near, columns, side)
-    out[...] = before[...]
 
     def emit(ab, j, row):
         out[ab, pl.ds(j, 1), :] = out[ab, pl.ds(j, 1), :] + row
@@ -633,15 +734,17 @@
     near.run(plan, emit)
 
 
-def near_call(kernel, operands, groups, charges, pairs, name, with_targets=False):
-    out_shape = jax.ShapeDtypeStruct(NEAR_SHAPE, F32)
-    if with_targets:
-        out_shape = out_shape, jax.ShapeDtypeStruct((4, ROWS, 128, FEATURES), BF16)
+def beside_x_kernel(received, targets, before, after, out, wide_ref, charge_ref):
+    out[...] = before[...]
+    beside_x(0, received, targets, out, wide_ref, charge_ref)
+
+
+def near_call(kernel, operands, groups, charges, pairs, name):
     return pl.pallas_call(
         kernel,
-        out_shape=out_shape,
+        out_shape=jax.ShapeDtypeStruct(NEAR_SHAPE, F32),
         in_specs=[VMEM] * len(operands),
-        out_specs=(VMEM, VMEM) if with_targets else VMEM,
+        out_specs=VMEM,
         scratch_shapes=near_scratch(groups, charges),
         compiler_params=pltpu.CompilerParams(vmem_limit_bytes=12 * MIB),
         cost_estimate=near_cost(pairs),
@@ -649,25 +752,103 @@
     )(*operands)
 
 
-def finish_kernel(count_x, count_y, refs):
-    (own_block, even_ref, odd_ref, from_even, from_odd, own_ones, other_ones, near_rows), refs = refs[:8], refs[8:]
-    constants, refs = refs[:3], refs[3:]
-    out, refs = refs[0], refs[1:]
-    small, flips, tiles, level_one, level_two, boxes, flipped, sums, local, semaphores = refs
+def store_reflected(boxes, flips, flipped, gx, gy):
+    high, low = halves(boxes[...])
+    rows = high.shape[0]
+    mixed = dot(jnp.concatenate([high, low], 0), flips[2 * (gx < 0) + (gy < 0)])
+    for z in range(2):
+        flipped[gx + 1, gy + 1, z, 0] = mixed[:rows, 256 * z : 256 * z + 256]
+        flipped[gx + 1, gy + 1, z, 1] = mixed[rows:, 256 * z : 256 * z + 256]
+
+
+def far_sums(columns, spans, flipped, flips, tiles):
+    odd_row = lax.rem(sublanes((16, 256)), 2) == 1
+    totals = {}
+    for position, (cx, cy, cz) in enumerate(canonical_tiles()):
+        entries = [
+            (gx, gy, dz)
+            for gx in sorted({cx, -cx})
+            for gy in sorted({cy, -cy})
+            for dz in sorted({cz, -cz})
+            if gx in columns
+        ]
+        if not entries:
+            continue
+        pieces = [[], []]
+        for gx, gy, dz in entries:
+            for part in range(2):
+                view = flipped.at[gx + 1, gy + 1, int(dz < 0), part]
+                windows = [view[first + dz : first + dz + size, :] for first, size in spans]
+                block = jnp.concatenate(windows, 0)
+                if abs(dz) == 3:
+                    block = jnp.where(odd_row if dz < 0 else ~odd_row, block, 0.0)
+                pieces[part].append(block.astype(BF16))
+        rows = 16 * len(entries)
+        part = tiles[0] if position < TILES_FIRST else tiles[1]
+        tile = part.at[position % TILES_FIRST]
+        both = dot(jnp.concatenate(pieces[0] + pieces[1], 0), tile[0])
+        result = both[:rows] + both[rows:] + dot(jnp.concatenate(pieces[0], 0), tile[1])
+        for order, (gx, gy, dz) in enumerate(entries):
+            key = (int(gx < 0), int(gy < 0), int(dz < 0))
+            piece = result[16 * order : 16 * order + 16]
+            totals[key] = totals[key] + piece if key in totals else piece
+    far = None
+    for (fx, fy, fz), total in totals.items():
+        if (fx, fy, fz) != (0, 0, 0):
+            high, low = halves(total)
+            table = flips[2 * fx + fy, :, 256 * fz : 256 * fz + 256]
+            both = dot(jnp.concatenate([high, low], 0), table)
+            total = both[:16] + both[16:]
+        far = total if far is None else far + total
+    return far
+
+
+def leaf_far(columns, halos, flips, tiles, boxes, flipped):
+    index, count = lax.axis_index("gx"), lax.axis_size("gx")
+    is_even = lax.rem(index, 2) == 0
+    boxes[...] = jnp.zeros_like(boxes)
+    for gx in columns:
+        for gy in (-1, 0, 1):
+            for h in range(2):
+                row = LEAF_ROWS * (gy + 1) + 16 * h
+                rows = slice(row, row + 16)
+                moments = halos[0][rows, :]
+                if gx != 0:
+                    moments = jnp.where(is_even == (gx == 1), moments, halos[1][rows, :])
+                    inside = index > 0 if gx < 0 else index < count - 1
+                    moments = jnp.where(inside, moments, 0.0)
+                boxes[8:24, 128 * h : 128 * h + 128] = moments
+            store_reflected(boxes, flips, flipped, gx, gy)
+    return far_sums(columns, ((8, 16),), flipped, flips, tiles)
+
+
+LEAF_SCRATCH = [pltpu.VMEM((32, 256), F32), pltpu.VMEM((3, 3, 2, 2, 32, 256), F32)]
+
+
+def far_own_call(row, flips, tiles, after):
+    def kernel(row_ref, flips_ref, tiles_ref, after_ref, out, boxes, flipped):
+        out[...] = leaf_far((0,), (row_ref,), flips_ref, (tiles_ref,), boxes, flipped)
+
+    return pl.pallas_call(
+        kernel,
+        out_shape=jax.ShapeDtypeStruct((LZ, 256), F32),
+        in_specs=[VMEM] * 4,
+        out_specs=VMEM,
+        scratch_shapes=LEAF_SCRATCH,
+        compiler_params=pltpu.CompilerParams(vmem_limit_bytes=8 * MIB),
+        cost_estimate=pl.CostEstimate(flops=500_000_000, bytes_accessed=600_000, transcendentals=0),
+        name="far_own",
+    )(row, flips, tiles, after)
+
+
+def upper_kernel(count_x, count_y, refs):
+    own_ones, other_ones, small, flips, *tiles, _, out = refs[:8]
+    refs = refs[8:]
+    level_one, level_two, boxes, flipped, sums, local = refs
 
     index_x, index_y = lax.axis_index("gx"), lax.axis_index("gy")
-    is_even = lax.rem(index_x, 2) == 0
     pairs_y = count_y // 2
-    has_low = index_x > 0
-    has_high = index_x < count_x - 1
-    fetches = [
-        pltpu.make_async_copy(constant, place, semaphores.at[k])
-        for k, (constant, place) in enumerate(zip(constants, (small, flips, tiles)))
-    ]
-    for fetch in fetches:
-        fetch.start()
-
-    fetches[0].wait()
+
     level_one[...] = jnp.zeros_like(level_one)
     level_two[...] = jnp.zeros_like(level_two)
     half_x = count_x // 2
@@ -723,68 +904,15 @@
         table = [small[pl.ds(pl.multiple_of(row + 128 * k, 128), 128), :] for k in range(2)]
         top_far = top_far + dot_three(jnp.broadcast_to(third, (16, 128)), table[0], table[1])
 
-    fetches[1].wait()
     boxes[...] = jnp.zeros_like(boxes)
     for gx in (-1, 0, 1):
         for gy in (-1, 0, 1):
             for h in range(2):
-                rows = slice(LEAF_ROWS * (gy + 1) + 16 * h, LEAF_ROWS * (gy + 1) + 16 * h + 16)
-                if gx == 0:
-                    moments = even_ref[rows, :]
-                else:
-                    moments = jnp.where(is_even == (gx == 1), from_even[rows, :], from_odd[rows, :])
-                    moments = jnp.where(has_low if gx < 0 else has_high, moments, 0.0)
-                span = slice(128 * h, 128 * h + 128)
-                boxes[8:24, span] = moments
-                boxes[32:40, span] = level_one[
-                    2 * (index_x // 2 + gx) + h + 2, index_y // 2 + gy + 1
-                ]
-            boxes[48:56, :] = second_group(quarter_x + gx, quarter_y + gy)
-            high, low = halves(boxes[...])
-            table = flips[2 * (gx < 0) + (gy < 0)]
-            mixed = dot(jnp.concatenate([high, low], 0), table)
-            group = 3 * (gx + 1) + gy + 1
-            for z in range(2):
-                flipped[group, z, 0] = mixed[:64, 256 * z : 256 * z + 256]
-                flipped[group, z, 1] = mixed[64:, 256 * z : 256 * z + 256]
-
-    fetches[2].wait()
-    odd_row = lax.rem(sublanes((32, 256)), 2) == 1
-    totals = {}
-    for position, (cx, cy, cz) in enumerate(canonical_tiles()):
-        entries = [
-            (gx, gy, dz)
-            for gx in sorted({cx, -cx})
-            for gy in sorted({cy, -cy})
-            for dz in sorted({cz, -cz})
-        ]
-        pieces = [[], []]
-        for gx, gy, dz in entries:
-            group = 3 * (gx + 1) + gy + 1
-            for part in range(2):
-                view = flipped.at[group, int(dz < 0), part]
-                block = jnp.concatenate(
-                    [view[8 + dz : 24 + dz, :], view[32 + dz : 40 + dz, :], view[48 + dz : 56 + dz, :]],
-                    0,
-                )
-                if abs(dz) == 3:
-                    block = jnp.where(odd_row if dz < 0 else ~odd_row, block, 0.0)
-                pieces[part].append(block.astype(BF16))
-        rows = 32 * len(entries)
-        both = dot(jnp.concatenate(pieces[0] + pieces[1], 0), tiles[position, 0])
-        result = both[:rows] + both[rows:] + dot(jnp.concatenate(pieces[0], 0), tiles[position, 1])
-        for order, (gx, gy, dz) in enumerate(entries):
-            key = (int(gx < 0), int(gy < 0), int(dz < 0))
-            piece = result[32 * order : 32 * order + 32]
-            totals[key] = totals[key] + piece if key in totals else piece
-    far = None
-    for (fx, fy, fz), total in totals.items():
-        if (fx, fy, fz) != (0, 0, 0):
-            high, low = halves(total)
-            table = flips[2 * fx + fy, :, 256 * fz : 256 * fz + 256]
-            both = dot(jnp.concatenate([high, low], 0), table)
-            total = both[:32] + both[32:]
-        far = total if far is None else far + total
+                step = 2 * (index_x // 2 + gx) + h + 2
+                boxes[8:16, 128 * h : 128 * h + 128] = level_one[step, index_y // 2 + gy + 1]
+            boxes[24:32, :] = second_group(quarter_x + gx, quarter_y + gy)
+            store_reflected(boxes, flips, flipped, gx, gy)
+    far = far_sums((-1, 0, 1), ((8, 8), (24, 8)), flipped, flips, tiles)
 
     def select(block, hx, hy):
         tile = jnp.where(hx == 1, block[:, 128:256], block[:, 0:128])
@@ -810,13 +938,43 @@
     children_far = refine(top_local)
     half_index_x, half_index_y = index_x // 2, index_y // 2
     second = select(children_far[0:8], lax.rem(half_index_x, 2), lax.rem(half_index_y, 2))
-    second = second + 0.25 * select(far[24:32], lax.rem(half_index_x, 2), lax.rem(half_index_y, 2))
+    second = second + 0.25 * select(far[8:16], lax.rem(half_index_x, 2), lax.rem(half_index_y, 2))
     zeros = jnp.zeros((8, 128), F32)
     children_far = refine(jnp.concatenate([second, zeros], 0))
     first = select(children_far[0:8], lax.rem(index_x, 2), lax.rem(index_y, 2))
-    first = first + 0.5 * select(far[16:24], lax.rem(index_x, 2), lax.rem(index_y, 2))
-    leaf = refine(jnp.concatenate([first, zeros], 0))[0:16] + far[0:16]
-
+    first = first + 0.5 * select(far[0:8], lax.rem(index_x, 2), lax.rem(index_y, 2))
+    out[...] = refine(jnp.concatenate([first, zeros], 0))[0:16]
+
+
+def upper_call(count_x, count_y, operands):
+    half_x, half_y = count_x // 2, count_y // 2
+    scratch = [
+        pltpu.VMEM((count_x + 4, half_y + 2, 8, 128), F32),
+        pltpu.VMEM((half_x + 4, half_y + 4, 8, 128), F32),
+        pltpu.VMEM((40, 256), F32),
+        pltpu.VMEM((3, 3, 2, 2, 40, 256), F32),
+        pltpu.VMEM((max(16, half_x * half_y * 8), 128), F32),
+        pltpu.VMEM((2, 32, 128), F32),
+    ]
+    return pl.pallas_call(
+        lambda *refs: upper_kernel(count_x, count_y, refs),
+        out_shape=jax.ShapeDtypeStruct((LZ, 256), F32),
+        in_specs=[VMEM] * len(operands),
+        out_specs=VMEM,
+        scratch_shapes=scratch,
+        compiler_params=pltpu.CompilerParams(vmem_limit_bytes=8 * MIB),
+        cost_estimate=pl.CostEstimate(flops=900_000_000, bytes_accessed=600_000, transcendentals=0),
+        name="upper",
+    )(*operands)
+
+
+def last_kernel(
+    own_block, before, local, far_own, partner, beyond, targets, flips, one, two, out, near_rows, *scratch
+):
+    near_rows[...] = before[...]
+    beside_x(1, beyond, targets, near_rows, *scratch[:2])
+    far_beside = leaf_far((-1, 1), (partner, beyond), flips, (one, two), *scratch[2:])
+    leaf = local[...] + far_own[...] + far_beside
     one, two = halves(leaf)
     turned = jnp.concatenate([one.astype(F32), two.astype(F32)], 0).T.astype(BF16)
     table = leaf_segments(2 * LZ)
@@ -838,27 +996,16 @@
                 out[x, y : y + 1, span] = value
 
 
-def finish_call(count_x, count_y, operands, constants):
-    half_x, half_y = count_x // 2, count_y // 2
-    scratch = [
-        *[pltpu.VMEM(constant.shape, BF16) for constant in constants],
-        pltpu.VMEM((count_x + 4, half_y + 2, 8, 128), F32),
-        pltpu.VMEM((half_x + 4, half_y + 4, 8, 128), F32),
-        pltpu.VMEM((64, 256), F32),
-        pltpu.VMEM((9, 2, 2, 64, 256), F32),
-        pltpu.VMEM((max(16, half_x * half_y * 8), 128), F32),
-        pltpu.VMEM((2, 32, 128), F32),
-        pltpu.SemaphoreType.DMA((3,)),
-    ]
+def last_call(operands):
     return pl.pallas_call(
-        lambda *refs: finish_kernel(count_x, count_y, refs),
+        last_kernel,
         out_shape=jax.ShapeDtypeStruct((CX, CY, LZ * 64), F32),
-        in_specs=[VMEM] * len(operands) + [HBM] * 3,
+        in_specs=[VMEM] * len(operands),
         out_specs=VMEM,
-        scratch_shapes=scratch,
-        compiler_params=pltpu.CompilerParams(vmem_limit_bytes=24 * MIB),
-        name="finish",
-    )(*operands, *constants)
+        scratch_shapes=[pltpu.VMEM(NEAR_SHAPE, F32), *near_scratch(8, 10), *LEAF_SCRATCH],
+        compiler_params=pltpu.CompilerParams(vmem_limit_bytes=12 * MIB),
+        name="last",
+    )(*operands)
 
 
 def in_hbm(value):
@@ -869,44 +1016,53 @@
     return lax.ppermute(value, axis, [(i, i ^ (1 << bit)) for i in range(lax.axis_size(axis))])
 
 
-def swap_odd_even(value, axis):
+def relay_ring(value, axis):
     count = lax.axis_size(axis)
-    partner = [i if i in (0, count - 1) else (i + 1 if i % 2 == 1 else i - 1) for i in range(count)]
-    return lax.ppermute(value, axis, list(enumerate(partner)))
+    steps = {i: i + 2 if i % 2 == 0 else i - 2 for i in range(count)}
+    steps[count - 2], steps[1] = count - 1, 0
+    return lax.ppermute(value, axis, list(steps.items()))
 
 
 def solution(mesh):
     count_x, count_y = mesh.shape["gx"], mesh.shape["gy"]
     levels_x, levels_y = count_x.bit_length() - 1, count_y.bit_length() - 1
-    tables = small_tables(count_x // 4, count_y // 4), reflection_tables(), translation_tiles()
+    tiles = translation_tiles()
+    small = small_tables(count_x // 4, count_y // 4)
+    tables = small, reflection_tables(), tiles[:TILES_FIRST], tiles[TILES_FIRST:]
 
     def body(offsets, charges):
-        constants = [in_hbm(jnp.asarray(table)) for table in tables]
-        block = moments_call(in_hbm(offsets), in_hbm(charges), constants[0])
+        small, flips, *tiles = [in_hbm(jnp.asarray(table)) for table in tables]
+        block = moments_call(in_hbm(offsets), in_hbm(charges), small)
         other = swap_bit(block, "gy", 0)
-        pair = block, other
         exchanged = []
-        for level in range(1, levels_y):
-            last = level == levels_y - 1
-            rows = (ONE_ROWS << (level - 1)) + EDGE_ROWS * (1 if last else 2)
-            sent = pack_call(functools.partial(group_kernel, level, last), rows, pair, "group")
-            pair = sent, swap_bit(sent, "gy", level)
-            exchanged += pair
-        near, targets = near_call(own_kernel, (block, sent), 8, 8, 4_500_000, "near_own", True)
-        ones, even, odd = row_call(levels_y, (block, other, *exchanged, near))
+
+        def exchange_y(after):
+            pair = block, other
+            for level in range(1, levels_y):
+                last = level == levels_y - 1
+                rows = (ONE_ROWS << (level - 1)) + EDGE_ROWS * (1 if last else 2)
+                kernel = functools.partial(group_kernel, level, last)
+                sent = pack_call(kernel, rows, (*pair, after), "group")
+                pair = sent, swap_bit(sent, "gy", level)
+                exchanged.extend(pair)
+            return exchanged[0]
+
+        near, targets, small, first_tiles = own_call(block, exchange_y, small, tiles[0])
+        ones, row = row_call(levels_y, (block, other, *exchanged, near))
         other_ones = swap_bit(ones, "gx", 0)
-        from_even = swap_bit(even, "gx", 0)
-        from_odd = swap_odd_even(odd, "gx")
-        near = near_call(beside_y_kernel, (even, odd, targets, near), 8, 8, 2_200_000, "near_y")
-        for bit in range(levels_x - 1):
-            ones = merge_call(bit, ones, other_ones, near)
+        near, flips, other_tiles = beside_y_call(row, targets, near, (flips, tiles[1]))
+        tables_near = flips, first_tiles, other_tiles
+        ones = merge_call(0, ones, other_ones, near)
+        other_ones = swap_bit(ones, "gx", 1)
+        partner = swap_bit(hand_on_call(row, ones), "gx", 0)
+        far_own = far_own_call(row, flips, first_tiles, ones)
+        for bit in range(1, levels_x - 1):
+            ones = merge_call(bit, ones, other_ones, far_own)
             other_ones = swap_bit(ones, "gx", bit + 1)
-            if bit < 2:
-                side = functools.partial(beside_x_kernel, bit)
-                operands = (from_even if bit == 0 else from_odd, targets, near, ones)
-                near = near_call(side, operands, 8, 10, 1_200_000, "near_x")
-        operands = (block, even, odd, from_even, from_odd, ones, other_ones, near)
-        return finish_call(count_x, count_y, operands, constants)
+        beyond = relay_ring(relay_call(partner, ones), "gx")
+        near = near_call(beside_x_kernel, (partner, targets, near, ones), 8, 10, 1_200_000, "near_x")
+        local = upper_call(count_x, count_y, (ones, other_ones, small, *tables_near, near))
+        return last_call((block, near, local, far_own, partner, beyond, targets, *tables_near))
 
     in_specs = (P(None, "gx", "gy", None), P("gx", "gy", None))
     out_specs = P("gx", "gy", None)

time: 33 us -> 30 us (0.909)
  starting transfers between devices: 15.6 us -> 12.9 us
  Pallas kernels: 15.9 us -> 15 us
  waiting for transfers between devices: 1.32 us -> 1.87 us
    ppermute x6, starting transfers between devices: 14.9 us -> 11.2 us  [swap_bit(): lax.ppermute(value, axis, [(i, i ^ 1 << bit) for i in range(lax.axis_size...]
    ppermute x1, starting transfers between devices: 0.66 us -> 1.63 us  [relay_ring(): return lax.ppermute(value, axis, list(steps.items()))]
    pallas_call x5 -> x7, Pallas kernels: 13.9 us -> 13 us  [the longest x1 3.43 us: last_call(): pl.pallas_call(last_kernel, out_shape=jax.ShapeDtypeStruct((CX, CY, LZ *...]
    ppermute x6, waiting for transfers between devices: 1.32 us -> 1.87 us  [swap_bit(): lax.ppermute(value, axis, [(i, i ^ 1 << bit) for i in range(lax.axis_size...]
  transfers between devices with their start and end apart: 7 -> 7, of which waited for: 3 -> 3; matrix products, arithmetic and copies ran while one was open for 0% -> 0% of each run, Pallas kernels for 25% -> 32%
where the time goes in v4:
time: 30 us; the launch traced here: 29.8 us
  Pallas kernels  15 us (50%)
  starting transfers between devices  12.9 us (43%)
  waiting for transfers between devices  1.87 us (6%)
    ppermute x6, starting transfers between devices, swap_bit(): lax.ppermute(value, axis, [(i, i ^ 1 << bit) for i in range(lax.axis_size...  11.2 us
    pallas_call x1, Pallas kernels, last_call(): pl.pallas_call(last_kernel, out_shape=jax.ShapeDtypeStruct((CX, CY, LZ *...  3.43 us
    pallas_call x1, Pallas kernels, upper_call(): pl.pallas_call(lambda *refs: upper_kernel(count_x, count_y, refs), out_sh...  3.03 us
    pallas_call x1, Pallas kernels, own_call(): pl.pallas_call(run, out_shape=(jax.ShapeDtypeStruct(NEAR_SHAPE, F32), jax...  2.02 us
    pallas_call x1, Pallas kernels, moments_call(): pl.pallas_call(moments_kernel, out_shape=jax.ShapeDtypeStruct((OWN_ROWS,...  1.92 us
    ppermute x6, waiting for transfers between devices, swap_bit(): lax.ppermute(value, axis, [(i, i ^ 1 << bit) for i in range(lax.axis_size...  1.87 us
    ppermute x1, starting transfers between devices, relay_ring(): return lax.ppermute(value, axis, list(steps.items()))  1.63 us
    pallas_call x1, Pallas kernels, beside_y_call(): pl.pallas_call(beside_y_kernel, out_shape=(near_shape, *tables), in_specs...  1.56 us
  transfers between devices with their start and end apart: 7, of which 3 were waited for; matrix products, arithmetic and copies ran while one was open for 0% of the time, Pallas kernels for 32%

profile of v4, /device:TPU:0, one launch (start us, length us, event | category | flops | bytes accessed | tf_op | source)
XLA Modules:
  0.0 29.8 jit_solution(13102385977624263059)
XLA Ops:
  0.0 1.9 %moments.1.block_ref.own_ref.refs_0_.own_block = f32[168,128]{1,0:T(8,128)S(1)} custom-call(f32[3,2,2,1024]{3,2,1,0:T(2,128)} %offsets_hbm.1, f32[2,2,1024]{2,1,0:T(2,128)} %charges_hbm.1, bf16[2304,128]{1,0:T(8,128)(2,1)} %constant.8.clone.small_hbm.small), custom_call_target="tpu_custom_call" | custom-call | flops 10000000 | bytes 300000 | tf_op jit(solution)/shard_map/moments/pallas_call | solution.py:451
  1.9 0.5 %collective-permute-start = (f32[168,128]{1,0:T(8,128)S(1)}, f32[168,128]{1,0:T(8,128)S(1)}, u32[]{:S(2)}, u32[]{:S(2)}) collective-permute-start(f32[168,128]{1,0:T(8,128)S(1)} %moments.1.block_ref.own_ref.refs_0_.own_block), channel_id=1, source_target_pairs={{0,1},{1,0},{2,3},{3,2},{4,5},{5,4},{6,7},{7,6},{8,9},{9,8},{10,11... | collective-permute-start | bytes 258056 | tf_op jit(solution)/shard_map/ppermute | solution.py:1016
  2.4 1.1 %features.1 = (bf16[4,8,128,32]{3,2,1,0:T(8,128)(2,1)S(1)}, f32[8,12,8,128]{3,2,1,0:T(8,128)S(1)}, f32[8,8,128]{2,1,0:T(8,128)S(1)}, bf16[2304,128]{1,0:T(8,128)(2,1)S(1)}) custom-call(f32[168,128]{1,0:T(8,128)S(1)} %moments.1.block_ref.own_ref.refs_0_.own_block, bf16[2304,128]{1,0:T(8,128)(2,1)} %constant.8.clone.small_hbm.small), custom_call_target="tpu_custom_call" | custom-call | flops 20000000 | bytes 600000 | tf_op jit(solution)/shard_map/features/pallas_call | solution.py:636
  3.5 0.0 collective-permute-done.other_ref.refs_1_
  3.6 2.7 %collective-permute-start.1 = (f32[104,128]{1,0:T(8,128)S(1)}, f32[104,128]{1,0:T(8,128)S(1)}, u32[]{:S(2)}, u32[]{:S(2)}) collective-permute-start(f32[104,128]{1,0:T(8,128)S(1)} %group.1.after_ref.refs_2_), channel_id=1, source_target_pairs={{0,2},{1,3},{2,0},{3,1},{4,6},{5,7},{6,4},{7,5},{8,10},{9,11},{10,... | collective-permute-start | bytes 159752 | tf_op jit(solution)/shard_map/ppermute | solution.py:1016
  6.3 2.0 %near_own.1 = (f32[4,8,128]{2,1,0:T(8,128)S(1)}, bf16[10,2,256,256]{3,2,1,0:T(8,128)(2,1)S(1)}) custom-call(bf16[4,8,128,32]{3,2,1,0:T(8,128)(2,1)S(1)} %get-tuple-element.17.targets, f32[8,12,8,128]{3,2,1,0:T(8,128)S(1)} %get-tuple-element.18.features, f32[8,8,128]{2,1,0:T(8,128)S(1)} %get-tuple-element.16.after.charges, ...), custom_call_target="tpu_custom_call" | custom-call | flops 180000000 | bytes 600000 | tf_op jit(solution)/shard_map/near_own/pallas_call | solution.py:651
  8.3 0.3 collective-permute-done.1.refs_3_
  8.7 1.9 %collective-permute-start.2 = (f32[16,128]{1,0:T(8,128)S(1)}, f32[16,128]{1,0:T(8,128)S(1)}, u32[]{:S(2)}, u32[]{:S(2)}) collective-permute-start(f32[16,128]{1,0:T(8,128)S(1)} %get-tuple-element.21.own_ref), channel_id=1, source_target_pairs={{0,4},{4,0},{8,12},{12,8},{16,20},{20,16},{24,28},{28,24},{1,5},{5... | collective-permute-start | bytes 24584 | tf_op jit(solution)/shard_map/ppermute | solution.py:1016
  10.6 1.6 %near_y.1 = (f32[4,8,128]{2,1,0:T(8,128)S(1)}, bf16[4,256,512]{2,1,0:T(8,128)(2,1)S(1)}, bf16[4,2,256,256]{3,2,1,0:T(8,128)(2,1)S(1)}) custom-call(f32[352,128]{1,0:T(8,128)S(1)} %get-tuple-element.20.row_ref.halo_ref, bf16[4,8,128,32]{3,2,1,0:T(8,128)(2,1)S(1)} %get-tuple-element.17.targets, f32[4,8,128]{2,1,0:T(8,128)S(1)} %get-tuple-element.19.refs_4_.before, ...), custom_call_target="tpu_custom_call" | custom-call | flops 88000000 | bytes 600000 | tf_op jit(solution)/shard_map/near_y/pallas_call | solution.py:702
  12.1 0.2 collective-permute-done.2.other_ref
  12.4 1.9 %collective-permute-start.3 = (f32[352,128]{1,0:T(8,128)S(1)}, f32[352,128]{1,0:T(8,128)S(1)}, u32[]{:S(2)}, u32[]{:S(2)}) collective-permute-start(f32[352,128]{1,0:T(8,128)S(1)} %hand_on.1), channel_id=1, source_target_pairs={{0,4},{4,0},{8,12},{12,8},{16,20},{20,16},{24,28},{28,24},{1,5},{5... | collective-permute-start | bytes 540680 | tf_op jit(solution)/shard_map/ppermute | solution.py:1016
  14.3 1.6 %collective-permute-start.4 = (f32[32,128]{1,0:T(8,128)S(1)}, f32[32,128]{1,0:T(8,128)S(1)}, u32[]{:S(2)}, u32[]{:S(2)}) collective-permute-start(f32[32,128]{1,0:T(8,128)S(1)} %merge.2.after_ref.own_ref), channel_id=1, source_target_pairs={{0,8},{4,12},{8,0},{12,4},{16,24},{20,28},{24,16},{28,20},{1,9},{5... | collective-permute-start | bytes 49160 | tf_op jit(solution)/shard_map/ppermute | solution.py:1016
  15.9 0.8 %far_own.1.after_ref = f32[16,256]{1,0:T(8,128)S(1)} custom-call(f32[352,128]{1,0:T(8,128)S(1)} %get-tuple-element.20.row_ref.halo_ref, bf16[4,256,512]{2,1,0:T(8,128)(2,1)S(1)} %get-tuple-element.23.flips_ref.refs_3_.flips, bf16[10,2,256,256]{3,2,1,0:T(8,128)(2,1)S(1)} %get-tuple-element.24.tiles_ref.refs_4_.one, f32[32,128]{1,0:T(8,128)S(1)} %merge.2.after_ref.own_ref), custom_call_target="tpu_custom_call" | custom-call | flops 500000000 | bytes 600000 | tf_op jit(solution)/shard_map/far_own/pallas_call | solution.py:832
  16.7 1.3 %collective-permute-done.4.other_ref = f32[32,128]{1,0:T(8,128)S(1)} collective-permute-done((f32[32,128]{1,0:T(8,128)S(1)}, f32[32,128]{1,0:T(8,128)S(1)}, u32[]{:S(2)}, u32[]{:S(2)}) %collective-permute-start.4) | collective-permute-done | bytes 16416 | tf_op jit(solution)/shard_map/ppermute | solution.py:1016
  18.1 2.6 %collective-permute-start.5 = (f32[64,128]{1,0:T(8,128)S(1)}, f32[64,128]{1,0:T(8,128)S(1)}, u32[]{:S(2)}, u32[]{:S(2)}) collective-permute-start(f32[64,128]{1,0:T(8,128)S(1)} %merge.3.after.refs_0_.after_ref), channel_id=1, source_target_pairs={{0,16},{4,20},{8,24},{12,28},{16,0},{20,4},{24,8},{28,12},{1,17},{... | collective-permute-start | bytes 98312 | tf_op jit(solution)/shard_map/ppermute | solution.py:1016
  20.6 0.0 collective-permute-done.3.received.received_ref.partner
  20.7 1.6 %collective-permute-start.6 = (f32[224,128]{1,0:T(8,128)S(1)}, f32[224,128]{1,0:T(8,128)S(1)}, u32[]{:S(2)}, u32[]{:S(2)}) collective-permute-start(f32[224,128]{1,0:T(8,128)S(1)} %relay.1), channel_id=1, source_target_pairs={{0,8},{4,0},{8,16},{12,4},{16,24},{20,12},{24,28},{28,20},{1,9},{5... | collective-permute-start | bytes 344072 | tf_op jit(solution)/shard_map/ppermute | solution.py:1023
  22.3 1.1 %near_x.1.refs_6_.before = f32[4,8,128]{2,1,0:T(8,128)S(1)} custom-call(f32[352,128]{1,0:T(8,128)S(1)} %collective-permute-done.3.received.received_ref.partner, bf16[4,8,128,32]{3,2,1,0:T(8,128)(2,1)S(1)} %get-tuple-element.17.targets, f32[4,8,128]{2,1,0:T(8,128)S(1)} %get-tuple-element.22.after_ref.before, f32[64,128]{1,0:T(8,128)S(1)} %merge.3.after.refs_0_.after_ref), custom_call_target="tpu_custom_call" | custom-call | flops 48000000 | bytes 600000 | tf_op jit(solution)/shard_map/near_x/pallas_call | solution.py:743
  23.4 0.0 collective-permute-done.5.refs_1_
  23.4 3.0 %upper.1.local = f32[16,256]{1,0:T(8,128)S(1)} custom-call(f32[64,128]{1,0:T(8,128)S(1)} %merge.3.after.refs_0_.after_ref, f32[64,128]{1,0:T(8,128)S(1)} %collective-permute-done.5.refs_1_, bf16[2304,128]{1,0:T(8,128)(2,1)S(1)} %get-tuple-element.25.refs_2_, bf16[4,256,512]{2,1,0:T(8,128)(2,1)S(1)} %get-tuple-element.23.flips_ref.refs_3_.flips, ...), custom_call_target="tpu_custom_call" | custom-call | flops 900000000 | bytes 600000 | tf_op jit(solution)/shard_map/upper/pallas_call | solution.py:959
  26.4 0.0 collective-permute-done.6.beyond
  26.4 3.4 %last.1 = f32[2,2,1024]{2,1,0:T(2,128)} custom-call(f32[168,128]{1,0:T(8,128)S(1)} %moments.1.block_ref.own_ref.refs_0_.own_block, f32[4,8,128]{2,1,0:T(8,128)S(1)} %near_x.1.refs_6_.before, f32[16,256]{1,0:T(8,128)S(1)} %upper.1.local, f32[16,256]{1,0:T(8,128)S(1)} %far_own.1.after_ref, f32[352,128]{1,0:T(8,128)S(1)} %collective-permute-done.3.received.received_ref.partner, ...), custom_call_target="tpu_custom_call" | custom-call | tf_op jit(solution)/shard_map/last/pallas_call | solution.py:1000
  (6 shorter events, 0.1 us)
Async XLA Ops:
  1.9 1.6 %collective-permute-start = (f32[168,128]{1,0:T(8,128)S(1)}, f32[168,128]{1,0:T(8,128)S(1)}, u32[]{:S(2)}, u32[]{:S(2)}) collective-permute-start(f32[168,128]{1,0:T(8,128)S(1)} %moments.1.block_ref.own_ref.refs_0_.own_block), channel_id=1, source_target_pairs={{0,1},{1,0},{2,3},{3,2},{4,5},{5,4},{6,7},{7,6},{8,9},{9,8},{10,11... | collective-permute-start | bytes 258056 | tf_op jit(solution)/shard_map/ppermute | solution.py:1016
  3.6 5.1 %collective-permute-start.1 = (f32[104,128]{1,0:T(8,128)S(1)}, f32[104,128]{1,0:T(8,128)S(1)}, u32[]{:S(2)}, u32[]{:S(2)}) collective-permute-start(f32[104,128]{1,0:T(8,128)S(1)} %group.1.after_ref.refs_2_), channel_id=1, source_target_pairs={{0,2},{1,3},{2,0},{3,1},{4,6},{5,7},{6,4},{7,5},{8,10},{9,11},{10,... | collective-permute-start | bytes 159752 | tf_op jit(solution)/shard_map/ppermute | solution.py:1016
  8.7 3.7 %collective-permute-start.2 = (f32[16,128]{1,0:T(8,128)S(1)}, f32[16,128]{1,0:T(8,128)S(1)}, u32[]{:S(2)}, u32[]{:S(2)}) collective-permute-start(f32[16,128]{1,0:T(8,128)S(1)} %get-tuple-element.21.own_ref), channel_id=1, source_target_pairs={{0,4},{4,0},{8,12},{12,8},{16,20},{20,16},{24,28},{28,24},{1,5},{5... | collective-permute-start | bytes 24584 | tf_op jit(solution)/shard_map/ppermute | solution.py:1016
  12.4 8.2 %collective-permute-start.3 = (f32[352,128]{1,0:T(8,128)S(1)}, f32[352,128]{1,0:T(8,128)S(1)}, u32[]{:S(2)}, u32[]{:S(2)}) collective-permute-start(f32[352,128]{1,0:T(8,128)S(1)} %hand_on.1), channel_id=1, source_target_pairs={{0,4},{4,0},{8,12},{12,8},{16,20},{20,16},{24,28},{28,24},{1,5},{5... | collective-permute-start | bytes 540680 | tf_op jit(solution)/shard_map/ppermute | solution.py:1016
  14.3 3.7 %collective-permute-start.4 = (f32[32,128]{1,0:T(8,128)S(1)}, f32[32,128]{1,0:T(8,128)S(1)}, u32[]{:S(2)}, u32[]{:S(2)}) collective-permute-start(f32[32,128]{1,0:T(8,128)S(1)} %merge.2.after_ref.own_ref), channel_id=1, source_target_pairs={{0,8},{4,12},{8,0},{12,4},{16,24},{20,28},{24,16},{28,20},{1,9},{5... | collective-permute-start | bytes 49160 | tf_op jit(solution)/shard_map/ppermute | solution.py:1016
  18.1 5.3 %collective-permute-start.5 = (f32[64,128]{1,0:T(8,128)S(1)}, f32[64,128]{1,0:T(8,128)S(1)}, u32[]{:S(2)}, u32[]{:S(2)}) collective-permute-start(f32[64,128]{1,0:T(8,128)S(1)} %merge.3.after.refs_0_.after_ref), channel_id=1, source_target_pairs={{0,16},{4,20},{8,24},{12,28},{16,0},{20,4},{24,8},{28,12},{1,17},{... | collective-permute-start | bytes 98312 | tf_op jit(solution)/shard_map/ppermute | solution.py:1016
  20.7 5.8 %collective-permute-start.6 = (f32[224,128]{1,0:T(8,128)S(1)}, f32[224,128]{1,0:T(8,128)S(1)}, u32[]{:S(2)}, u32[]{:S(2)}) collective-permute-start(f32[224,128]{1,0:T(8,128)S(1)} %relay.1), channel_id=1, source_target_pairs={{0,8},{4,0},{8,16},{12,4},{16,24},{20,12},{24,28},{28,20},{1,9},{5... | collective-permute-start | bytes 344072 | tf_op jit(solution)/shard_map/ppermute | solution.py:1023

commit v5 on v4

--- a/solution.py
+++ b/solution.py
@@ -534,7 +534,7 @@
 
 
 def row_kernel(levels, block, other, *refs):
-    exchanged, (ones_out, out) = refs[: 2 * (levels - 1)], refs[-2:]
+    exchanged, out = refs[: 2 * (levels - 1)], refs[-1]
     index = lax.axis_index("gy")
     even = lax.rem(lax.axis_index("gx"), 2) == 0
     is_first = bit_of(index, 0) == 0
@@ -550,7 +550,7 @@
         low = jnp.where(upper & (below == 0), facing, low)
         high = jnp.where(~upper & (below == (1 << level) - 1), facing, high)
         if level == levels - 1:
-            ones_out[...] = in_order(~upper, own[0:ones, :], received[0:ones, :])
+            out[ROW_BOTH:, :] = in_order(~upper, own[0:ones, :], received[0:ones, :])
     leaf = block[ONE_ROWS : ONE_ROWS + LEAF_ROWS, :]
     for piece, rows in enumerate((low[0:LEAF_ROWS], leaf, high[0:LEAF_ROWS])):
         out[LEAF_ROWS * piece : LEAF_ROWS * (piece + 1), :] = rows
@@ -568,31 +568,30 @@
 
 def row_call(levels, operands):
     return pl.pallas_call(
-        lambda *refs: row_kernel(levels, *refs[: 2 * levels], *refs[-2:]),
-        out_shape=[
-            jax.ShapeDtypeStruct((rows, 128), F32) for rows in (ONE_ROWS << (levels - 1), ROW_BOTH)
-        ],
+        lambda *refs: row_kernel(levels, *refs[: 2 * levels], refs[-1]),
+        out_shape=jax.ShapeDtypeStruct((ROW_BOTH + (ONE_ROWS << (levels - 1)), 128), F32),
         in_specs=[VMEM] * len(operands),
-        out_specs=[VMEM] * 2,
+        out_specs=VMEM,
         compiler_params=pltpu.CompilerParams(vmem_limit_bytes=8 * MIB),
         cost_estimate=pl.CostEstimate(flops=100_000, bytes_accessed=600_000, transcendentals=0),
         name="row",
     )(*operands)
 
 
-def merge_call(bit, own, other, after):
+SENT_ROWS = 192
+
+
+def merge_call(bit, own, other, first, rows, least, after):
+    total = max(2 * rows, least)
+
     def kernel(own_ref, other_ref, after_ref, out):
         is_first = bit_of(lax.axis_index("gx"), bit) == 0
-        out[...] = in_order(is_first, own_ref[...], other_ref[...])
-
-    return pack_call(kernel, 2 * own.shape[0], (own, other, after), "merge")
-
-
-def hand_on_call(halo, after):
-    def kernel(halo_ref, after_ref, out):
-        out[...] = halo_ref[...]
-
-    return pack_call(kernel, halo.shape[0], (halo, after), "hand_on")
+        span = slice(first, first + rows)
+        out[0 : 2 * rows, :] = in_order(is_first, own_ref[span, :], other_ref[span, :])
+        if total > 2 * rows:
+            out[2 * rows :, :] = jnp.zeros((total - 2 * rows, 128), F32)
+
+    return pack_call(kernel, total, (own, other, after), "merge")
 
 
 def relay_call(received, after):
@@ -752,13 +751,30 @@
     )(*operands)
 
 
-def store_reflected(boxes, flips, flipped, gx, gy):
-    high, low = halves(boxes[...])
-    rows = high.shape[0]
-    mixed = dot(jnp.concatenate([high, low], 0), flips[2 * (gx < 0) + (gy < 0)])
-    for z in range(2):
-        flipped[gx + 1, gy + 1, z, 0] = mixed[:rows, 256 * z : 256 * z + 256]
-        flipped[gx + 1, gy + 1, z, 1] = mixed[rows:, 256 * z : 256 * z + 256]
+def store_reflected(moments, flips, flipped):
+    def store(group, z, part, value):
+        for half in range(2):
+            place = flipped.at[group[0] + 1, group[1] + 1, z, part, half]
+            place[...] = value[:, 128 * half : 128 * half + 128]
+
+    parts = {group: halves(value) for group, value in moments.items()}
+    for fx in range(2):
+        for fy in range(2):
+            groups = [group for group in moments if (group[0] < 0, group[1] < 0) == (fx == 1, fy == 1)]
+            if not groups:
+                continue
+            stacked = jnp.concatenate([part for group in groups for part in parts[group]], 0)
+            rows = stacked.shape[0] // (2 * len(groups))
+            first = 0 if fx + fy > 0 else 1
+            mixed = dot(stacked, flips[2 * fx + fy, :, 256 * first :])
+            for order, group in enumerate(groups):
+                for part in range(2):
+                    start = rows * (2 * order + part)
+                    if first == 1:
+                        store(group, 0, part, parts[group][part].astype(F32))
+                    for z in range(first, 2):
+                        span = slice(256 * (z - first), 256 * (z - first) + 256)
+                        store(group, z, part, mixed[start : start + rows, span])
 
 
 def far_sums(columns, spans, flipped, flips, tiles):
@@ -778,8 +794,11 @@
         for gx, gy, dz in entries:
             for part in range(2):
                 view = flipped.at[gx + 1, gy + 1, int(dz < 0), part]
-                windows = [view[first + dz : first + dz + size, :] for first, size in spans]
-                block = jnp.concatenate(windows, 0)
+                windows = [
+                    [view[half, first + dz : first + dz + size, :] for first, size in spans]
+                    for half in range(2)
+                ]
+                block = jnp.concatenate([jnp.concatenate(window, 0) for window in windows], 1)
                 if abs(dz) == 3:
                     block = jnp.where(odd_row if dz < 0 else ~odd_row, block, 0.0)
                 pieces[part].append(block.astype(BF16))
@@ -803,12 +822,14 @@
     return far
 
 
-def leaf_far(columns, halos, flips, tiles, boxes, flipped):
+def store_leaves(columns, halos, flips, flipped):
     index, count = lax.axis_index("gx"), lax.axis_size("gx")
     is_even = lax.rem(index, 2) == 0
-    boxes[...] = jnp.zeros_like(boxes)
+    edge = jnp.zeros((8, 128), F32)
+    groups = {}
     for gx in columns:
         for gy in (-1, 0, 1):
+            tiles_h = []
             for h in range(2):
                 row = LEAF_ROWS * (gy + 1) + 16 * h
                 rows = slice(row, row + 16)
@@ -817,34 +838,84 @@
                     moments = jnp.where(is_even == (gx == 1), moments, halos[1][rows, :])
                     inside = index > 0 if gx < 0 else index < count - 1
                     moments = jnp.where(inside, moments, 0.0)
-                boxes[8:24, 128 * h : 128 * h + 128] = moments
-            store_reflected(boxes, flips, flipped, gx, gy)
-    return far_sums(columns, ((8, 16),), flipped, flips, tiles)
-
-
-LEAF_SCRATCH = [pltpu.VMEM((32, 256), F32), pltpu.VMEM((3, 3, 2, 2, 32, 256), F32)]
-
-
-def far_own_call(row, flips, tiles, after):
-    def kernel(row_ref, flips_ref, tiles_ref, after_ref, out, boxes, flipped):
-        out[...] = leaf_far((0,), (row_ref,), flips_ref, (tiles_ref,), boxes, flipped)
-
+                tiles_h.append(jnp.concatenate([edge, moments, edge], 0))
+            groups[gx, gy] = jnp.concatenate(tiles_h, 1)
+    store_reflected(groups, flips, flipped)
+
+
+LEAF_SHAPE = (3, 3, 2, 2, 2, 32, 128)
+LEAF_SPANS = ((8, 16),)
+
+
+def far_call(kernel, shape, operands, name):
     return pl.pallas_call(
         kernel,
-        out_shape=jax.ShapeDtypeStruct((LZ, 256), F32),
-        in_specs=[VMEM] * 4,
+        out_shape=jax.ShapeDtypeStruct(shape, F32),
+        in_specs=[VMEM] * len(operands),
         out_specs=VMEM,
-        scratch_shapes=LEAF_SCRATCH,
         compiler_params=pltpu.CompilerParams(vmem_limit_bytes=8 * MIB),
-        cost_estimate=pl.CostEstimate(flops=500_000_000, bytes_accessed=600_000, transcendentals=0),
-        name="far_own",
-    )(row, flips, tiles, after)
+        cost_estimate=pl.CostEstimate(flops=300_000_000, bytes_accessed=600_000, transcendentals=0),
+        name=name,
+    )(*operands)
+
+
+def own_leaves_call(row, flips, block):
+    def kernel(row_ref, flips_ref, block_ref, out, basis_out):
+        store_leaves((0,), (row_ref,), flips_ref, out)
+        tables = basis_rows()
+        for x in range(CX):
+            for y in range(CY):
+                for j in range(ROWS):
+                    places = [part_row(c, x, y) + j for c in range(3)]
+                    rows = [block_ref[place : place + 1, :] for place in places]
+                    for k, tile in enumerate(basis_tile(*rows, None, tables)):
+                        basis_out[x * CY + y, j, 8 * k : 8 * k + 8, :] = tile
+
+    shapes = LEAF_SHAPE, (CX * CY, ROWS, 64, 128)
+    return pl.pallas_call(
+        kernel,
+        out_shape=[jax.ShapeDtypeStruct(shape, F32) for shape in shapes],
+        in_specs=[VMEM] * 3,
+        out_specs=[VMEM] * 2,
+        compiler_params=pltpu.CompilerParams(vmem_limit_bytes=8 * MIB),
+        cost_estimate=near_cost(100_000),
+        name="own_leaves",
+    )(row, flips, block)
+
+
+def far_own_call(leaves, flips, tiles):
+    def kernel(leaves_ref, flips_ref, tiles_ref, out):
+        out[...] = far_sums((0,), LEAF_SPANS, leaves_ref, flips_ref, (tiles_ref,))
+
+    return far_call(kernel, (LZ, 256), (leaves, flips, tiles), "far_own")
+
+
+def beyond_kernel(
+    before, partner, beyond, targets, flips, one, two, after, out, far_out, wide_ref, charge_ref, leaves
+):
+    out[...] = before[...]
+    beside_x(1, beyond, targets, out, wide_ref, charge_ref)
+    store_leaves((-1, 1), (partner, beyond), flips, leaves)
+    far_out[...] = far_sums((-1, 1), LEAF_SPANS, leaves, flips, (one, two))
+
+
+def beyond_call(operands):
+    return pl.pallas_call(
+        beyond_kernel,
+        out_shape=(jax.ShapeDtypeStruct(NEAR_SHAPE, F32), jax.ShapeDtypeStruct((LZ, 256), F32)),
+        in_specs=[VMEM] * len(operands),
+        out_specs=(VMEM,) * 2,
+        scratch_shapes=near_scratch(8, 10) + [pltpu.VMEM(LEAF_SHAPE, F32)],
+        compiler_params=pltpu.CompilerParams(vmem_limit_bytes=12 * MIB),
+        cost_estimate=near_cost(2_400_000),
+        name="beyond",
+    )(*operands)
 
 
 def upper_kernel(count_x, count_y, refs):
     own_ones, other_ones, small, flips, *tiles, _, out = refs[:8]
     refs = refs[8:]
-    level_one, level_two, boxes, flipped, sums, local = refs
+    level_one, level_two, flipped, sums, local = refs
 
     index_x, index_y = lax.axis_index("gx"), lax.axis_index("gy")
     pairs_y = count_y // 2
@@ -904,14 +975,16 @@
         table = [small[pl.ds(pl.multiple_of(row + 128 * k, 128), 128), :] for k in range(2)]
         top_far = top_far + dot_three(jnp.broadcast_to(third, (16, 128)), table[0], table[1])
 
-    boxes[...] = jnp.zeros_like(boxes)
+    edge = jnp.zeros((8, 256), F32)
+    groups = {}
     for gx in (-1, 0, 1):
         for gy in (-1, 0, 1):
-            for h in range(2):
-                step = 2 * (index_x // 2 + gx) + h + 2
-                boxes[8:16, 128 * h : 128 * h + 128] = level_one[step, index_y // 2 + gy + 1]
-            boxes[24:32, :] = second_group(quarter_x + gx, quarter_y + gy)
-            store_reflected(boxes, flips, flipped, gx, gy)
+            steps = [2 * (index_x // 2 + gx) + h + 2 for h in range(2)]
+            first_level = [level_one[step, index_y // 2 + gy + 1] for step in steps]
+            second_level = second_group(quarter_x + gx, quarter_y + gy)
+            blocks = [edge, jnp.concatenate(first_level, 1), edge, second_level, edge, edge]
+            groups[gx, gy] = jnp.concatenate(blocks, 0)
+    store_reflected(groups, flips, flipped)
     far = far_sums((-1, 0, 1), ((8, 8), (24, 8)), flipped, flips, tiles)
 
     def select(block, hx, hy):
@@ -951,8 +1024,7 @@
     scratch = [
         pltpu.VMEM((count_x + 4, half_y + 2, 8, 128), F32),
         pltpu.VMEM((half_x + 4, half_y + 4, 8, 128), F32),
-        pltpu.VMEM((40, 256), F32),
-        pltpu.VMEM((3, 3, 2, 2, 40, 256), F32),
+        pltpu.VMEM((3, 3, 2, 2, 2, 48, 128), F32),
         pltpu.VMEM((max(16, half_x * half_y * 8), 128), F32),
         pltpu.VMEM((2, 32, 128), F32),
     ]
@@ -968,29 +1040,21 @@
     )(*operands)
 
 
-def last_kernel(
-    own_block, before, local, far_own, partner, beyond, targets, flips, one, two, out, near_rows, *scratch
-):
-    near_rows[...] = before[...]
-    beside_x(1, beyond, targets, near_rows, *scratch[:2])
-    far_beside = leaf_far((-1, 1), (partner, beyond), flips, (one, two), *scratch[2:])
-    leaf = local[...] + far_own[...] + far_beside
+def last_kernel(basis, near_rows, local, far_own, far_beside, out):
+    leaf = local[...] + far_own[...] + far_beside[...]
+
     one, two = halves(leaf)
     turned = jnp.concatenate([one.astype(F32), two.astype(F32)], 0).T.astype(BF16)
     table = leaf_segments(2 * LZ)
-    tables = basis_rows()
     for x in range(CX):
         for y in range(CY):
             column = x * CY + y
             spread = dot(turned[64 * column : 64 * column + 64], table)
             for j in range(ROWS):
                 span = slice(128 * j, 128 * j + 128)
-                places = [part_row(c, x, y) + j for c in range(3)]
-                rows = [own_block[place : place + 1, :] for place in places]
-                basis = basis_tile(*rows, None, tables)
                 total = None
                 for k in range(8):
-                    term = basis[k] * spread[8 * k : 8 * k + 8, span]
+                    term = basis[column, j, 8 * k : 8 * k + 8, :] * spread[8 * k : 8 * k + 8, span]
                     total = term if total is None else total + term
                 value = jnp.sum(total, 0, keepdims=True) + near_rows[column, j : j + 1, :]
                 out[x, y : y + 1, span] = value
@@ -1002,8 +1066,7 @@
         out_shape=jax.ShapeDtypeStruct((CX, CY, LZ * 64), F32),
         in_specs=[VMEM] * len(operands),
         out_specs=VMEM,
-        scratch_shapes=[pltpu.VMEM(NEAR_SHAPE, F32), *near_scratch(8, 10), *LEAF_SCRATCH],
-        compiler_params=pltpu.CompilerParams(vmem_limit_bytes=12 * MIB),
+        compiler_params=pltpu.CompilerParams(vmem_limit_bytes=8 * MIB),
         name="last",
     )(*operands)
 
@@ -1048,21 +1111,23 @@
             return exchanged[0]
 
         near, targets, small, first_tiles = own_call(block, exchange_y, small, tiles[0])
-        ones, row = row_call(levels_y, (block, other, *exchanged, near))
-        other_ones = swap_bit(ones, "gx", 0)
+        row = row_call(levels_y, (block, other, *exchanged, near))
+        partner = swap_bit(row, "gx", 0)
         near, flips, other_tiles = beside_y_call(row, targets, near, (flips, tiles[1]))
-        tables_near = flips, first_tiles, other_tiles
-        ones = merge_call(0, ones, other_ones, near)
+        leaves, basis = own_leaves_call(row, flips, block)
+        far_own = far_own_call(leaves, flips, first_tiles)
+        rows = ONE_ROWS << (levels_y - 1)
+        ones = merge_call(0, row, partner, ROW_BOTH, rows, SENT_ROWS, far_own)
         other_ones = swap_bit(ones, "gx", 1)
-        partner = swap_bit(hand_on_call(row, ones), "gx", 0)
-        far_own = far_own_call(row, flips, first_tiles, ones)
-        for bit in range(1, levels_x - 1):
-            ones = merge_call(bit, ones, other_ones, far_own)
-            other_ones = swap_bit(ones, "gx", bit + 1)
         beyond = relay_ring(relay_call(partner, ones), "gx")
         near = near_call(beside_x_kernel, (partner, targets, near, ones), 8, 10, 1_200_000, "near_x")
-        local = upper_call(count_x, count_y, (ones, other_ones, small, *tables_near, near))
-        return last_call((block, near, local, far_own, partner, beyond, targets, *tables_near))
+        for bit in range(1, levels_x - 1):
+            ones = merge_call(bit, ones, other_ones, 0, rows << bit, 0, near)
+            other_ones = swap_bit(ones, "gx", bit + 1)
+        far_tables = flips, first_tiles, other_tiles
+        near, far_beside = beyond_call((near, partner, beyond, targets, *far_tables, ones))
+        local = upper_call(count_x, count_y, (ones, other_ones, small, *far_tables, near))
+        return last_call((basis, near, local, far_own, far_beside))
 
     in_specs = (P(None, "gx", "gy", None), P("gx", "gy", None))
     out_specs = P("gx", "gy", None)

time: 30 us -> 28.6 us (0.953)
  starting transfers between devices: 12.9 us -> 9.85 us
  waiting for transfers between devices: 1.87 us -> 3.89 us
  Pallas kernels: 15 us -> 14.6 us
    pallas_call x1, Pallas kernels: 3.43 us -> 0.98 us  [last_call(): pl.pallas_call(last_kernel, out_shape=jax.ShapeDtypeStruct((CX, CY, LZ *...]
    pallas_call x2 -> x4, Pallas kernels: 0.85 us -> 3.2 us  [the longest x1 2.13 us: beyond_call(): pl.pallas_call(beyond_kernel, out_shape=(jax.ShapeDtypeStruct(NEAR_SHAPE,...]
    ppermute x6 -> x5, waiting for transfers between devices: 1.87 us -> 3.89 us  [swap_bit(): lax.ppermute(value, axis, [(i, i ^ 1 << bit) for i in range(lax.axis_size...]
    ppermute x6 -> x5, starting transfers between devices: 11.2 us -> 9.3 us  [swap_bit(): lax.ppermute(value, axis, [(i, i ^ 1 << bit) for i in range(lax.axis_size...]
    ppermute x1, starting transfers between devices: 1.63 us -> 0.55 us  [relay_ring(): return lax.ppermute(value, axis, list(steps.items()))]
    pallas_call x1, Pallas kernels: 3.03 us -> 2.7 us  [upper_call(): pl.pallas_call(lambda *refs: upper_kernel(count_x, count_y, refs), out_sh...]
  transfers between devices with their start and end apart: 7 -> 6, of which waited for: 3 -> 4; matrix products, arithmetic and copies ran while one was open for 0% -> 0% of each run, Pallas kernels for 32% -> 31%
where the time goes in v5:
time: 28.6 us; the launch traced here: 28.4 us
  Pallas kernels  14.6 us (51%)
  starting transfers between devices  9.85 us (34%)
  waiting for transfers between devices  3.89 us (14%)
    ppermute x5, starting transfers between devices, swap_bit(): lax.ppermute(value, axis, [(i, i ^ 1 << bit) for i in range(lax.axis_size...  9.3 us
    ppermute x5, waiting for transfers between devices, swap_bit(): lax.ppermute(value, axis, [(i, i ^ 1 << bit) for i in range(lax.axis_size...  3.89 us
    pallas_call x1, Pallas kernels, upper_call(): pl.pallas_call(lambda *refs: upper_kernel(count_x, count_y, refs), out_sh...  2.7 us
    pallas_call x1, Pallas kernels, beyond_call(): pl.pallas_call(beyond_kernel, out_shape=(jax.ShapeDtypeStruct(NEAR_SHAPE,...  2.13 us
    pallas_call x1, Pallas kernels, own_call(): pl.pallas_call(run, out_shape=(jax.ShapeDtypeStruct(NEAR_SHAPE, F32), jax...  2.04 us
    pallas_call x1, Pallas kernels, moments_call(): pl.pallas_call(moments_kernel, out_shape=jax.ShapeDtypeStruct((OWN_ROWS,...  1.92 us
    pallas_call x1, Pallas kernels, beside_y_call(): pl.pallas_call(beside_y_kernel, out_shape=(near_shape, *tables), in_specs...  1.56 us
    pallas_call x1, Pallas kernels, own_call(): pl.pallas_call(prepare, out_shape=(jax.ShapeDtypeStruct((4, ROWS, 128, FE...  1.07 us
  transfers between devices with their start and end apart: 6, of which 4 were waited for; matrix products, arithmetic and copies ran while one was open for 0% of the time, Pallas kernels for 31%

profile of v5, /device:TPU:0, one launch (start us, length us, event | category | flops | bytes accessed | tf_op | source)
XLA Modules:
  0.0 28.4 jit_solution(18285301010481216223)
XLA Ops:
  0.0 1.9 %moments.1.block_ref.own_ref.refs_0_ = f32[168,128]{1,0:T(8,128)S(1)} custom-call(f32[3,2,2,1024]{3,2,1,0:T(2,128)} %offsets_hbm.1, f32[2,2,1024]{2,1,0:T(2,128)} %charges_hbm.1, bf16[2304,128]{1,0:T(8,128)(2,1)} %constant.8.clone.small_hbm.small), custom_call_target="tpu_custom_call" | custom-call | flops 10000000 | bytes 300000 | tf_op jit(solution)/shard_map/moments/pallas_call | solution.py:451
  1.9 0.5 %collective-permute-start = (f32[168,128]{1,0:T(8,128)S(1)}, f32[168,128]{1,0:T(8,128)S(1)}, u32[]{:S(2)}, u32[]{:S(2)}) collective-permute-start(f32[168,128]{1,0:T(8,128)S(1)} %moments.1.block_ref.own_ref.refs_0_), channel_id=1, source_target_pairs={{0,1},{1,0},{2,3},{3,2},{4,5},{5,4},{6,7},{7,6},{8,9},{9,8},{10,11... | collective-permute-start | bytes 258056 | tf_op jit(solution)/shard_map/ppermute | solution.py:1079
  2.5 1.1 %features.1 = (bf16[4,8,128,32]{3,2,1,0:T(8,128)(2,1)S(1)}, f32[8,12,8,128]{3,2,1,0:T(8,128)S(1)}, f32[8,8,128]{2,1,0:T(8,128)S(1)}, bf16[2304,128]{1,0:T(8,128)(2,1)S(1)}) custom-call(f32[168,128]{1,0:T(8,128)S(1)} %moments.1.block_ref.own_ref.refs_0_, bf16[2304,128]{1,0:T(8,128)(2,1)} %constant.8.clone.small_hbm.small), custom_call_target="tpu_custom_call" | custom-call | flops 20000000 | bytes 600000 | tf_op jit(solution)/shard_map/features/pallas_call | solution.py:635
  3.5 0.0 collective-permute-done.other_ref.refs_1_
  3.6 2.7 %collective-permute-start.1 = (f32[104,128]{1,0:T(8,128)S(1)}, f32[104,128]{1,0:T(8,128)S(1)}, u32[]{:S(2)}, u32[]{:S(2)}) collective-permute-start(f32[104,128]{1,0:T(8,128)S(1)} %group.1.after_ref.refs_2_), channel_id=1, source_target_pairs={{0,2},{1,3},{2,0},{3,1},{4,6},{5,7},{6,4},{7,5},{8,10},{9,11},{10,... | collective-permute-start | bytes 159752 | tf_op jit(solution)/shard_map/ppermute | solution.py:1079
  6.3 2.0 %near_own.1 = (f32[4,8,128]{2,1,0:T(8,128)S(1)}, bf16[10,2,256,256]{3,2,1,0:T(8,128)(2,1)S(1)}) custom-call(bf16[4,8,128,32]{3,2,1,0:T(8,128)(2,1)S(1)} %get-tuple-element.19.targets, f32[8,12,8,128]{3,2,1,0:T(8,128)S(1)} %get-tuple-element.20.features, f32[8,8,128]{2,1,0:T(8,128)S(1)} %get-tuple-element.18.after.charges, ...), custom_call_target="tpu_custom_call" | custom-call | flops 180000000 | bytes 600000 | tf_op jit(solution)/shard_map/near_own/pallas_call | solution.py:650
  8.4 0.3 collective-permute-done.1.refs_3_
  8.7 1.9 %collective-permute-start.2 = (f32[368,128]{1,0:T(8,128)S(1)}, f32[368,128]{1,0:T(8,128)S(1)}, u32[]{:S(2)}, u32[]{:S(2)}) collective-permute-start(f32[368,128]{1,0:T(8,128)S(1)} %row.1.row_ref.own_ref), channel_id=1, source_target_pairs={{0,4},{4,0},{8,12},{12,8},{16,20},{20,16},{24,28},{28,24},{1,5},{5... | collective-permute-start | bytes 565256 | tf_op jit(solution)/shard_map/ppermute | solution.py:1079
  10.6 1.6 %near_y.1 = (f32[4,8,128]{2,1,0:T(8,128)S(1)}, bf16[4,256,512]{2,1,0:T(8,128)(2,1)S(1)}, bf16[4,2,256,256]{3,2,1,0:T(8,128)(2,1)S(1)}) custom-call(f32[368,128]{1,0:T(8,128)S(1)} %row.1.row_ref.own_ref, bf16[4,8,128,32]{3,2,1,0:T(8,128)(2,1)S(1)} %get-tuple-element.19.targets, f32[4,8,128]{2,1,0:T(8,128)S(1)} %get-tuple-element.21.refs_4_.before, ...), custom_call_target="tpu_custom_call" | custom-call | flops 88000000 | bytes 600000 | tf_op jit(solution)/shard_map/near_y/pallas_call | solution.py:701
  12.1 0.5 %own_leaves.1 = (f32[3,3,2,2,2,32,128]{6,5,4,3,2,1,0:T(8,128)S(1)}, f32[4,8,64,128]{3,2,1,0:T(8,128)S(1)}) custom-call(f32[368,128]{1,0:T(8,128)S(1)} %row.1.row_ref.own_ref, bf16[4,256,512]{2,1,0:T(8,128)(2,1)S(1)} %get-tuple-element.22.flips_ref.flips.refs_3_, f32[168,128]{1,0:T(8,128)S(1)} %moments.1.block_ref.own_ref.refs_0_), custom_call_target="tpu_custom_call" | custom-call | flops 4000000 | bytes 600000 | tf_op jit(solution)/shard_map/own_leaves/pallas_call | solution.py:875
  12.6 0.6 %far_own.1.after_ref = f32[16,256]{1,0:T(8,128)S(1)} custom-call(f32[3,3,2,2,2,32,128]{6,5,4,3,2,1,0:T(8,128)S(1)} %get-tuple-element.25.leaves_ref, bf16[4,256,512]{2,1,0:T(8,128)(2,1)S(1)} %get-tuple-element.22.flips_ref.flips.refs_3_, bf16[10,2,256,256]{3,2,1,0:T(8,128)(2,1)S(1)} %get-tuple-element.26.tiles_ref.one.refs_4_), custom_call_target="tpu_custom_call" | custom-call | flops 300000000 | bytes 600000 | tf_op jit(solution)/shard_map/far_own/pallas_call | solution.py:851
  13.2 2.0 %collective-permute-done.2.other_ref.received.received_ref.partner = f32[368,128]{1,0:T(8,128)S(1)} collective-permute-done((f32[368,128]{1,0:T(8,128)S(1)}, f32[368,128]{1,0:T(8,128)S(1)}, u32[]{:S(2)}, u32[]{:S(2)}) %collective-permute-start.2) | collective-permute-done | bytes 188448 | tf_op jit(solution)/shard_map/ppermute | solution.py:1079
  15.2 1.6 %collective-permute-start.4 = (f32[192,128]{1,0:T(8,128)S(1)}, f32[192,128]{1,0:T(8,128)S(1)}, u32[]{:S(2)}, u32[]{:S(2)}) collective-permute-start(f32[192,128]{1,0:T(8,128)S(1)} %merge.2.after.after_ref.own_ref), channel_id=1, source_target_pairs={{0,8},{4,12},{8,0},{12,4},{16,24},{20,28},{24,16},{28,20},{1,9},{5... | collective-permute-start | bytes 294920 | tf_op jit(solution)/shard_map/ppermute | solution.py:1079
  16.8 0.5 %collective-permute-start.3 = (f32[224,128]{1,0:T(8,128)S(1)}, f32[224,128]{1,0:T(8,128)S(1)}, u32[]{:S(2)}, u32[]{:S(2)}) collective-permute-start(f32[224,128]{1,0:T(8,128)S(1)} %relay.1), channel_id=1, source_target_pairs={{0,8},{4,0},{8,16},{12,4},{16,24},{20,12},{24,28},{28,20},{1,9},{5... | collective-permute-start | bytes 344072 | tf_op jit(solution)/shard_map/ppermute | solution.py:1086
  17.4 1.1 %near_x.1.after_ref.before = f32[4,8,128]{2,1,0:T(8,128)S(1)} custom-call(f32[368,128]{1,0:T(8,128)S(1)} %collective-permute-done.2.other_ref.received.received_ref.partner, bf16[4,8,128,32]{3,2,1,0:T(8,128)(2,1)S(1)} %get-tuple-element.19.targets, f32[4,8,128]{2,1,0:T(8,128)S(1)} %get-tuple-element.24.before, f32[192,128]{1,0:T(8,128)S(1)} %merge.2.after.after_ref.own_ref), custom_call_target="tpu_custom_call" | custom-call | flops 48000000 | bytes 600000 | tf_op jit(solution)/shard_map/near_x/pallas_call | solution.py:742
  18.4 1.5 %collective-permute-done.4.other_ref = f32[192,128]{1,0:T(8,128)S(1)} collective-permute-done((f32[192,128]{1,0:T(8,128)S(1)}, f32[192,128]{1,0:T(8,128)S(1)}, u32[]{:S(2)}, u32[]{:S(2)}) %collective-permute-start.4) | collective-permute-done | bytes 98336 | tf_op jit(solution)/shard_map/ppermute | solution.py:1079
  19.9 2.5 %collective-permute-start.5 = (f32[64,128]{1,0:T(8,128)S(1)}, f32[64,128]{1,0:T(8,128)S(1)}, u32[]{:S(2)}, u32[]{:S(2)}) collective-permute-start(f32[64,128]{1,0:T(8,128)S(1)} %merge.3.after.refs_0_), channel_id=1, source_target_pairs={{0,16},{4,20},{8,24},{12,28},{16,0},{20,4},{24,8},{28,12},{1,17},{... | collective-permute-start | bytes 98312 | tf_op jit(solution)/shard_map/ppermute | solution.py:1079
  22.4 0.0 collective-permute-done.3.beyond
  22.4 2.1 %beyond.1 = (f32[4,8,128]{2,1,0:T(8,128)S(1)}, f32[16,256]{1,0:T(8,128)S(1)}) custom-call(f32[4,8,128]{2,1,0:T(8,128)S(1)} %near_x.1.after_ref.before, f32[368,128]{1,0:T(8,128)S(1)} %collective-permute-done.2.other_ref.received.received_ref.partner, f32[224,128]{1,0:T(8,128)S(1)} %collective-permute-done.3.beyond, ...), custom_call_target="tpu_custom_call" | custom-call | flops 96000000 | bytes 600000 | tf_op jit(solution)/shard_map/beyond/pallas_call | solution.py:903
  24.6 0.1 collective-permute-done.5.refs_1_
  24.7 2.7 %upper.1.local = f32[16,256]{1,0:T(8,128)S(1)} custom-call(f32[64,128]{1,0:T(8,128)S(1)} %merge.3.after.refs_0_, f32[64,128]{1,0:T(8,128)S(1)} %collective-permute-done.5.refs_1_, bf16[2304,128]{1,0:T(8,128)(2,1)S(1)} %get-tuple-element.29.refs_2_, bf16[4,256,512]{2,1,0:T(8,128)(2,1)S(1)} %get-tuple-element.22.flips_ref.flips.refs_3_, ...), custom_call_target="tpu_custom_call" | custom-call | flops 900000000 | bytes 600000 | tf_op jit(solution)/shard_map/upper/pallas_call | solution.py:1031
  27.4 1.0 %last.1 = f32[2,2,1024]{2,1,0:T(2,128)} custom-call(f32[4,8,64,128]{3,2,1,0:T(8,128)S(1)} %get-tuple-element.23.basis, f32[4,8,128]{2,1,0:T(8,128)S(1)} %get-tuple-element.28.refs_6_.near_rows, f32[16,256]{1,0:T(8,128)S(1)} %upper.1.local, f32[16,256]{1,0:T(8,128)S(1)} %far_own.1.after_ref, f32[16,256]{1,0:T(8,128)S(1)} %get-tuple-element.30.far_beside), custom_call_target="tpu_custom_call" | custom-call | tf_op jit(solution)/shard_map/last/pallas_call | solution.py:1064
  (5 shorter events, 0.1 us)
Async XLA Ops:
  1.9 1.6 %collective-permute-start = (f32[168,128]{1,0:T(8,128)S(1)}, f32[168,128]{1,0:T(8,128)S(1)}, u32[]{:S(2)}, u32[]{:S(2)}) collective-permute-start(f32[168,128]{1,0:T(8,128)S(1)} %moments.1.block_ref.own_ref.refs_0_), channel_id=1, source_target_pairs={{0,1},{1,0},{2,3},{3,2},{4,5},{5,4},{6,7},{7,6},{8,9},{9,8},{10,11... | collective-permute-start | bytes 258056 | tf_op jit(solution)/shard_map/ppermute | solution.py:1079
  3.6 5.1 %collective-permute-start.1 = (f32[104,128]{1,0:T(8,128)S(1)}, f32[104,128]{1,0:T(8,128)S(1)}, u32[]{:S(2)}, u32[]{:S(2)}) collective-permute-start(f32[104,128]{1,0:T(8,128)S(1)} %group.1.after_ref.refs_2_), channel_id=1, source_target_pairs={{0,2},{1,3},{2,0},{3,1},{4,6},{5,7},{6,4},{7,5},{8,10},{9,11},{10,... | collective-permute-start | bytes 159752 | tf_op jit(solution)/shard_map/ppermute | solution.py:1079
  8.7 6.5 %collective-permute-start.2 = (f32[368,128]{1,0:T(8,128)S(1)}, f32[368,128]{1,0:T(8,128)S(1)}, u32[]{:S(2)}, u32[]{:S(2)}) collective-permute-start(f32[368,128]{1,0:T(8,128)S(1)} %row.1.row_ref.own_ref), channel_id=1, source_target_pairs={{0,4},{4,0},{8,12},{12,8},{16,20},{20,16},{24,28},{28,24},{1,5},{5... | collective-permute-start | bytes 565256 | tf_op jit(solution)/shard_map/ppermute | solution.py:1079
  15.2 4.7 %collective-permute-start.4 = (f32[192,128]{1,0:T(8,128)S(1)}, f32[192,128]{1,0:T(8,128)S(1)}, u32[]{:S(2)}, u32[]{:S(2)}) collective-permute-start(f32[192,128]{1,0:T(8,128)S(1)} %merge.2.after.after_ref.own_ref), channel_id=1, source_target_pairs={{0,8},{4,12},{8,0},{12,4},{16,24},{20,28},{24,16},{28,20},{1,9},{5... | collective-permute-start | bytes 294920 | tf_op jit(solution)/shard_map/ppermute | solution.py:1079
  16.8 5.6 %collective-permute-start.3 = (f32[224,128]{1,0:T(8,128)S(1)}, f32[224,128]{1,0:T(8,128)S(1)}, u32[]{:S(2)}, u32[]{:S(2)}) collective-permute-start(f32[224,128]{1,0:T(8,128)S(1)} %relay.1), channel_id=1, source_target_pairs={{0,8},{4,0},{8,16},{12,4},{16,24},{20,12},{24,28},{28,20},{1,9},{5... | collective-permute-start | bytes 344072 | tf_op jit(solution)/shard_map/ppermute | solution.py:1086
  19.9 4.8 %collective-permute-start.5 = (f32[64,128]{1,0:T(8,128)S(1)}, f32[64,128]{1,0:T(8,128)S(1)}, u32[]{:S(2)}, u32[]{:S(2)}) collective-permute-start(f32[64,128]{1,0:T(8,128)S(1)} %merge.3.after.refs_0_), channel_id=1, source_target_pairs={{0,16},{4,20},{8,24},{12,28},{16,0},{20,4},{24,8},{28,12},{1,17},{... | collective-permute-start | bytes 98312 | tf_op jit(solution)/shard_map/ppermute | solution.py:1079

commit v6 on v5

--- a/solution.py
+++ b/solution.py
@@ -526,7 +526,6 @@
 ROW_LEAF = 3 * LEAF_ROWS
 ROW_PART = 4 * 4 * ROWS
 ROW_ROWS = ROW_LEAF + ROW_PART
-ROW_BOTH = ROW_ROWS + ROW_PART
 
 
 def row_part(c, y):
@@ -534,7 +533,7 @@
 
 
 def row_kernel(levels, block, other, *refs):
-    exchanged, out = refs[: 2 * (levels - 1)], refs[-1]
+    exchanged, (out, far_out) = refs[: 2 * (levels - 1)], refs[-2:]
     index = lax.axis_index("gy")
     even = lax.rem(lax.axis_index("gx"), 2) == 0
     is_first = bit_of(index, 0) == 0
@@ -550,7 +549,7 @@
         low = jnp.where(upper & (below == 0), facing, low)
         high = jnp.where(~upper & (below == (1 << level) - 1), facing, high)
         if level == levels - 1:
-            out[ROW_BOTH:, :] = in_order(~upper, own[0:ones, :], received[0:ones, :])
+            out[ROW_ROWS:, :] = in_order(~upper, own[0:ones, :], received[0:ones, :])
     leaf = block[ONE_ROWS : ONE_ROWS + LEAF_ROWS, :]
     for piece, rows in enumerate((low[0:LEAF_ROWS], leaf, high[0:LEAF_ROWS])):
         out[LEAF_ROWS * piece : LEAF_ROWS * (piece + 1), :] = rows
@@ -561,17 +560,20 @@
             own = [block[part_row(c, x, y) : part_row(c, x, y) + ROWS, :] for y in range(CY)]
             columns.append([low[row : row + ROWS], *own, high[row : row + ROWS]])
         for y in range(4):
-            facing, far = row_part(c, y), row_part(c, y) + ROW_PART
+            facing, far = row_part(c, y), row_part(c, y) - ROW_LEAF
             out[facing : facing + ROWS, :] = jnp.where(even, columns[1][y], columns[0][y])
-            out[far : far + ROWS, :] = jnp.where(even, columns[0][y], columns[1][y])
+            far_out[far : far + ROWS, :] = jnp.where(even, columns[0][y], columns[1][y])
 
 
 def row_call(levels, operands):
     return pl.pallas_call(
-        lambda *refs: row_kernel(levels, *refs[: 2 * levels], refs[-1]),
-        out_shape=jax.ShapeDtypeStruct((ROW_BOTH + (ONE_ROWS << (levels - 1)), 128), F32),
+        lambda *refs: row_kernel(levels, *refs[: 2 * levels], *refs[-2:]),
+        out_shape=[
+            jax.ShapeDtypeStruct((rows, 128), F32)
+            for rows in (ROW_ROWS + (ONE_ROWS << (levels - 1)), ROW_PART)
+        ],
         in_specs=[VMEM] * len(operands),
-        out_specs=VMEM,
+        out_specs=[VMEM] * 2,
         compiler_params=pltpu.CompilerParams(vmem_limit_bytes=8 * MIB),
         cost_estimate=pl.CostEstimate(flops=100_000, bytes_accessed=600_000, transcendentals=0),
         name="row",
@@ -594,12 +596,12 @@
     return pack_call(kernel, total, (own, other, after), "merge")
 
 
-def relay_call(received, after):
-    def kernel(received_ref, after_ref, out):
+def relay_call(received, received_far, after):
+    def kernel(received_ref, far_ref, after_ref, out):
         out[0:ROW_LEAF, :] = received_ref[0:ROW_LEAF, :]
-        out[ROW_LEAF:ROW_ROWS, :] = received_ref[ROW_ROWS:ROW_BOTH, :]
-
-    return pack_call(kernel, ROW_ROWS, (received, after), "relay")
+        out[ROW_LEAF:ROW_ROWS, :] = far_ref[...]
+
+    return pack_call(kernel, ROW_ROWS, (received, received_far, after), "relay")
 
 
 def own_kernel(block, targets, features, charges):
@@ -664,7 +666,7 @@
 
 
 def beside_y_kernel(
-    row_ref, targets, before, flips, tiles, out, flips_out, tiles_out, wide_ref, charge_ref, semaphores
+    row_ref, far_ref, targets, before, flips, tiles, out, flips_out, tiles_out, wide_ref, charge_ref, semaphores
 ):
     copies = [
         pltpu.make_async_copy(flips, flips_out, semaphores.at[0]),
@@ -677,8 +679,8 @@
 
     def raw(x, y):
         def read(c):
-            facing, far = row_part(c, y), row_part(c, y) + ROW_PART
-            own = row_ref[facing : facing + ROWS, :], row_ref[far : far + ROWS, :]
+            facing, far = row_part(c, y), row_part(c, y) - ROW_LEAF
+            own = row_ref[facing : facing + ROWS, :], far_ref[far : far + ROWS, :]
             return jnp.where(even == (x == 1), *own)
 
         return read
@@ -695,19 +697,19 @@
         copy.wait()
 
 
-def beside_y_call(row, targets, before, constants):
+def beside_y_call(row, far, targets, before, constants):
     near_shape = jax.ShapeDtypeStruct(NEAR_SHAPE, F32)
     tables = [jax.ShapeDtypeStruct(constant.shape, BF16) for constant in constants]
     return pl.pallas_call(
         beside_y_kernel,
         out_shape=(near_shape, *tables),
-        in_specs=[VMEM] * 3 + [HBM] * 2,
+        in_specs=[VMEM] * 4 + [HBM] * 2,
         out_specs=(VMEM,) * 3,
         scratch_shapes=near_scratch(8, 8) + [pltpu.SemaphoreType.DMA((2,))],
         compiler_params=pltpu.CompilerParams(vmem_limit_bytes=8 * MIB),
         cost_estimate=near_cost(2_200_000),
         name="near_y",
-    )(row, targets, before, *constants)
+    )(row, far, targets, before, *constants)
 
 
 def beside_x(parity, received, targets, out, wide_ref, charge_ref):
@@ -1111,15 +1113,16 @@
             return exchanged[0]
 
         near, targets, small, first_tiles = own_call(block, exchange_y, small, tiles[0])
-        row = row_call(levels_y, (block, other, *exchanged, near))
+        row, far = row_call(levels_y, (block, other, *exchanged, near))
         partner = swap_bit(row, "gx", 0)
-        near, flips, other_tiles = beside_y_call(row, targets, near, (flips, tiles[1]))
+        partner_far = swap_bit(far, "gx", 0)
+        near, flips, other_tiles = beside_y_call(row, far, targets, near, (flips, tiles[1]))
         leaves, basis = own_leaves_call(row, flips, block)
         far_own = far_own_call(leaves, flips, first_tiles)
         rows = ONE_ROWS << (levels_y - 1)
-        ones = merge_call(0, row, partner, ROW_BOTH, rows, SENT_ROWS, far_own)
+        ones = merge_call(0, row, partner, ROW_ROWS, rows, SENT_ROWS, far_own)
         other_ones = swap_bit(ones, "gx", 1)
-        beyond = relay_ring(relay_call(partner, ones), "gx")
+        beyond = relay_ring(relay_call(partner, partner_far, ones), "gx")
         near = near_call(beside_x_kernel, (partner, targets, near, ones), 8, 10, 1_200_000, "near_x")
         for bit in range(1, levels_x - 1):
             ones = merge_call(bit, ones, other_ones, 0, rows << bit, 0, near)

time: 28.6 us -> 27.9 us (0.976)
  waiting for transfers between devices: 3.89 us -> 2.85 us
  starting transfers between devices: 9.85 us -> 10.2 us
    ppermute x5 -> x6, waiting for transfers between devices: 3.89 us -> 2.85 us  [swap_bit(): lax.ppermute(value, axis, [(i, i ^ 1 << bit) for i in range(lax.axis_size...]
    ppermute x5 -> x6, starting transfers between devices: 9.3 us -> 9.52 us  [swap_bit(): lax.ppermute(value, axis, [(i, i ^ 1 << bit) for i in range(lax.axis_size...]
  transfers between devices with their start and end apart: 6 -> 7, of which waited for: 4 -> 4; matrix products, arithmetic and copies ran while one was open for 0% -> 0% of each run, Pallas kernels for 31% -> 32%
where the time goes in v6:
time: 27.9 us; the launch traced here: 27.7 us
  Pallas kernels  14.6 us (52%)
  starting transfers between devices  10.2 us (37%)
  waiting for transfers between devices  2.85 us (10%)
    ppermute x6, starting transfers between devices, swap_bit(): lax.ppermute(value, axis, [(i, i ^ 1 << bit) for i in range(lax.axis_size...  9.52 us
    ppermute x6, waiting for transfers between devices, swap_bit(): lax.ppermute(value, axis, [(i, i ^ 1 << bit) for i in range(lax.axis_size...  2.85 us
    pallas_call x1, Pallas kernels, upper_call(): pl.pallas_call(lambda *refs: upper_kernel(count_x, count_y, refs), out_sh...  2.7 us
    pallas_call x1, Pallas kernels, beyond_call(): pl.pallas_call(beyond_kernel, out_shape=(jax.ShapeDtypeStruct(NEAR_SHAPE,...  2.12 us
    pallas_call x1, Pallas kernels, own_call(): pl.pallas_call(run, out_shape=(jax.ShapeDtypeStruct(NEAR_SHAPE, F32), jax...  2.02 us
    pallas_call x1, Pallas kernels, moments_call(): pl.pallas_call(moments_kernel, out_shape=jax.ShapeDtypeStruct((OWN_ROWS,...  1.92 us
    pallas_call x1, Pallas kernels, beside_y_call(): pl.pallas_call(beside_y_kernel, out_shape=(near_shape, *tables), in_specs...  1.56 us
    pallas_call x1, Pallas kernels, own_call(): pl.pallas_call(prepare, out_shape=(jax.ShapeDtypeStruct((4, ROWS, 128, FE...  1.07 us
  transfers between devices with their start and end apart: 7, of which 4 were waited for; matrix products, arithmetic and copies ran while one was open for 0% of the time, Pallas kernels for 32%

profile of v6, /device:TPU:0, one launch (start us, length us, event | category | flops | bytes accessed | tf_op | source)
XLA Modules:
  0.0 27.7 jit_solution(14432577196130212891)
XLA Ops:
  0.0 1.9 %moments.1.block_ref.own_ref.refs_0_ = f32[168,128]{1,0:T(8,128)S(1)} custom-call(f32[3,2,2,1024]{3,2,1,0:T(2,128)} %offsets_hbm.1, f32[2,2,1024]{2,1,0:T(2,128)} %charges_hbm.1, bf16[2304,128]{1,0:T(8,128)(2,1)} %constant.8.clone.small_hbm.small), custom_call_target="tpu_custom_call" | custom-call | flops 10000000 | bytes 300000 | tf_op jit(solution)/shard_map/moments/pallas_call | solution.py:451
  1.9 0.5 %collective-permute-start = (f32[168,128]{1,0:T(8,128)S(1)}, f32[168,128]{1,0:T(8,128)S(1)}, u32[]{:S(2)}, u32[]{:S(2)}) collective-permute-start(f32[168,128]{1,0:T(8,128)S(1)} %moments.1.block_ref.own_ref.refs_0_), channel_id=1, source_target_pairs={{0,1},{1,0},{2,3},{3,2},{4,5},{5,4},{6,7},{7,6},{8,9},{9,8},{10,11... | collective-permute-start | bytes 258056 | tf_op jit(solution)/shard_map/ppermute | solution.py:1081
  2.4 1.1 %features.1 = (bf16[4,8,128,32]{3,2,1,0:T(8,128)(2,1)S(1)}, f32[8,12,8,128]{3,2,1,0:T(8,128)S(1)}, f32[8,8,128]{2,1,0:T(8,128)S(1)}, bf16[2304,128]{1,0:T(8,128)(2,1)S(1)}) custom-call(f32[168,128]{1,0:T(8,128)S(1)} %moments.1.block_ref.own_ref.refs_0_, bf16[2304,128]{1,0:T(8,128)(2,1)} %constant.8.clone.small_hbm.small), custom_call_target="tpu_custom_call" | custom-call | flops 20000000 | bytes 600000 | tf_op jit(solution)/shard_map/features/pallas_call | solution.py:637
  3.5 0.0 collective-permute-done.other_ref.refs_1_
  3.6 2.7 %collective-permute-start.1 = (f32[104,128]{1,0:T(8,128)S(1)}, f32[104,128]{1,0:T(8,128)S(1)}, u32[]{:S(2)}, u32[]{:S(2)}) collective-permute-start(f32[104,128]{1,0:T(8,128)S(1)} %group.1.after_ref.refs_2_), channel_id=1, source_target_pairs={{0,2},{1,3},{2,0},{3,1},{4,6},{5,7},{6,4},{7,5},{8,10},{9,11},{10,... | collective-permute-start | bytes 159752 | tf_op jit(solution)/shard_map/ppermute | solution.py:1081
  6.3 2.0 %near_own.1 = (f32[4,8,128]{2,1,0:T(8,128)S(1)}, bf16[10,2,256,256]{3,2,1,0:T(8,128)(2,1)S(1)}) custom-call(bf16[4,8,128,32]{3,2,1,0:T(8,128)(2,1)S(1)} %get-tuple-element.21.targets, f32[8,12,8,128]{3,2,1,0:T(8,128)S(1)} %get-tuple-element.22.features, f32[8,8,128]{2,1,0:T(8,128)S(1)} %get-tuple-element.20.after.charges, ...), custom_call_target="tpu_custom_call" | custom-call | flops 180000000 | bytes 600000 | tf_op jit(solution)/shard_map/near_own/pallas_call | solution.py:652
  8.3 0.3 %collective-permute-done.1.refs_3_ = f32[104,128]{1,0:T(8,128)S(1)} collective-permute-done((f32[104,128]{1,0:T(8,128)S(1)}, f32[104,128]{1,0:T(8,128)S(1)}, u32[]{:S(2)}, u32[]{:S(2)}) %collective-permute-start.1) | collective-permute-done | bytes 53280 | tf_op jit(solution)/shard_map/ppermute | solution.py:1081
  8.7 1.9 %collective-permute-start.2 = (f32[240,128]{1,0:T(8,128)S(1)}, f32[240,128]{1,0:T(8,128)S(1)}, u32[]{:S(2)}, u32[]{:S(2)}) collective-permute-start(f32[240,128]{1,0:T(8,128)S(1)} %get-tuple-element.24.row_ref.own_ref), channel_id=1, source_target_pairs={{0,4},{4,0},{8,12},{12,8},{16,20},{20,16},{24,28},{28,24},{1,5},{5... | collective-permute-start | bytes 368648 | tf_op jit(solution)/shard_map/ppermute | solution.py:1081
  10.6 0.2 collective-permute-start.3
  10.8 1.6 %near_y.1 = (f32[4,8,128]{2,1,0:T(8,128)S(1)}, bf16[4,256,512]{2,1,0:T(8,128)(2,1)S(1)}, bf16[4,2,256,256]{3,2,1,0:T(8,128)(2,1)S(1)}) custom-call(f32[240,128]{1,0:T(8,128)S(1)} %get-tuple-element.24.row_ref.own_ref, f32[128,128]{1,0:T(8,128)S(1)} %get-tuple-element.25.far_ref, bf16[4,8,128,32]{3,2,1,0:T(8,128)(2,1)S(1)} %get-tuple-element.21.targets, ...), custom_call_target="tpu_custom_call" | custom-call | flops 88000000 | bytes 600000 | tf_op jit(solution)/shard_map/near_y/pallas_call | solution.py:703
  12.3 0.5 %own_leaves.1 = (f32[3,3,2,2,2,32,128]{6,5,4,3,2,1,0:T(8,128)S(1)}, f32[4,8,64,128]{3,2,1,0:T(8,128)S(1)}) custom-call(f32[240,128]{1,0:T(8,128)S(1)} %get-tuple-element.24.row_ref.own_ref, bf16[4,256,512]{2,1,0:T(8,128)(2,1)S(1)} %get-tuple-element.26.flips_ref.flips.refs_3_, f32[168,128]{1,0:T(8,128)S(1)} %moments.1.block_ref.own_ref.refs_0_), custom_call_target="tpu_custom_call" | custom-call | flops 4000000 | bytes 600000 | tf_op jit(solution)/shard_map/own_leaves/pallas_call | solution.py:877
  12.8 0.6 %far_own.1.after_ref = f32[16,256]{1,0:T(8,128)S(1)} custom-call(f32[3,3,2,2,2,32,128]{6,5,4,3,2,1,0:T(8,128)S(1)} %get-tuple-element.29.leaves_ref, bf16[4,256,512]{2,1,0:T(8,128)(2,1)S(1)} %get-tuple-element.26.flips_ref.flips.refs_3_, bf16[10,2,256,256]{3,2,1,0:T(8,128)(2,1)S(1)} %get-tuple-element.30.tiles_ref.one.refs_4_), custom_call_target="tpu_custom_call" | custom-call | flops 300000000 | bytes 600000 | tf_op jit(solution)/shard_map/far_own/pallas_call | solution.py:853
  13.4 1.1 %collective-permute-done.2.other_ref.received.received_ref.partner = f32[240,128]{1,0:T(8,128)S(1)} collective-permute-done((f32[240,128]{1,0:T(8,128)S(1)}, f32[240,128]{1,0:T(8,128)S(1)}, u32[]{:S(2)}, u32[]{:S(2)}) %collective-permute-start.2) | collective-permute-done | bytes 122912 | tf_op jit(solution)/shard_map/ppermute | solution.py:1081
  14.5 1.6 %collective-permute-start.5 = (f32[192,128]{1,0:T(8,128)S(1)}, f32[192,128]{1,0:T(8,128)S(1)}, u32[]{:S(2)}, u32[]{:S(2)}) collective-permute-start(f32[192,128]{1,0:T(8,128)S(1)} %merge.2.after.after_ref.own_ref), channel_id=1, source_target_pairs={{0,8},{4,12},{8,0},{12,4},{16,24},{20,28},{24,16},{28,20},{1,9},{5... | collective-permute-start | bytes 294920 | tf_op jit(solution)/shard_map/ppermute | solution.py:1081
  16.1 0.0 collective-permute-done.3.far_ref
  16.1 0.7 %collective-permute-start.4 = (f32[224,128]{1,0:T(8,128)S(1)}, f32[224,128]{1,0:T(8,128)S(1)}, u32[]{:S(2)}, u32[]{:S(2)}) collective-permute-start(f32[224,128]{1,0:T(8,128)S(1)} %relay.1), channel_id=1, source_target_pairs={{0,8},{4,0},{8,16},{12,4},{16,24},{20,12},{24,28},{28,20},{1,9},{5... | collective-permute-start | bytes 344072 | tf_op jit(solution)/shard_map/ppermute | solution.py:1088
  16.8 1.1 %near_x.1.after_ref.before = f32[4,8,128]{2,1,0:T(8,128)S(1)} custom-call(f32[240,128]{1,0:T(8,128)S(1)} %collective-permute-done.2.other_ref.received.received_ref.partner, bf16[4,8,128,32]{3,2,1,0:T(8,128)(2,1)S(1)} %get-tuple-element.21.targets, f32[4,8,128]{2,1,0:T(8,128)S(1)} %get-tuple-element.28.before, f32[192,128]{1,0:T(8,128)S(1)} %merge.2.after.after_ref.own_ref), custom_call_target="tpu_custom_call" | custom-call | flops 48000000 | bytes 600000 | tf_op jit(solution)/shard_map/near_x/pallas_call | solution.py:744
  17.8 1.3 %collective-permute-done.5.other_ref = f32[192,128]{1,0:T(8,128)S(1)} collective-permute-done((f32[192,128]{1,0:T(8,128)S(1)}, f32[192,128]{1,0:T(8,128)S(1)}, u32[]{:S(2)}, u32[]{:S(2)}) %collective-permute-start.5) | collective-permute-done | bytes 98336 | tf_op jit(solution)/shard_map/ppermute | solution.py:1081
  19.2 2.6 %collective-permute-start.6 = (f32[64,128]{1,0:T(8,128)S(1)}, f32[64,128]{1,0:T(8,128)S(1)}, u32[]{:S(2)}, u32[]{:S(2)}) collective-permute-start(f32[64,128]{1,0:T(8,128)S(1)} %merge.3.after.refs_0_), channel_id=1, source_target_pairs={{0,16},{4,20},{8,24},{12,28},{16,0},{20,4},{24,8},{28,12},{1,17},{... | collective-permute-start | bytes 98312 | tf_op jit(solution)/shard_map/ppermute | solution.py:1081
  21.8 0.0 collective-permute-done.4.beyond
  21.8 2.1 %beyond.1 = (f32[4,8,128]{2,1,0:T(8,128)S(1)}, f32[16,256]{1,0:T(8,128)S(1)}) custom-call(f32[4,8,128]{2,1,0:T(8,128)S(1)} %near_x.1.after_ref.before, f32[240,128]{1,0:T(8,128)S(1)} %collective-permute-done.2.other_ref.received.received_ref.partner, f32[224,128]{1,0:T(8,128)S(1)} %collective-permute-done.4.beyond, ...), custom_call_target="tpu_custom_call" | custom-call | flops 96000000 | bytes 600000 | tf_op jit(solution)/shard_map/beyond/pallas_call | solution.py:905
  23.9 0.1 collective-permute-done.6.refs_1_
  24.0 2.7 %upper.1.local = f32[16,256]{1,0:T(8,128)S(1)} custom-call(f32[64,128]{1,0:T(8,128)S(1)} %merge.3.after.refs_0_, f32[64,128]{1,0:T(8,128)S(1)} %collective-permute-done.6.refs_1_, bf16[2304,128]{1,0:T(8,128)(2,1)S(1)} %get-tuple-element.33.refs_2_, bf16[4,256,512]{2,1,0:T(8,128)(2,1)S(1)} %get-tuple-element.26.flips_ref.flips.refs_3_, ...), custom_call_target="tpu_custom_call" | custom-call | flops 900000000 | bytes 600000 | tf_op jit(solution)/shard_map/upper/pallas_call | solution.py:1033
  26.7 1.0 %last.1 = f32[2,2,1024]{2,1,0:T(2,128)} custom-call(f32[4,8,64,128]{3,2,1,0:T(8,128)S(1)} %get-tuple-element.27.basis, f32[4,8,128]{2,1,0:T(8,128)S(1)} %get-tuple-element.32.refs_6_.near_rows, f32[16,256]{1,0:T(8,128)S(1)} %upper.1.local, f32[16,256]{1,0:T(8,128)S(1)} %far_own.1.after_ref, f32[16,256]{1,0:T(8,128)S(1)} %get-tuple-element.34.far_beside), custom_call_target="tpu_custom_call" | custom-call | tf_op jit(solution)/shard_map/last/pallas_call | solution.py:1066
  (5 shorter events, 0.1 us)
Async XLA Ops:
  1.9 1.6 %collective-permute-start = (f32[168,128]{1,0:T(8,128)S(1)}, f32[168,128]{1,0:T(8,128)S(1)}, u32[]{:S(2)}, u32[]{:S(2)}) collective-permute-start(f32[168,128]{1,0:T(8,128)S(1)} %moments.1.block_ref.own_ref.refs_0_), channel_id=1, source_target_pairs={{0,1},{1,0},{2,3},{3,2},{4,5},{5,4},{6,7},{7,6},{8,9},{9,8},{10,11... | collective-permute-start | bytes 258056 | tf_op jit(solution)/shard_map/ppermute | solution.py:1081
  3.6 5.1 %collective-permute-start.1 = (f32[104,128]{1,0:T(8,128)S(1)}, f32[104,128]{1,0:T(8,128)S(1)}, u32[]{:S(2)}, u32[]{:S(2)}) collective-permute-start(f32[104,128]{1,0:T(8,128)S(1)} %group.1.after_ref.refs_2_), channel_id=1, source_target_pairs={{0,2},{1,3},{2,0},{3,1},{4,6},{5,7},{6,4},{7,5},{8,10},{9,11},{10,... | collective-permute-start | bytes 159752 | tf_op jit(solution)/shard_map/ppermute | solution.py:1081
  8.7 5.8 %collective-permute-start.2 = (f32[240,128]{1,0:T(8,128)S(1)}, f32[240,128]{1,0:T(8,128)S(1)}, u32[]{:S(2)}, u32[]{:S(2)}) collective-permute-start(f32[240,128]{1,0:T(8,128)S(1)} %get-tuple-element.24.row_ref.own_ref), channel_id=1, source_target_pairs={{0,4},{4,0},{8,12},{12,8},{16,20},{20,16},{24,28},{28,24},{1,5},{5... | collective-permute-start | bytes 368648 | tf_op jit(solution)/shard_map/ppermute | solution.py:1081
  10.6 5.5 %collective-permute-start.3 = (f32[128,128]{1,0:T(8,128)S(1)}, f32[128,128]{1,0:T(8,128)S(1)}, u32[]{:S(2)}, u32[]{:S(2)}) collective-permute-start(f32[128,128]{1,0:T(8,128)S(1)} %get-tuple-element.25.far_ref), channel_id=1, source_target_pairs={{0,4},{4,0},{8,12},{12,8},{16,20},{20,16},{24,28},{28,24},{1,5},{5... | collective-permute-start | bytes 196616 | tf_op jit(solution)/shard_map/ppermute | solution.py:1081
  14.5 4.7 %collective-permute-start.5 = (f32[192,128]{1,0:T(8,128)S(1)}, f32[192,128]{1,0:T(8,128)S(1)}, u32[]{:S(2)}, u32[]{:S(2)}) collective-permute-start(f32[192,128]{1,0:T(8,128)S(1)} %merge.2.after.after_ref.own_ref), channel_id=1, source_target_pairs={{0,8},{4,12},{8,0},{12,4},{16,24},{20,28},{24,16},{28,20},{1,9},{5... | collective-permute-start | bytes 294920 | tf_op jit(solution)/shard_map/ppermute | solution.py:1081
  16.1 5.7 %collective-permute-start.4 = (f32[224,128]{1,0:T(8,128)S(1)}, f32[224,128]{1,0:T(8,128)S(1)}, u32[]{:S(2)}, u32[]{:S(2)}) collective-permute-start(f32[224,128]{1,0:T(8,128)S(1)} %relay.1), channel_id=1, source_target_pairs={{0,8},{4,0},{8,16},{12,4},{16,24},{20,12},{24,28},{28,20},{1,9},{5... | collective-permute-start | bytes 344072 | tf_op jit(solution)/shard_map/ppermute | solution.py:1088
  19.2 4.8 %collective-permute-start.6 = (f32[64,128]{1,0:T(8,128)S(1)}, f32[64,128]{1,0:T(8,128)S(1)}, u32[]{:S(2)}, u32[]{:S(2)}) collective-permute-start(f32[64,128]{1,0:T(8,128)S(1)} %merge.3.after.refs_0_), channel_id=1, source_target_pairs={{0,16},{4,20},{8,24},{12,28},{16,0},{20,4},{24,8},{28,12},{1,17},{... | collective-permute-start | bytes 98312 | tf_op jit(solution)/shard_map/ppermute | solution.py:1081

commit v7 on v6

--- a/solution.py
+++ b/solution.py
@@ -813,35 +813,29 @@
             key = (int(gx < 0), int(gy < 0), int(dz < 0))
             piece = result[16 * order : 16 * order + 16]
             totals[key] = totals[key] + piece if key in totals else piece
+    return totals
+
+
+def unreflect(totals, flips):
     far = None
     for (fx, fy, fz), total in totals.items():
         if (fx, fy, fz) != (0, 0, 0):
-            high, low = halves(total)
             table = flips[2 * fx + fy, :, 256 * fz : 256 * fz + 256]
-            both = dot(jnp.concatenate([high, low], 0), table)
+            both = dot(jnp.concatenate(halves(total), 0), table)
             total = both[:16] + both[16:]
         far = total if far is None else far + total
     return far
 
 
-def store_leaves(columns, halos, flips, flipped):
-    index, count = lax.axis_index("gx"), lax.axis_size("gx")
-    is_even = lax.rem(index, 2) == 0
+def store_leaves(row, flips, flipped):
     edge = jnp.zeros((8, 128), F32)
     groups = {}
-    for gx in columns:
-        for gy in (-1, 0, 1):
-            tiles_h = []
-            for h in range(2):
-                row = LEAF_ROWS * (gy + 1) + 16 * h
-                rows = slice(row, row + 16)
-                moments = halos[0][rows, :]
-                if gx != 0:
-                    moments = jnp.where(is_even == (gx == 1), moments, halos[1][rows, :])
-                    inside = index > 0 if gx < 0 else index < count - 1
-                    moments = jnp.where(inside, moments, 0.0)
-                tiles_h.append(jnp.concatenate([edge, moments, edge], 0))
-            groups[gx, gy] = jnp.concatenate(tiles_h, 1)
+    for gy in (-1, 0, 1):
+        columns = []
+        for h in range(2):
+            start = LEAF_ROWS * (gy + 1) + 16 * h
+            columns.append(jnp.concatenate([edge, row[start : start + 16, :], edge], 0))
+        groups[0, gy] = jnp.concatenate(columns, 1)
     store_reflected(groups, flips, flipped)
 
 
@@ -863,7 +857,7 @@
 
 def own_leaves_call(row, flips, block):
     def kernel(row_ref, flips_ref, block_ref, out, basis_out):
-        store_leaves((0,), (row_ref,), flips_ref, out)
+        store_leaves(row_ref, flips_ref, out)
         tables = basis_rows()
         for x in range(CX):
             for y in range(CY):
@@ -887,18 +881,61 @@
 
 def far_own_call(leaves, flips, tiles):
     def kernel(leaves_ref, flips_ref, tiles_ref, out):
-        out[...] = far_sums((0,), LEAF_SPANS, leaves_ref, flips_ref, (tiles_ref,))
+        out[...] = unreflect(far_sums((0,), LEAF_SPANS, leaves_ref, flips_ref, (tiles_ref,)), flips_ref)
 
     return far_call(kernel, (LZ, 256), (leaves, flips, tiles), "far_own")
 
 
+def far_side(halo, side_is_low, inside, flips, tiles, flipped):
+    flip_x = jnp.where(side_is_low, 1, 0)
+    edge = jnp.zeros((8, 128), F32)
+    for flip_y, steps in ((0, (0, 1)), (1, (-1,))):
+        stacked = []
+        for gy in steps:
+            columns = []
+            for h in range(2):
+                row = LEAF_ROWS * (gy + 1) + 16 * h
+                moments = jnp.where(inside, halo[row : row + 16, :], 0.0)
+                columns.append(jnp.concatenate([edge, moments, edge], 0))
+            stacked += halves(jnp.concatenate(columns, 1))
+        mixed = dot(jnp.concatenate(stacked, 0), flips[2 * flip_x + flip_y])
+        for order, gy in enumerate(steps):
+            for part, z, half in itertools.product(range(2), range(2), range(2)):
+                start, lane = 32 * (2 * order + part), 256 * z + 128 * half
+                flipped[2, gy + 1, z, part, half] = mixed[start : start + 32, lane : lane + 128]
+    far = None
+    for (_, fy, fz), total in far_sums((1,), LEAF_SPANS, flipped, flips, tiles).items():
+        table = flips[2 * flip_x + fy][:, 256 * fz : 256 * fz + 256]
+        both = dot(jnp.concatenate(halves(total), 0), table)
+        far = both[:16] + both[16:] if far is None else far + both[:16] + both[16:]
+    return far
+
+
+def far_partner_call(partner, tables, after):
+    def kernel(partner_ref, flips, one, two, after_ref, out, flipped):
+        odd = lax.rem(lax.axis_index("gx"), 2) == 1
+        out[...] = far_side(partner_ref, odd, odd | ~odd, flips, (one, two), flipped)
+
+    return pl.pallas_call(
+        kernel,
+        out_shape=jax.ShapeDtypeStruct((LZ, 256), F32),
+        in_specs=[VMEM] * 5,
+        out_specs=VMEM,
+        scratch_shapes=[pltpu.VMEM(LEAF_SHAPE, F32)],
+        compiler_params=pltpu.CompilerParams(vmem_limit_bytes=8 * MIB),
+        cost_estimate=pl.CostEstimate(flops=300_000_000, bytes_accessed=600_000, transcendentals=0),
+        name="far_partner",
+    )(partner, *tables, after)
+
+
 def beyond_kernel(
-    before, partner, beyond, targets, flips, one, two, after, out, far_out, wide_ref, charge_ref, leaves
+    before, beyond, targets, flips, one, two, after, out, far_out, wide_ref, charge_ref, flipped
 ):
     out[...] = before[...]
     beside_x(1, beyond, targets, out, wide_ref, charge_ref)
-    store_leaves((-1, 1), (partner, beyond), flips, leaves)
-    far_out[...] = far_sums((-1, 1), LEAF_SPANS, leaves, flips, (one, two))
+    index, count = lax.axis_index("gx"), lax.axis_size("gx")
+    inside = (index > 0) & (index < count - 1)
+    far_out[...] = far_side(beyond, lax.rem(index, 2) == 0, inside, flips, (one, two), flipped)
 
 
 def beyond_call(operands):
@@ -987,7 +1024,7 @@
             blocks = [edge, jnp.concatenate(first_level, 1), edge, second_level, edge, edge]
             groups[gx, gy] = jnp.concatenate(blocks, 0)
     store_reflected(groups, flips, flipped)
-    far = far_sums((-1, 0, 1), ((8, 8), (24, 8)), flipped, flips, tiles)
+    far = unreflect(far_sums((-1, 0, 1), ((8, 8), (24, 8)), flipped, flips, tiles), flips)
 
     def select(block, hx, hy):
         tile = jnp.where(hx == 1, block[:, 128:256], block[:, 0:128])
@@ -1042,8 +1079,8 @@
     )(*operands)
 
 
-def last_kernel(basis, near_rows, local, far_own, far_beside, out):
-    leaf = local[...] + far_own[...] + far_beside[...]
+def last_kernel(basis, near_rows, local, far_own, far_partner, far_beyond, out):
+    leaf = local[...] + far_own[...] + far_partner[...] + far_beyond[...]
 
     one, two = halves(leaf)
     turned = jnp.concatenate([one.astype(F32), two.astype(F32)], 0).T.astype(BF16)
@@ -1123,14 +1160,15 @@
         ones = merge_call(0, row, partner, ROW_ROWS, rows, SENT_ROWS, far_own)
         other_ones = swap_bit(ones, "gx", 1)
         beyond = relay_ring(relay_call(partner, partner_far, ones), "gx")
-        near = near_call(beside_x_kernel, (partner, targets, near, ones), 8, 10, 1_200_000, "near_x")
+        far_tables = flips, first_tiles, other_tiles
+        far_partner = far_partner_call(partner, far_tables, ones)
+        near = near_call(beside_x_kernel, (partner, targets, near, far_partner), 8, 10, 1_200_000, "near_x")
         for bit in range(1, levels_x - 1):
             ones = merge_call(bit, ones, other_ones, 0, rows << bit, 0, near)
             other_ones = swap_bit(ones, "gx", bit + 1)
-        far_tables = flips, first_tiles, other_tiles
-        near, far_beside = beyond_call((near, partner, beyond, targets, *far_tables, ones))
+        near, far_beyond = beyond_call((near, beyond, targets, *far_tables, ones))
         local = upper_call(count_x, count_y, (ones, other_ones, small, *far_tables, near))
-        return last_call((basis, near, local, far_own, far_beside))
+        return last_call((basis, near, local, far_own, far_partner, far_beyond))
 
     in_specs = (P(None, "gx", "gy", None), P("gx", "gy", None))
     out_specs = P("gx", "gy", None)

time: 27.9 us -> 27.9 us (level)
  waiting for transfers between devices: 2.85 us -> 2.08 us
  Pallas kernels: 14.6 us -> 15.3 us
    pallas_call x0 -> x1, Pallas kernels: none -> 0.94 us  [far_partner_call(): pl.pallas_call(kernel, out_shape=jax.ShapeDtypeStruct((LZ, 256), F32), in...]
    ppermute x6, waiting for transfers between devices: 2.85 us -> 2.08 us  [swap_bit(): lax.ppermute(value, axis, [(i, i ^ 1 << bit) for i in range(lax.axis_size...]
  transfers between devices with their start and end apart: 7 -> 7, of which waited for: 4 -> 4; matrix products, arithmetic and copies ran while one was open for 0% -> 0% of each run, Pallas kernels for 32% -> 35%
where the time goes in v7:
time: 27.9 us; the launch traced here: 27.7 us
  Pallas kernels  15.3 us (55%)
  starting transfers between devices  10.2 us (37%)
  waiting for transfers between devices  2.08 us (7%)
    ppermute x6, starting transfers between devices, swap_bit(): lax.ppermute(value, axis, [(i, i ^ 1 << bit) for i in range(lax.axis_size...  9.48 us
    pallas_call x1, Pallas kernels, upper_call(): pl.pallas_call(lambda *refs: upper_kernel(count_x, count_y, refs), out_sh...  2.66 us
    ppermute x6, waiting for transfers between devices, swap_bit(): lax.ppermute(value, axis, [(i, i ^ 1 << bit) for i in range(lax.axis_size...  2.08 us
    pallas_call x1, Pallas kernels, own_call(): pl.pallas_call(run, out_shape=(jax.ShapeDtypeStruct(NEAR_SHAPE, F32), jax...  2.04 us
    pallas_call x1, Pallas kernels, beyond_call(): pl.pallas_call(beyond_kernel, out_shape=(jax.ShapeDtypeStruct(NEAR_SHAPE,...  1.98 us
    pallas_call x1, Pallas kernels, moments_call(): pl.pallas_call(moments_kernel, out_shape=jax.ShapeDtypeStruct((OWN_ROWS,...  1.92 us
    pallas_call x1, Pallas kernels, beside_y_call(): pl.pallas_call(beside_y_kernel, out_shape=(near_shape, *tables), in_specs...  1.56 us
    pallas_call x1, Pallas kernels, near_call(): pl.pallas_call(kernel, out_shape=jax.ShapeDtypeStruct(NEAR_SHAPE, F32), i...  1.08 us
  transfers between devices with their start and end apart: 7, of which 4 were waited for; matrix products, arithmetic and copies ran while one was open for 0% of the time, Pallas kernels for 35%

profile of v7, /device:TPU:0, one launch (start us, length us, event | category | flops | bytes accessed | tf_op | source)
XLA Modules:
  0.0 27.7 jit_solution(3113246733905665829)
XLA Ops:
  0.0 1.9 %moments.1.block_ref.own_ref.refs_0_ = f32[168,128]{1,0:T(8,128)S(1)} custom-call(f32[3,2,2,1024]{3,2,1,0:T(2,128)} %offsets_hbm.1, f32[2,2,1024]{2,1,0:T(2,128)} %charges_hbm.1, bf16[2304,128]{1,0:T(8,128)(2,1)} %constant.8.clone.small_hbm.small), custom_call_target="tpu_custom_call" | custom-call | flops 10000000 | bytes 300000 | tf_op jit(solution)/shard_map/moments/pallas_call | solution.py:451
  1.9 0.5 %collective-permute-start = (f32[168,128]{1,0:T(8,128)S(1)}, f32[168,128]{1,0:T(8,128)S(1)}, u32[]{:S(2)}, u32[]{:S(2)}) collective-permute-start(f32[168,128]{1,0:T(8,128)S(1)} %moments.1.block_ref.own_ref.refs_0_), channel_id=1, source_target_pairs={{0,1},{1,0},{2,3},{3,2},{4,5},{5,4},{6,7},{7,6},{8,9},{9,8},{10,11... | collective-permute-start | bytes 258056 | tf_op jit(solution)/shard_map/ppermute | solution.py:1118
  2.4 1.1 %features.1 = (bf16[4,8,128,32]{3,2,1,0:T(8,128)(2,1)S(1)}, f32[8,12,8,128]{3,2,1,0:T(8,128)S(1)}, f32[8,8,128]{2,1,0:T(8,128)S(1)}, bf16[2304,128]{1,0:T(8,128)(2,1)S(1)}) custom-call(f32[168,128]{1,0:T(8,128)S(1)} %moments.1.block_ref.own_ref.refs_0_, bf16[2304,128]{1,0:T(8,128)(2,1)} %constant.8.clone.small_hbm.small), custom_call_target="tpu_custom_call" | custom-call | flops 20000000 | bytes 600000 | tf_op jit(solution)/shard_map/features/pallas_call | solution.py:637
  3.5 0.0 collective-permute-done.other_ref.refs_1_
  3.6 2.7 %collective-permute-start.1 = (f32[104,128]{1,0:T(8,128)S(1)}, f32[104,128]{1,0:T(8,128)S(1)}, u32[]{:S(2)}, u32[]{:S(2)}) collective-permute-start(f32[104,128]{1,0:T(8,128)S(1)} %group.1.after_ref.refs_2_), channel_id=1, source_target_pairs={{0,2},{1,3},{2,0},{3,1},{4,6},{5,7},{6,4},{7,5},{8,10},{9,11},{10,... | collective-permute-start | bytes 159752 | tf_op jit(solution)/shard_map/ppermute | solution.py:1118
  6.3 2.0 %near_own.1 = (f32[4,8,128]{2,1,0:T(8,128)S(1)}, bf16[10,2,256,256]{3,2,1,0:T(8,128)(2,1)S(1)}) custom-call(bf16[4,8,128,32]{3,2,1,0:T(8,128)(2,1)S(1)} %get-tuple-element.21.targets, f32[8,12,8,128]{3,2,1,0:T(8,128)S(1)} %get-tuple-element.22.features, f32[8,8,128]{2,1,0:T(8,128)S(1)} %get-tuple-element.20.after.charges, ...), custom_call_target="tpu_custom_call" | custom-call | flops 180000000 | bytes 600000 | tf_op jit(solution)/shard_map/near_own/pallas_call | solution.py:652
  8.4 0.3 collective-permute-done.1.refs_3_
  8.7 1.9 %collective-permute-start.2 = (f32[240,128]{1,0:T(8,128)S(1)}, f32[240,128]{1,0:T(8,128)S(1)}, u32[]{:S(2)}, u32[]{:S(2)}) collective-permute-start(f32[240,128]{1,0:T(8,128)S(1)} %get-tuple-element.24.row_ref.own_ref), channel_id=1, source_target_pairs={{0,4},{4,0},{8,12},{12,8},{16,20},{20,16},{24,28},{28,24},{1,5},{5... | collective-permute-start | bytes 368648 | tf_op jit(solution)/shard_map/ppermute | solution.py:1118
  10.6 0.2 collective-permute-start.3
  10.8 1.6 %near_y.1 = (f32[4,8,128]{2,1,0:T(8,128)S(1)}, bf16[4,256,512]{2,1,0:T(8,128)(2,1)S(1)}, bf16[4,2,256,256]{3,2,1,0:T(8,128)(2,1)S(1)}) custom-call(f32[240,128]{1,0:T(8,128)S(1)} %get-tuple-element.24.row_ref.own_ref, f32[128,128]{1,0:T(8,128)S(1)} %get-tuple-element.25.far_ref, bf16[4,8,128,32]{3,2,1,0:T(8,128)(2,1)S(1)} %get-tuple-element.21.targets, ...), custom_call_target="tpu_custom_call" | custom-call | flops 88000000 | bytes 600000 | tf_op jit(solution)/shard_map/near_y/pallas_call | solution.py:703
  12.3 0.5 %own_leaves.1 = (f32[3,3,2,2,2,32,128]{6,5,4,3,2,1,0:T(8,128)S(1)}, f32[4,8,64,128]{3,2,1,0:T(8,128)S(1)}) custom-call(f32[240,128]{1,0:T(8,128)S(1)} %get-tuple-element.24.row_ref.own_ref, bf16[4,256,512]{2,1,0:T(8,128)(2,1)S(1)} %get-tuple-element.26.flips_ref.flips.refs_3_, f32[168,128]{1,0:T(8,128)S(1)} %moments.1.block_ref.own_ref.refs_0_), custom_call_target="tpu_custom_call" | custom-call | flops 4000000 | bytes 600000 | tf_op jit(solution)/shard_map/own_leaves/pallas_call | solution.py:871
  12.8 0.6 %far_own.1.after_ref = f32[16,256]{1,0:T(8,128)S(1)} custom-call(f32[3,3,2,2,2,32,128]{6,5,4,3,2,1,0:T(8,128)S(1)} %get-tuple-element.31.leaves_ref, bf16[4,256,512]{2,1,0:T(8,128)(2,1)S(1)} %get-tuple-element.26.flips_ref.flips.refs_3_, bf16[10,2,256,256]{3,2,1,0:T(8,128)(2,1)S(1)} %get-tuple-element.29.tiles_ref.one.refs_4_), custom_call_target="tpu_custom_call" | custom-call | flops 300000000 | bytes 600000 | tf_op jit(solution)/shard_map/far_own/pallas_call | solution.py:847
  13.4 1.1 %collective-permute-done.2.other_ref.partner_ref.received.received_ref = f32[240,128]{1,0:T(8,128)S(1)} collective-permute-done((f32[240,128]{1,0:T(8,128)S(1)}, f32[240,128]{1,0:T(8,128)S(1)}, u32[]{:S(2)}, u32[]{:S(2)}) %collective-permute-start.2) | collective-permute-done | bytes 122912 | tf_op jit(solution)/shard_map/ppermute | solution.py:1118
  14.5 1.6 %collective-permute-start.5 = (f32[192,128]{1,0:T(8,128)S(1)}, f32[192,128]{1,0:T(8,128)S(1)}, u32[]{:S(2)}, u32[]{:S(2)}) collective-permute-start(f32[192,128]{1,0:T(8,128)S(1)} %merge.2.after_ref.own_ref), channel_id=1, source_target_pairs={{0,8},{4,12},{8,0},{12,4},{16,24},{20,28},{24,16},{28,20},{1,9},{5... | collective-permute-start | bytes 294920 | tf_op jit(solution)/shard_map/ppermute | solution.py:1118
  16.1 0.0 collective-permute-done.3.far_ref
  16.1 0.7 %collective-permute-start.4 = (f32[224,128]{1,0:T(8,128)S(1)}, f32[224,128]{1,0:T(8,128)S(1)}, u32[]{:S(2)}, u32[]{:S(2)}) collective-permute-start(f32[224,128]{1,0:T(8,128)S(1)} %relay.1), channel_id=1, source_target_pairs={{0,8},{4,0},{8,16},{12,4},{16,24},{20,12},{24,28},{28,20},{1,9},{5... | collective-permute-start | bytes 344072 | tf_op jit(solution)/shard_map/ppermute | solution.py:1125
  16.8 0.9 %far_partner.1.after = f32[16,256]{1,0:T(8,128)S(1)} custom-call(f32[240,128]{1,0:T(8,128)S(1)} %collective-permute-done.2.other_ref.partner_ref.received.received_ref, bf16[4,256,512]{2,1,0:T(8,128)(2,1)S(1)} %get-tuple-element.26.flips_ref.flips.refs_3_, bf16[10,2,256,256]{3,2,1,0:T(8,128)(2,1)S(1)} %get-tuple-element.29.tiles_ref.one.refs_4_, ...), custom_call_target="tpu_custom_call" | custom-call | flops 300000000 | bytes 600000 | tf_op jit(solution)/shard_map/far_partner/pallas_call | solution.py:919
  17.7 1.1 %near_x.1.after_ref.before = f32[4,8,128]{2,1,0:T(8,128)S(1)} custom-call(f32[240,128]{1,0:T(8,128)S(1)} %collective-permute-done.2.other_ref.partner_ref.received.received_ref, bf16[4,8,128,32]{3,2,1,0:T(8,128)(2,1)S(1)} %get-tuple-element.21.targets, f32[4,8,128]{2,1,0:T(8,128)S(1)} %get-tuple-element.28.before, f32[16,256]{1,0:T(8,128)S(1)} %far_partner.1.after), custom_call_target="tpu_custom_call" | custom-call | flops 48000000 | bytes 600000 | tf_op jit(solution)/shard_map/near_x/pallas_call | solution.py:744
  18.8 0.4 %collective-permute-done.5.other_ref = f32[192,128]{1,0:T(8,128)S(1)} collective-permute-done((f32[192,128]{1,0:T(8,128)S(1)}, f32[192,128]{1,0:T(8,128)S(1)}, u32[]{:S(2)}, u32[]{:S(2)}) %collective-permute-start.5) | collective-permute-done | bytes 98336 | tf_op jit(solution)/shard_map/ppermute | solution.py:1118
  19.2 2.5 %collective-permute-start.6 = (f32[64,128]{1,0:T(8,128)S(1)}, f32[64,128]{1,0:T(8,128)S(1)}, u32[]{:S(2)}, u32[]{:S(2)}) collective-permute-start(f32[64,128]{1,0:T(8,128)S(1)} %merge.3.after.refs_0_), channel_id=1, source_target_pairs={{0,16},{4,20},{8,24},{12,28},{16,0},{20,4},{24,8},{28,12},{1,17},{... | collective-permute-start | bytes 98312 | tf_op jit(solution)/shard_map/ppermute | solution.py:1118
  21.7 0.0 collective-permute-done.4.beyond
  21.7 2.0 %beyond.1 = (f32[4,8,128]{2,1,0:T(8,128)S(1)}, f32[16,256]{1,0:T(8,128)S(1)}) custom-call(f32[4,8,128]{2,1,0:T(8,128)S(1)} %near_x.1.after_ref.before, f32[224,128]{1,0:T(8,128)S(1)} %collective-permute-done.4.beyond, bf16[4,8,128,32]{3,2,1,0:T(8,128)(2,1)S(1)} %get-tuple-element.21.targets, ...), custom_call_target="tpu_custom_call" | custom-call | flops 96000000 | bytes 600000 | tf_op jit(solution)/shard_map/beyond/pallas_call | solution.py:942
  23.7 0.3 %collective-permute-done.6.refs_1_ = f32[64,128]{1,0:T(8,128)S(1)} collective-permute-done((f32[64,128]{1,0:T(8,128)S(1)}, f32[64,128]{1,0:T(8,128)S(1)}, u32[]{:S(2)}, u32[]{:S(2)}) %collective-permute-start.6) | collective-permute-done | bytes 32800 | tf_op jit(solution)/shard_map/ppermute | solution.py:1118
  24.0 2.7 %upper.1.local = f32[16,256]{1,0:T(8,128)S(1)} custom-call(f32[64,128]{1,0:T(8,128)S(1)} %merge.3.after.refs_0_, f32[64,128]{1,0:T(8,128)S(1)} %collective-permute-done.6.refs_1_, bf16[2304,128]{1,0:T(8,128)(2,1)S(1)} %get-tuple-element.33.refs_2_, bf16[4,256,512]{2,1,0:T(8,128)(2,1)S(1)} %get-tuple-element.26.flips_ref.flips.refs_3_, ...), custom_call_target="tpu_custom_call" | custom-call | flops 900000000 | bytes 600000 | tf_op jit(solution)/shard_map/upper/pallas_call | solution.py:1070
  26.7 1.0 %last.1 = f32[2,2,1024]{2,1,0:T(2,128)} custom-call(f32[4,8,64,128]{3,2,1,0:T(8,128)S(1)} %get-tuple-element.27.basis, f32[4,8,128]{2,1,0:T(8,128)S(1)} %get-tuple-element.32.refs_6_.near_rows, f32[16,256]{1,0:T(8,128)S(1)} %upper.1.local, f32[16,256]{1,0:T(8,128)S(1)} %far_own.1.after_ref, f32[16,256]{1,0:T(8,128)S(1)} %far_partner.1.after, ...), custom_call_target="tpu_custom_call" | custom-call | tf_op jit(solution)/shard_map/last/pallas_call | solution.py:1103
  (5 shorter events, 0.1 us)
Async XLA Ops:
  1.9 1.6 %collective-permute-start = (f32[168,128]{1,0:T(8,128)S(1)}, f32[168,128]{1,0:T(8,128)S(1)}, u32[]{:S(2)}, u32[]{:S(2)}) collective-permute-start(f32[168,128]{1,0:T(8,128)S(1)} %moments.1.block_ref.own_ref.refs_0_), channel_id=1, source_target_pairs={{0,1},{1,0},{2,3},{3,2},{4,5},{5,4},{6,7},{7,6},{8,9},{9,8},{10,11... | collective-permute-start | bytes 258056 | tf_op jit(solution)/shard_map/ppermute | solution.py:1118
  3.6 5.1 %collective-permute-start.1 = (f32[104,128]{1,0:T(8,128)S(1)}, f32[104,128]{1,0:T(8,128)S(1)}, u32[]{:S(2)}, u32[]{:S(2)}) collective-permute-start(f32[104,128]{1,0:T(8,128)S(1)} %group.1.after_ref.refs_2_), channel_id=1, source_target_pairs={{0,2},{1,3},{2,0},{3,1},{4,6},{5,7},{6,4},{7,5},{8,10},{9,11},{10,... | collective-permute-start | bytes 159752 | tf_op jit(solution)/shard_map/ppermute | solution.py:1118
  8.7 5.8 %collective-permute-start.2 = (f32[240,128]{1,0:T(8,128)S(1)}, f32[240,128]{1,0:T(8,128)S(1)}, u32[]{:S(2)}, u32[]{:S(2)}) collective-permute-start(f32[240,128]{1,0:T(8,128)S(1)} %get-tuple-element.24.row_ref.own_ref), channel_id=1, source_target_pairs={{0,4},{4,0},{8,12},{12,8},{16,20},{20,16},{24,28},{28,24},{1,5},{5... | collective-permute-start | bytes 368648 | tf_op jit(solution)/shard_map/ppermute | solution.py:1118
  10.6 5.5 %collective-permute-start.3 = (f32[128,128]{1,0:T(8,128)S(1)}, f32[128,128]{1,0:T(8,128)S(1)}, u32[]{:S(2)}, u32[]{:S(2)}) collective-permute-start(f32[128,128]{1,0:T(8,128)S(1)} %get-tuple-element.25.far_ref), channel_id=1, source_target_pairs={{0,4},{4,0},{8,12},{12,8},{16,20},{20,16},{24,28},{28,24},{1,5},{5... | collective-permute-start | bytes 196616 | tf_op jit(solution)/shard_map/ppermute | solution.py:1118
  14.5 4.7 %collective-permute-start.5 = (f32[192,128]{1,0:T(8,128)S(1)}, f32[192,128]{1,0:T(8,128)S(1)}, u32[]{:S(2)}, u32[]{:S(2)}) collective-permute-start(f32[192,128]{1,0:T(8,128)S(1)} %merge.2.after_ref.own_ref), channel_id=1, source_target_pairs={{0,8},{4,12},{8,0},{12,4},{16,24},{20,28},{24,16},{28,20},{1,9},{5... | collective-permute-start | bytes 294920 | tf_op jit(solution)/shard_map/ppermute | solution.py:1118
  16.1 5.6 %collective-permute-start.4 = (f32[224,128]{1,0:T(8,128)S(1)}, f32[224,128]{1,0:T(8,128)S(1)}, u32[]{:S(2)}, u32[]{:S(2)}) collective-permute-start(f32[224,128]{1,0:T(8,128)S(1)} %relay.1), channel_id=1, source_target_pairs={{0,8},{4,0},{8,16},{12,4},{16,24},{20,12},{24,28},{28,20},{1,9},{5... | collective-permute-start | bytes 344072 | tf_op jit(solution)/shard_map/ppermute | solution.py:1125
  19.2 4.8 %collective-permute-start.6 = (f32[64,128]{1,0:T(8,128)S(1)}, f32[64,128]{1,0:T(8,128)S(1)}, u32[]{:S(2)}, u32[]{:S(2)}) collective-permute-start(f32[64,128]{1,0:T(8,128)S(1)} %merge.3.after.refs_0_), channel_id=1, source_target_pairs={{0,16},{4,20},{8,24},{12,28},{16,0},{20,4},{24,8},{28,12},{1,17},{... | collective-permute-start | bytes 98312 | tf_op jit(solution)/shard_map/ppermute | solution.py:1118

commit v8 on v7

--- a/solution.py
+++ b/solution.py
@@ -580,7 +580,7 @@
     )(*operands)
 
 
-SENT_ROWS = 192
+SENT_ROWS = 184
 
 
 def merge_call(bit, own, other, first, rows, least, after):

time: 27.9 us -> 27.8 us (level)
  no operation moved by 1% of the time
where the time goes in v8:
time: 27.8 us; the launch traced here: 27.6 us
  Pallas kernels  15.4 us (55%)
  starting transfers between devices  10.1 us (36%)
  waiting for transfers between devices  1.99 us (7%)
    ppermute x6, starting transfers between devices, swap_bit(): lax.ppermute(value, axis, [(i, i ^ 1 << bit) for i in range(lax.axis_size...  9.48 us
    pallas_call x1, Pallas kernels, upper_call(): pl.pallas_call(lambda *refs: upper_kernel(count_x, count_y, refs), out_sh...  2.66 us
    pallas_call x1, Pallas kernels, own_call(): pl.pallas_call(run, out_shape=(jax.ShapeDtypeStruct(NEAR_SHAPE, F32), jax...  2.03 us
    pallas_call x1, Pallas kernels, beyond_call(): pl.pallas_call(beyond_kernel, out_shape=(jax.ShapeDtypeStruct(NEAR_SHAPE,...  2.02 us
    ppermute x6, waiting for transfers between devices, swap_bit(): lax.ppermute(value, axis, [(i, i ^ 1 << bit) for i in range(lax.axis_size...  1.99 us
    pallas_call x1, Pallas kernels, moments_call(): pl.pallas_call(moments_kernel, out_shape=jax.ShapeDtypeStruct((OWN_ROWS,...  1.92 us
    pallas_call x1, Pallas kernels, beside_y_call(): pl.pallas_call(beside_y_kernel, out_shape=(near_shape, *tables), in_specs...  1.56 us
    pallas_call x1, Pallas kernels, near_call(): pl.pallas_call(kernel, out_shape=jax.ShapeDtypeStruct(NEAR_SHAPE, F32), i...  1.09 us
  transfers between devices with their start and end apart: 7, of which 4 were waited for; matrix products, arithmetic and copies ran while one was open for 0% of the time, Pallas kernels for 35%

profile of v8, /device:TPU:0, one launch (start us, length us, event | category | flops | bytes accessed | tf_op | source)
XLA Modules:
  0.0 27.6 jit_solution(3681208413120733440)
XLA Ops:
  0.0 1.9 %moments.1.block_ref.own_ref.refs_0_ = f32[168,128]{1,0:T(8,128)S(1)} custom-call(f32[3,2,2,1024]{3,2,1,0:T(2,128)} %offsets_hbm.1, f32[2,2,1024]{2,1,0:T(2,128)} %charges_hbm.1, bf16[2304,128]{1,0:T(8,128)(2,1)} %constant.8.clone.small_hbm.small), custom_call_target="tpu_custom_call" | custom-call | flops 10000000 | bytes 300000 | tf_op jit(solution)/shard_map/moments/pallas_call | solution.py:451
  1.9 0.5 %collective-permute-start = (f32[168,128]{1,0:T(8,128)S(1)}, f32[168,128]{1,0:T(8,128)S(1)}, u32[]{:S(2)}, u32[]{:S(2)}) collective-permute-start(f32[168,128]{1,0:T(8,128)S(1)} %moments.1.block_ref.own_ref.refs_0_), channel_id=1, source_target_pairs={{0,1},{1,0},{2,3},{3,2},{4,5},{5,4},{6,7},{7,6},{8,9},{9,8},{10,11... | collective-permute-start | bytes 258056 | tf_op jit(solution)/shard_map/ppermute | solution.py:1118
  2.4 1.1 %features.1 = (bf16[4,8,128,32]{3,2,1,0:T(8,128)(2,1)S(1)}, f32[8,12,8,128]{3,2,1,0:T(8,128)S(1)}, f32[8,8,128]{2,1,0:T(8,128)S(1)}, bf16[2304,128]{1,0:T(8,128)(2,1)S(1)}) custom-call(f32[168,128]{1,0:T(8,128)S(1)} %moments.1.block_ref.own_ref.refs_0_, bf16[2304,128]{1,0:T(8,128)(2,1)} %constant.8.clone.small_hbm.small), custom_call_target="tpu_custom_call" | custom-call | flops 20000000 | bytes 600000 | tf_op jit(solution)/shard_map/features/pallas_call | solution.py:637
  3.5 0.0 collective-permute-done.other_ref.refs_1_
  3.6 2.7 %collective-permute-start.1 = (f32[104,128]{1,0:T(8,128)S(1)}, f32[104,128]{1,0:T(8,128)S(1)}, u32[]{:S(2)}, u32[]{:S(2)}) collective-permute-start(f32[104,128]{1,0:T(8,128)S(1)} %group.1.after_ref.refs_2_), channel_id=1, source_target_pairs={{0,2},{1,3},{2,0},{3,1},{4,6},{5,7},{6,4},{7,5},{8,10},{9,11},{10,... | collective-permute-start | bytes 159752 | tf_op jit(solution)/shard_map/ppermute | solution.py:1118
  6.3 2.0 %near_own.1 = (f32[4,8,128]{2,1,0:T(8,128)S(1)}, bf16[10,2,256,256]{3,2,1,0:T(8,128)(2,1)S(1)}) custom-call(bf16[4,8,128,32]{3,2,1,0:T(8,128)(2,1)S(1)} %get-tuple-element.21.targets, f32[8,12,8,128]{3,2,1,0:T(8,128)S(1)} %get-tuple-element.22.features, f32[8,8,128]{2,1,0:T(8,128)S(1)} %get-tuple-element.20.after.charges, ...), custom_call_target="tpu_custom_call" | custom-call | flops 180000000 | bytes 600000 | tf_op jit(solution)/shard_map/near_own/pallas_call | solution.py:652
  8.4 0.3 %collective-permute-done.1.refs_3_ = f32[104,128]{1,0:T(8,128)S(1)} collective-permute-done((f32[104,128]{1,0:T(8,128)S(1)}, f32[104,128]{1,0:T(8,128)S(1)}, u32[]{:S(2)}, u32[]{:S(2)}) %collective-permute-start.1) | collective-permute-done | bytes 53280 | tf_op jit(solution)/shard_map/ppermute | solution.py:1118
  8.7 1.9 %collective-permute-start.2 = (f32[240,128]{1,0:T(8,128)S(1)}, f32[240,128]{1,0:T(8,128)S(1)}, u32[]{:S(2)}, u32[]{:S(2)}) collective-permute-start(f32[240,128]{1,0:T(8,128)S(1)} %get-tuple-element.24.row_ref.own_ref), channel_id=1, source_target_pairs={{0,4},{4,0},{8,12},{12,8},{16,20},{20,16},{24,28},{28,24},{1,5},{5... | collective-permute-start | bytes 368648 | tf_op jit(solution)/shard_map/ppermute | solution.py:1118
  10.6 0.2 collective-permute-start.3
  10.8 1.6 %near_y.1 = (f32[4,8,128]{2,1,0:T(8,128)S(1)}, bf16[4,256,512]{2,1,0:T(8,128)(2,1)S(1)}, bf16[4,2,256,256]{3,2,1,0:T(8,128)(2,1)S(1)}) custom-call(f32[240,128]{1,0:T(8,128)S(1)} %get-tuple-element.24.row_ref.own_ref, f32[128,128]{1,0:T(8,128)S(1)} %get-tuple-element.25.far_ref, bf16[4,8,128,32]{3,2,1,0:T(8,128)(2,1)S(1)} %get-tuple-element.21.targets, ...), custom_call_target="tpu_custom_call" | custom-call | flops 88000000 | bytes 600000 | tf_op jit(solution)/shard_map/near_y/pallas_call | solution.py:703
  12.3 0.5 %own_leaves.1 = (f32[3,3,2,2,2,32,128]{6,5,4,3,2,1,0:T(8,128)S(1)}, f32[4,8,64,128]{3,2,1,0:T(8,128)S(1)}) custom-call(f32[240,128]{1,0:T(8,128)S(1)} %get-tuple-element.24.row_ref.own_ref, bf16[4,256,512]{2,1,0:T(8,128)(2,1)S(1)} %get-tuple-element.26.flips_ref.flips.refs_3_, f32[168,128]{1,0:T(8,128)S(1)} %moments.1.block_ref.own_ref.refs_0_), custom_call_target="tpu_custom_call" | custom-call | flops 4000000 | bytes 600000 | tf_op jit(solution)/shard_map/own_leaves/pallas_call | solution.py:871
  12.8 0.6 %far_own.1.after_ref = f32[16,256]{1,0:T(8,128)S(1)} custom-call(f32[3,3,2,2,2,32,128]{6,5,4,3,2,1,0:T(8,128)S(1)} %get-tuple-element.31.leaves_ref, bf16[4,256,512]{2,1,0:T(8,128)(2,1)S(1)} %get-tuple-element.26.flips_ref.flips.refs_3_, bf16[10,2,256,256]{3,2,1,0:T(8,128)(2,1)S(1)} %get-tuple-element.29.tiles_ref.one.refs_4_), custom_call_target="tpu_custom_call" | custom-call | flops 300000000 | bytes 600000 | tf_op jit(solution)/shard_map/far_own/pallas_call | solution.py:847
  13.4 1.1 %collective-permute-done.2.other_ref.partner_ref.received.received_ref = f32[240,128]{1,0:T(8,128)S(1)} collective-permute-done((f32[240,128]{1,0:T(8,128)S(1)}, f32[240,128]{1,0:T(8,128)S(1)}, u32[]{:S(2)}, u32[]{:S(2)}) %collective-permute-start.2) | collective-permute-done | bytes 122912 | tf_op jit(solution)/shard_map/ppermute | solution.py:1118
  14.5 1.6 %collective-permute-start.5 = (f32[184,128]{1,0:T(8,128)S(1)}, f32[184,128]{1,0:T(8,128)S(1)}, u32[]{:S(2)}, u32[]{:S(2)}) collective-permute-start(f32[184,128]{1,0:T(8,128)S(1)} %merge.2.after_ref.own_ref), channel_id=1, source_target_pairs={{0,8},{4,12},{8,0},{12,4},{16,24},{20,28},{24,16},{28,20},{1,9},{5... | collective-permute-start | bytes 282632 | tf_op jit(solution)/shard_map/ppermute | solution.py:1118
  16.1 0.0 collective-permute-done.3.far_ref
  16.1 0.7 %collective-permute-start.4 = (f32[224,128]{1,0:T(8,128)S(1)}, f32[224,128]{1,0:T(8,128)S(1)}, u32[]{:S(2)}, u32[]{:S(2)}) collective-permute-start(f32[224,128]{1,0:T(8,128)S(1)} %relay.1), channel_id=1, source_target_pairs={{0,8},{4,0},{8,16},{12,4},{16,24},{20,12},{24,28},{28,20},{1,9},{5... | collective-permute-start | bytes 344072 | tf_op jit(solution)/shard_map/ppermute | solution.py:1125
  16.8 0.9 %far_partner.1.after = f32[16,256]{1,0:T(8,128)S(1)} custom-call(f32[240,128]{1,0:T(8,128)S(1)} %collective-permute-done.2.other_ref.partner_ref.received.received_ref, bf16[4,256,512]{2,1,0:T(8,128)(2,1)S(1)} %get-tuple-element.26.flips_ref.flips.refs_3_, bf16[10,2,256,256]{3,2,1,0:T(8,128)(2,1)S(1)} %get-tuple-element.29.tiles_ref.one.refs_4_, ...), custom_call_target="tpu_custom_call" | custom-call | flops 300000000 | bytes 600000 | tf_op jit(solution)/shard_map/far_partner/pallas_call | solution.py:919
  17.7 1.1 %near_x.1.after_ref.before = f32[4,8,128]{2,1,0:T(8,128)S(1)} custom-call(f32[240,128]{1,0:T(8,128)S(1)} %collective-permute-done.2.other_ref.partner_ref.received.received_ref, bf16[4,8,128,32]{3,2,1,0:T(8,128)(2,1)S(1)} %get-tuple-element.21.targets, f32[4,8,128]{2,1,0:T(8,128)S(1)} %get-tuple-element.28.before, f32[16,256]{1,0:T(8,128)S(1)} %far_partner.1.after), custom_call_target="tpu_custom_call" | custom-call | flops 48000000 | bytes 600000 | tf_op jit(solution)/shard_map/near_x/pallas_call | solution.py:744
  18.8 0.3 %collective-permute-done.5.other_ref = f32[184,128]{1,0:T(8,128)S(1)} collective-permute-done((f32[184,128]{1,0:T(8,128)S(1)}, f32[184,128]{1,0:T(8,128)S(1)}, u32[]{:S(2)}, u32[]{:S(2)}) %collective-permute-start.5) | collective-permute-done | bytes 94240 | tf_op jit(solution)/shard_map/ppermute | solution.py:1118
  19.2 2.5 %collective-permute-start.6 = (f32[64,128]{1,0:T(8,128)S(1)}, f32[64,128]{1,0:T(8,128)S(1)}, u32[]{:S(2)}, u32[]{:S(2)}) collective-permute-start(f32[64,128]{1,0:T(8,128)S(1)} %merge.3.after.refs_0_), channel_id=1, source_target_pairs={{0,16},{4,20},{8,24},{12,28},{16,0},{20,4},{24,8},{28,12},{1,17},{... | collective-permute-start | bytes 98312 | tf_op jit(solution)/shard_map/ppermute | solution.py:1118
  21.7 0.0 collective-permute-done.4.beyond
  21.7 2.0 %beyond.1 = (f32[4,8,128]{2,1,0:T(8,128)S(1)}, f32[16,256]{1,0:T(8,128)S(1)}) custom-call(f32[4,8,128]{2,1,0:T(8,128)S(1)} %near_x.1.after_ref.before, f32[224,128]{1,0:T(8,128)S(1)} %collective-permute-done.4.beyond, bf16[4,8,128,32]{3,2,1,0:T(8,128)(2,1)S(1)} %get-tuple-element.21.targets, ...), custom_call_target="tpu_custom_call" | custom-call | flops 96000000 | bytes 600000 | tf_op jit(solution)/shard_map/beyond/pallas_call | solution.py:942
  23.7 0.3 collective-permute-done.6.refs_1_
  24.0 2.7 %upper.1.local = f32[16,256]{1,0:T(8,128)S(1)} custom-call(f32[64,128]{1,0:T(8,128)S(1)} %merge.3.after.refs_0_, f32[64,128]{1,0:T(8,128)S(1)} %collective-permute-done.6.refs_1_, bf16[2304,128]{1,0:T(8,128)(2,1)S(1)} %get-tuple-element.33.refs_2_, bf16[4,256,512]{2,1,0:T(8,128)(2,1)S(1)} %get-tuple-element.26.flips_ref.flips.refs_3_, ...), custom_call_target="tpu_custom_call" | custom-call | flops 900000000 | bytes 600000 | tf_op jit(solution)/shard_map/upper/pallas_call | solution.py:1070
  26.6 1.0 %last.1 = f32[2,2,1024]{2,1,0:T(2,128)} custom-call(f32[4,8,64,128]{3,2,1,0:T(8,128)S(1)} %get-tuple-element.27.basis, f32[4,8,128]{2,1,0:T(8,128)S(1)} %get-tuple-element.32.refs_6_.near_rows, f32[16,256]{1,0:T(8,128)S(1)} %upper.1.local, f32[16,256]{1,0:T(8,128)S(1)} %far_own.1.after_ref, f32[16,256]{1,0:T(8,128)S(1)} %far_partner.1.after, ...), custom_call_target="tpu_custom_call" | custom-call | tf_op jit(solution)/shard_map/last/pallas_call | solution.py:1103
  (5 shorter events, 0.1 us)
Async XLA Ops:
  1.9 1.6 %collective-permute-start = (f32[168,128]{1,0:T(8,128)S(1)}, f32[168,128]{1,0:T(8,128)S(1)}, u32[]{:S(2)}, u32[]{:S(2)}) collective-permute-start(f32[168,128]{1,0:T(8,128)S(1)} %moments.1.block_ref.own_ref.refs_0_), channel_id=1, source_target_pairs={{0,1},{1,0},{2,3},{3,2},{4,5},{5,4},{6,7},{7,6},{8,9},{9,8},{10,11... | collective-permute-start | bytes 258056 | tf_op jit(solution)/shard_map/ppermute | solution.py:1118
  3.6 5.1 %collective-permute-start.1 = (f32[104,128]{1,0:T(8,128)S(1)}, f32[104,128]{1,0:T(8,128)S(1)}, u32[]{:S(2)}, u32[]{:S(2)}) collective-permute-start(f32[104,128]{1,0:T(8,128)S(1)} %group.1.after_ref.refs_2_), channel_id=1, source_target_pairs={{0,2},{1,3},{2,0},{3,1},{4,6},{5,7},{6,4},{7,5},{8,10},{9,11},{10,... | collective-permute-start | bytes 159752 | tf_op jit(solution)/shard_map/ppermute | solution.py:1118
  8.7 5.8 %collective-permute-start.2 = (f32[240,128]{1,0:T(8,128)S(1)}, f32[240,128]{1,0:T(8,128)S(1)}, u32[]{:S(2)}, u32[]{:S(2)}) collective-permute-start(f32[240,128]{1,0:T(8,128)S(1)} %get-tuple-element.24.row_ref.own_ref), channel_id=1, source_target_pairs={{0,4},{4,0},{8,12},{12,8},{16,20},{20,16},{24,28},{28,24},{1,5},{5... | collective-permute-start | bytes 368648 | tf_op jit(solution)/shard_map/ppermute | solution.py:1118
  10.6 5.5 %collective-permute-start.3 = (f32[128,128]{1,0:T(8,128)S(1)}, f32[128,128]{1,0:T(8,128)S(1)}, u32[]{:S(2)}, u32[]{:S(2)}) collective-permute-start(f32[128,128]{1,0:T(8,128)S(1)} %get-tuple-element.25.far_ref), channel_id=1, source_target_pairs={{0,4},{4,0},{8,12},{12,8},{16,20},{20,16},{24,28},{28,24},{1,5},{5... | collective-permute-start | bytes 196616 | tf_op jit(solution)/shard_map/ppermute | solution.py:1118
  14.5 4.6 %collective-permute-start.5 = (f32[184,128]{1,0:T(8,128)S(1)}, f32[184,128]{1,0:T(8,128)S(1)}, u32[]{:S(2)}, u32[]{:S(2)}) collective-permute-start(f32[184,128]{1,0:T(8,128)S(1)} %merge.2.after_ref.own_ref), channel_id=1, source_target_pairs={{0,8},{4,12},{8,0},{12,4},{16,24},{20,28},{24,16},{28,20},{1,9},{5... | collective-permute-start | bytes 282632 | tf_op jit(solution)/shard_map/ppermute | solution.py:1118
  16.1 5.6 %collective-permute-start.4 = (f32[224,128]{1,0:T(8,128)S(1)}, f32[224,128]{1,0:T(8,128)S(1)}, u32[]{:S(2)}, u32[]{:S(2)}) collective-permute-start(f32[224,128]{1,0:T(8,128)S(1)} %relay.1), channel_id=1, source_target_pairs={{0,8},{4,0},{8,16},{12,4},{16,24},{20,12},{24,28},{28,20},{1,9},{5... | collective-permute-start | bytes 344072 | tf_op jit(solution)/shard_map/ppermute | solution.py:1125
  19.2 4.8 %collective-permute-start.6 = (f32[64,128]{1,0:T(8,128)S(1)}, f32[64,128]{1,0:T(8,128)S(1)}, u32[]{:S(2)}, u32[]{:S(2)}) collective-permute-start(f32[64,128]{1,0:T(8,128)S(1)} %merge.3.after.refs_0_), channel_id=1, source_target_pairs={{0,16},{4,20},{8,24},{12,28},{16,0},{20,4},{24,8},{28,12},{1,17},{... | collective-permute-start | bytes 98312 | tf_op jit(solution)/shard_map/ppermute | solution.py:1118
